TPU v7x, 512 devices: a whole 4x4x16 slice. The times are simulated.
512 devices in a mesh: segment: 64 (over x, z_lo, core), slab: 8 (over y, z_hi).
Axes of the slice: x: 4, y: 4, z: 16 (z_hi: 2, z_lo: 8; z = z_hi * 8 + z_lo), core: 2. Of those that a mesh axis runs over, the one named last changes fastest.
Arguments:
- fwd_in: bfloat16 [64, 2, 32, 16, 4, 128], P('segment', None, None, 'slab'), may hold values from -6 to 6
- back_out: bfloat16 [64, 2, 32, 16, 4, 128], P('segment', None, None, 'slab'), may hold values from -6 to 6
- back_grad: bfloat16 [64, 2, 32, 16, 4, 128], P('segment', None, None, 'slab'), may hold values from -6 to 6
- batch_next: bfloat16 [2, 32, 16, 4, 128], P(None, None, 'slab'), may hold values from -6 to 6
- loss_grad: bfloat16 [2, 2, 32, 16, 4, 128], P(None, None, None, 'slab'), may hold values from -6 to 6
- weights: bfloat16 [64, 2, 32, 864], P('segment'), may hold values from -0.21875 to 0.21875
Outputs:
- fwd_out: bfloat16 [64, 2, 32, 16, 4, 128], P('segment', None, None, 'slab')
- back_acts: bfloat16 [64, 2, 32, 16, 4, 128], P('segment', None, None, 'slab')
- back_grads: bfloat16 [64, 2, 32, 16, 4, 128], P('segment', None, None, 'slab')
- weight_grads: float32 [64, 2, 32, 864], P('segment', None, None, 'slab')
All inputs are finite; a program needn't handle non-finite values.
Results may differ from a plain program's by a relative error of at most 0.012.
Values may be sent and summed in bfloat16 or wider, within the bound.
No kernel may reach another device: no remote copies, remote signals or barrier semaphores. Data moves between devices by JAX's collectives and lax.ppermute only.
A program may use at most 64 MiB of HBM per device.

v0:
```python
import functools

import jax
import jax.numpy as jnp
from jax import lax
from jax.experimental import pallas as pl
from jax.experimental.pallas import tpu as pltpu
from jax.sharding import PartitionSpec as P

F32 = jnp.float32
BF16 = jnp.bfloat16
C = 32
H = 4
R = C * H
W = 128
SNAKE = 16


def wide(v):
    return v.astype(F32)


def silu(v):
    v = wide(v)
    return (v / (1.0 + jnp.exp(-v))).astype(BF16)


def slope(v):
    v = wide(v)
    sig = 1.0 / (1.0 + jnp.exp(-v))
    return sig * (1.0 + v * (1.0 - sig))


def conv_planes(w_ref, field, start, count, use):
    lane = lax.broadcasted_iota(jnp.int32, (R, W), 1)
    d = start
    while d < start + count:
        n = min(2, start + count - d)
        x = jnp.concatenate(
            [jnp.concatenate([field[d + k + a] for a in range(3)], axis=0) for k in range(n)], axis=1
        )
        y = jnp.dot(w_ref[...], x, preferred_element_type=F32)
        for k in range(n):
            cols = slice(k * W, (k + 1) * W)
            left = jnp.where(lane >= 1, pltpu.roll(y[:R, cols], 1, 1), 0.0)
            right = jnp.where(lane < W - 1, pltpu.roll(y[2 * R :, cols], W - 1, 1), 0.0)
            use(d + k, y[R : 2 * R, cols] + left + right)
        d += n


def stages(n, keep_lo, keep_hi, w_ref, fb, fa, bb, ba, db, da, fo_a, fo_b, bo_a, bo_b, go_a, go_b, act_b, act_a):
    inner = n - 2

    def mask(d, v):
        if d == 0:
            v = v * keep_lo
        if d == inner - 1:
            v = v * keep_hi
        return v

    def fwd():
        for p in range(n):
            act_b[p] = silu(fb[p])

        def one(d, v):
            out = mask(d, wide(fa[d]) + v).astype(BF16)
            fo_a[d] = out
            act_a[d] = silu(out)

        conv_planes(w_ref.at[0], act_b, 0, inner, one)

        def two(d, v):
            fo_b[d] = (wide(fb[d + 2]) + v).astype(BF16)

        conv_planes(w_ref.at[1], act_a, 0, inner - 2, two)

    def back():
        for p in range(n):
            act_b[p] = silu(bb[p])

        def rec_a(d, v):
            out = mask(d, wide(ba[d]) - v).astype(BF16)
            bo_a[d] = out
            act_a[d] = silu(out)

        conv_planes(w_ref.at[1], act_b, 0, inner, rec_a)

        def grad_a(d, v):
            go_a[d] = mask(d, wide(da[d]) + slope(bb[d + 1]) * v).astype(BF16)

        conv_planes(w_ref.at[3], db, 0, inner, grad_a)

        def rec_b(d, v):
            bo_b[d] = (wide(bb[d + 2]) - v).astype(BF16)

        conv_planes(w_ref.at[0], act_a, 0, inner - 2, rec_b)

        def grad_b(d, v):
            go_b[d] = (wide(db[d + 2]) + slope(bo_a[d + 1]) * v).astype(BF16)

        conv_planes(w_ref.at[2], go_a, 0, inner - 2, grad_b)

    fwd()
    back()


def put(win, at, piece):
    for k in range(piece.shape[0]):
        win[at + k] = piece[k]


def tick1_kernel(flags, w_ref, nat, swp, yn, yf, fm, fd, bm, bd, ld, y1w, h4, u4, e1p, *scratch):
    fb, fa, bb, ba, db, da, fo_b, bo_a, bo_b, go_a, go_b, act_b, act_a = scratch
    zh, keep_lo, keep_hi, fz, bz = (flags[k] for k in range(5))
    for k, win in enumerate((fb, bb, db)):
        put(win, 2 + 2 * zh, nat.at[k])
        put(win, 4 - 2 * zh, swp.at[k])
        put(win, 6 - 6 * zh, yn.at[pl.ds(2 * k, 2)])
        put(win, 6 * zh, yf.at[pl.ds(2 * k, 2)])
    for k, win in enumerate((fa, ba, da)):
        put(win, 1 + 2 * zh, nat.at[3 + k])
        put(win, 3 - 2 * zh, swp.at[3 + k])
        put(win, 5 - 5 * zh, yn.at[pl.ds(6 + k, 1)])
        put(win, 5 * zh, yf.at[pl.ds(6 + k, 1)])
    stages(
        8, keep_lo.astype(F32), keep_hi.astype(F32), w_ref, fb, fa, bb, ba, db, da,
        y1w, fo_b, bo_a, bo_b, go_a, go_b, act_b, act_a,
    )
    for k in range(4):
        fm[k] = fo_b[k]
        fm[4 + k] = y1w[2 * fz + k]
        bm[k] = bo_b[k]
        bm[4 + k] = go_b[k]
        bm[8 + k] = bo_a[2 * bz + k]
        bm[12 + k] = go_a[2 * bz + k]
        h4[k] = act_b[1 + 2 * zh + k]
        u4[k] = act_a[2 * zh + k]
    for k in range(2):
        fd[k] = fo_b[2 - 2 * fz + k]
        bd[k] = bo_b[2 - 2 * bz + k]
        bd[2 + k] = go_b[2 - 2 * bz + k]
        e1p[k] = go_a[1 + 2 * zh + k]
    ld[zh] = y1w[3 - zh]
    ld[1 - zh] = fo_b[3 - 3 * zh]


def tick2_kernel(
    flags, w_ref, fm, fd, bm, bd, sp1, sp2, first_own, last_own, y1w, own, ld, out_f, out_b, h4, u4, e1p, d2p, *scratch
):
    fb, fa, bb, ba, db, da, fo_a, fo_b, bo_a, bo_b, go_a, go_b, act_b, act_a = scratch
    zh, keep_lo, keep_hi, first, last = (flags[k] for k in range(5))
    main, halo = (2 - 2 * zh, 4 * zh)

    def special(b_win, a_win, own):
        put(b_win, 2, own.at[1])
        put(b_win, 4 - 4 * zh, sp1.at[1])
        put(b_win, 4 * zh, sp2.at[1])
        put(a_win, 1, own.at[0])
        a_win[3 - 3 * zh] = sp1[0, zh]
        a_win[3 * zh] = sp2[0, 1 - zh]

    @pl.when(first == 1)
    def _():
        special(fb, fa, first_own)

    @pl.when(first == 0)
    def _():
        put(fb, main, fm.at[pl.ds(0, 4)])
        put(fb, halo, fd)
        put(fa, 0, fm.at[pl.ds(4, 4)])

    @pl.when(last == 1)
    def _():
        special(db, da, last_own)
        for k in range(5):
            bb[1 - zh + k] = y1w[zh + k]
        bb[5 * zh] = ld[zh]
        for k in range(3):
            ba[1 - zh + k] = own[zh + k]
        ba[3 * zh] = ld[1 - zh]

    @pl.when(last == 0)
    def _():
        put(bb, main, bm.at[pl.ds(0, 4)])
        put(bb, halo, bd.at[pl.ds(0, 2)])
        put(db, main, bm.at[pl.ds(4, 4)])
        put(db, halo, bd.at[pl.ds(2, 2)])
        put(ba, 0, bm.at[pl.ds(8, 4)])
        put(da, 0, bm.at[pl.ds(12, 4)])

    stages(
        6, keep_lo.astype(F32), keep_hi.astype(F32), w_ref, fb, fa, bb, ba, db, da,
        fo_a, fo_b, bo_a, bo_b, go_a, go_b, act_b, act_a,
    )
    for k in range(2):
        out_f[k] = fo_a[1 + k]
        out_f[2 + k] = fo_b[k]
        out_b[k] = bo_b[k]
        out_b[2 + k] = bo_a[1 + k]
        out_b[4 + k] = go_a[1 + k]
        out_b[6 + k] = go_b[k]
        e1p[k] = go_a[1 + k]
        d2p[k] = db[2 + k]
    for k in range(4):
        h4[k] = act_b[1 + k]
        u4[k] = act_a[k]


def wgrad_pair(g_ref, u_ref):
    lane = lax.broadcasted_iota(jnp.int32, (C, W), 1)
    zero = jnp.zeros((C, W), BF16)
    left, right = ([], [])
    for d in range(2):
        for h in range(H):
            g = wide(g_ref[d, h * C : (h + 1) * C])
            down = jnp.where(lane < W - 1, pltpu.roll(g, W - 1, 1), 0.0)
            up = jnp.where(lane >= 1, pltpu.roll(g, 1, 1), 0.0)
            left.append(jnp.concatenate([down, g, up], axis=0).astype(BF16))
            rows = []
            for a in range(3):
                for b in range(3):
                    at = h + b - 1
                    rows.append(u_ref[d + a, at * C : (at + 1) * C] if 0 <= at < H else zero)
            right.append(jnp.concatenate(rows, axis=0))
    return lax.dot_general(
        jnp.concatenate(left, axis=1),
        jnp.concatenate(right, axis=1),
        (((1,), (1,)), ((), ())),
        preferred_element_type=F32,
    )


def wgrad_kernel(e1, u4, d2, h4, out):
    out[0] = wgrad_pair(e1, u4)
    out[1] = wgrad_pair(d2, h4)


def wgrad_add_kernel(scale, e1, u4, d2, h4, prev, out):
    out[0] = (prev[0] + wgrad_pair(e1, u4)) * scale
    out[1] = (prev[1] + wgrad_pair(d2, h4)) * scale


VMEM = pl.BlockSpec(memory_space=pltpu.VMEM)
SMEM = pl.BlockSpec(memory_space=pltpu.SMEM)


def call(kernel, outs, scratch, args, flops, flagged=True):
    n = len(args)
    return pl.pallas_call(
        kernel,
        out_shape=tuple(jax.ShapeDtypeStruct(s, t) for s, t in outs),
        in_specs=([SMEM] + [VMEM] * (n - 1)) if flagged else [VMEM] * n,
        out_specs=tuple(VMEM for _ in outs),
        scratch_shapes=scratch,
        compiler_params=pltpu.CompilerParams(vmem_limit_bytes=40 * 2**20),
        cost_estimate=pl.CostEstimate(flops=flops, bytes_accessed=4_000_000, transcendentals=400_000),
    )(*args)


def planes(*lead):
    return pltpu.VMEM((*lead, R, W), BF16)


def shaped(*lead):
    return ((*lead, R, W), BF16)


def inside(value):
    s, _, d = value.shape[:3]
    return value.transpose(0, 2, 3, 1, 4).reshape(s, d, R, W)


def outside(value):
    s, d = value.shape[:2]
    return value.reshape(s, d, H, C, W).transpose(0, 3, 1, 2, 4)


def matrices(flat):
    k = flat.reshape(2, C, C, 3, 3, 3)
    turned = jnp.flip(k, (3, 4, 5)).transpose(0, 2, 1, 3, 4, 5)
    both = jnp.concatenate([k, turned])
    rows = both.transpose(0, 5, 1, 3, 4, 2)
    rows = jnp.pad(rows, ((0, 0), (0, 0), (0, 0), (0, 0), (2, 2), (0, 0)))
    bands = jnp.stack([rows[:, :, :, :, 3 - h : 7 - h] for h in range(H)], axis=2)
    return bands.reshape(4, 3 * R, 3 * R)


def local(fwd_in, back_out, back_grad, batch_next, loss_grad, weights):
    seg = lax.axis_index("segment")
    slab = lax.axis_index("slab")
    count = lax.axis_size("segment")
    slabs = lax.axis_size("slab")
    ny = slabs // 2
    y, zh = (slab // 2, slab % 2)
    scale = float(fwd_in.shape[3] * slabs * fwd_in.shape[4] * fwd_in.shape[5]) ** (-0.5)

    def route(value, to):
        pairs = []
        for s in range(count):
            for yy in range(ny):
                for zz in range(2):
                    target = to(s, yy, zz)
                    if target is None:
                        continue
                    ts, ty, tz = target
                    if 0 <= ts < count and 0 <= ty < ny:
                        pairs.append((s * slabs + 2 * yy + zz, ts * slabs + 2 * ty + tz))
        return lax.ppermute(value, ("segment", "slab"), pairs)

    def fwd_side(s, zz):
        return 1 - zz if s % SNAKE == SNAKE - 1 and s < count - 1 else zz

    def back_side(s, zz):
        return 1 - zz if s % SNAKE == 0 and s > 0 else zz

    fz = jnp.where((seg % SNAKE == SNAKE - 1) & (seg < count - 1), 1 - zh, zh)
    bz = jnp.where((seg % SNAKE == 0) & (seg > 0), 1 - zh, zh)
    is_first, is_last = (seg == 0, seg == count - 1)

    native = jnp.stack(
        [inside(v[0, k : k + 1])[0] for k, v in ((1, fwd_in), (0, back_out), (1, back_grad), (0, fwd_in), (1, back_out), (0, back_grad))]
    )
    swapped = route(native, lambda s, yy, zz: (s, yy, 1 - zz))

    def rim(value, high):
        return jnp.concatenate([value[:3].reshape(6, R, W), jnp.where(high, value[3:, 1], value[3:, 0])])

    near = route(rim(native, zh == 1), lambda s, yy, zz: (s, yy - 1 + 2 * zz, zz))

    from_first, from_last = (14 % count, (count - 15) % count)
    first_own, last_own = (inside(batch_next), inside(loss_grad[0]))
    ends = jnp.where(seg == from_first, first_own, last_own)

    def end_of(s):
        return 0 if s == from_first else count - 1 if s == from_last else -1

    sp1 = route(ends, lambda s, yy, zz: (end_of(s), yy, 1 - zz))
    sp2 = route(ends, lambda s, yy, zz: (end_of(s), yy + (1 if zz == 1 else -1), 1 - zz))

    mats = matrices(weights[0])
    far = route(rim(swapped, zh == 0), lambda s, yy, zz: (s, yy + 1 - 2 * zz, zz))

    def as_flags(*values):
        return jnp.stack([jnp.asarray(v).astype(jnp.int32) for v in values])

    flags1 = as_flags(zh, y > 0, y < ny - 1, fz, bz)
    fm, fd, bm, bd, ld, y1w, h4, u4, e1p = call(
        tick1_kernel,
        [shaped(8), shaped(2), shaped(16), shaped(4), shaped(2), shaped(6), shaped(4), shaped(4), shaped(2)],
        [planes(8), planes(6), planes(8), planes(6), planes(8), planes(6), planes(4), planes(6), planes(4), planes(6),
         planes(4), planes(8), planes(6)],
        (flags1, mats, native, swapped, near, far),
        3_000_000_000,
    )

    def fwd_diag(s, yy, zz):
        r = fwd_side(s, zz)
        return (s + 1, yy + 1 - 2 * r, r)

    def back_diag(s, yy, zz):
        r = back_side(s, zz)
        return (s - 1, yy + 1 - 2 * r, r)

    bm2 = route(bm, lambda s, yy, zz: (s - 1, yy, back_side(s, zz)))
    bd2 = route(bd, back_diag)
    fm2 = route(fm, lambda s, yy, zz: (s + 1, yy, fwd_side(s, zz)))
    fd2 = route(fd, fwd_diag)
    ld2 = route(ld, lambda s, yy, zz: (s if s == count - 1 else -1, yy + 1 - 2 * zz, zz))
    (dw,) = call(
        wgrad_kernel, [((2, 3 * C, 9 * C), F32)], [], (e1p, u4, native[2], h4), 300_000_000, flagged=False
    )

    flags2 = as_flags(zh, (y > 0) | (zh == 1), (y < ny - 1) | (zh == 0), is_first, is_last)
    out_f, out_b, h4, u4, e1p, d2p = call(
        tick2_kernel,
        [shaped(4), shaped(8), shaped(4), shaped(4), shaped(2), shaped(2)],
        [planes(6), planes(4), planes(6), planes(4), planes(6), planes(4), planes(4), planes(2), planes(4), planes(2),
         planes(4), planes(2), planes(6), planes(4)],
        (flags2, mats, fm2, fd2, bm2, bd2, sp1, sp2, first_own, last_own, y1w, fm, ld2),
        2_000_000_000,
    )
    (dw,) = call(
        functools.partial(wgrad_add_kernel, scale),
        [((2, 3 * C, 9 * C), F32)],
        [],
        (e1p, u4, d2p, h4, dw),
        300_000_000,
        flagged=False,
    )
    back = route(out_b, lambda s, yy, zz: (s - 1, yy, zz))

    parts = dw.reshape(2, 3, C, 9, slabs, C // slabs).transpose(4, 0, 1, 2, 3, 5)
    parts = parts.reshape(slabs, -1, 128)
    parts = lax.all_to_all(parts, "slab", 0, 0, tiled=True)
    total = jnp.sum(parts, axis=0).reshape(2, 3, C, 9, C // slabs)
    total = total.transpose(0, 2, 4, 3, 1).reshape(1, 2, C, -1)

    fwd_out = outside(out_f.reshape(2, 2, R, W))
    back = outside(back.reshape(4, 2, R, W))
    acts = jnp.where(is_last, fwd_out, back[:2])
    grads = jnp.where(is_last, loss_grad[1], back[2:])
    return (fwd_out[None], acts[None], grads[None], total)


def solution(mesh):
    placed = (
        P("segment", None, None, "slab", None, None),
        P("segment", None, None, "slab", None, None),
        P("segment", None, None, "slab", None, None),
        P(None, None, "slab", None, None),
        P(None, None, None, "slab", None, None),
        P("segment", None, None, None),
    )
    return jax.shard_map(
        local,
        mesh=mesh,
        in_specs=placed,
        out_specs=(
            P("segment", None, None, "slab", None, None),
            P("segment", None, None, "slab", None, None),
            P("segment", None, None, "slab", None, None),
            P("segment", None, None, "slab"),
        ),
        check_vma=False,
    )
```

profile of v0, /device:TPU:36, one launch (start us, length us, event | category | flops | bytes accessed | tf_op | source)
XLA Modules:
  0.0 154.1 jit_solution(7638221522122802813)
XLA Ops:
  2.5 1.0 slice_bitcast_fusion.1
  3.7 14.8 %collective-permute-start = (bf16[6,2,128,128]{3,2,0,1:T(8,128)(2,1)S(1)}, bf16[6,2,128,128]{3,2,0,1:T(8,128)(2,1)S(1)}, u32[]{:S(2)}, u32[]{:S(2)}) collective-permute-start(bf16[6,2,128,128]{3,2,0,1:T(8,128)(2,1)S(1)} %constant_dynamic-update-slice_fusion), channel_id=1, source_target_pairs={{0,1},{1,0},{2,3},{3,2},{4,5},{5,4},{6,7},{7,6},{8,9},{9,8},{10,11... | collective-permute-start | bytes 1179656 | tf_op jit(solution)/shard_map/ppermute | solution.py:308
  19.4 1.3 collective-permute-start.1
  22.4 1.1 maximum_bitcast_fusion
  23.6 2.0 %fusion = (bf16[4,3,1,32,3,4,32]{3,0,1,5,4,6,2:T(4,128)(2,1)S(1)}, bf16[4,3,1,32,3,4,32]{3,0,1,5,4,6,2:T(4,128)(2,1)S(1)}, bf16[4,3,1,32,3,4,32]{3,0,1,5,4,6,2:T...) fusion(bf16[4,3,32,3,3,32]{2,0,1,4,3,5:T(4,128)(2,1)S(1)} %maximum_bitcast_fusion), kind=kLoop, calls=%fused_computation.5 | loop fusion | bytes 1400832 | tf_op jit(solution)/shard_map/stack | solution.py:284
  25.6 27.6 %collective-permute-done = bf16[6,2,128,128]{3,2,0,1:T(8,128)(2,1)S(1)} collective-permute-done((bf16[6,2,128,128]{3,2,0,1:T(8,128)(2,1)S(1)}, bf16[6,2,128,128]{3,2,0,1:T(8,128)(2,1)S(1)}, u32[]{:S(2)}, u32[]{:S(2)}) %collective-permute-start) | collective-permute-done | bytes 393248 | tf_op jit(solution)/shard_map/ppermute | solution.py:308
  54.0 3.5 %collective-permute-start.2 = (bf16[9,128,128]{2,1,0:T(8,128)(2,1)}, bf16[9,128,128]{2,1,0:T(8,128)(2,1)S(1)}, u32[]{:S(2)}, u32[]{:S(2)}) collective-permute-start(bf16[9,128,128]{2,1,0:T(8,128)(2,1)} %pad_maximum_fusion.2), channel_id=1, source_target_pairs={{0,2},{2,4},{3,1},{4,6},{5,3},{7,5},{8,10},{10,12},{11,9},{12,14},... | collective-permute-start | bytes 884744 | tf_op jit(solution)/shard_map/ppermute | solution.py:308
  57.5 5.9 %pad_maximum_fusion = bf16[4,3,4,32,3,4,32]{3,0,1,5,4,6,2:T(4,128)(2,1)} fusion(bf16[4,3,1,32,3,4,32]{3,0,1,5,4,6,2:T(4,128)(2,1)S(1)} %get-tuple-element.45, bf16[4,3,1,32,3,4,32]{3,0,1,5,4,6,2:T(4,128)(2,1)S(1)} %get-tuple-element.44, bf16[4,3,1,32,3,4,32]{3,0,1,5,4,6,2:T(4,128)(2,1)S(1)} %get-tuple-element.43, ...), kind=kLoop, calls=%fused_computation | loop fusion | flops 1769472 | bytes 2359296 | tf_op jit(solution)/shard_map/stack | solution.py:284
  63.5 10.5 %copy.52 = bf16[4,3,4,32,3,4,32]{6,5,4,3,2,1,0:T(4,128)(2,1)} copy(bf16[4,3,4,32,3,4,32]{3,0,1,5,4,6,2:T(4,128)(2,1)} %pad_maximum_fusion) | data formatting | bytes 2359296 | tf_op jit(solution)/shard_map/stack | solution.py:284
  73.9 5.9 %reshape.39.w_ref = bf16[4,384,384]{2,1,0:T(8,128)(2,1)S(1)} reshape(bf16[4,3,4,32,3,4,32]{6,5,4,3,2,1,0:T(4,128)(2,1)} %copy.52) | data formatting | bytes 2359296 | tf_op jit(solution)/shard_map/reshape | solution.py:285
  80.0 3.0 %shard_map.93 = (bf16[8,128,128]{2,1,0:T(8,128)(2,1)S(1)}, bf16[2,128,128]{2,1,0:T(8,128)(2,1)S(1)}, bf16[16,128,128]{2,1,0:T(8,128)(2,1)S(1)}, bf16[4,128,128]{...) custom-call(s32[5]{0:T(128)S(1)} %stack.95.flags, ...), custom_call_target="tpu_custom_call" | custom-call | flops 3000000000 | bytes 4000000 | tf_op jit(solution)/shard_map/pallas_call | solution.py:249
  86.8 1.9 %collective-permute-start.5 = (bf16[16,128,128]{2,1,0:T(8,128)(2,1)S(1)}, bf16[16,128,128]{2,1,0:T(8,128)(2,1)S(1)}, u32[]{:S(2)}, u32[]{:S(2)}) collective-permute-start(bf16[16,128,128]{2,1,0:T(8,128)(2,1)S(1)} %get-tuple-element.21), channel_id=1, source_target_pairs={{8,0},{9,1},{10,2},{11,3},{12,4},{13,5},{14,6},{15,7},{16,8},{17,9... | collective-permute-start | bytes 1572872 | tf_op jit(solution)/shard_map/ppermute | solution.py:308
  88.9 2.4 %collective-permute-start.3 = (bf16[8,128,128]{2,1,0:T(8,128)(2,1)S(1)}, bf16[8,128,128]{2,1,0:T(8,128)(2,1)S(1)}, u32[]{:S(2)}, u32[]{:S(2)}) collective-permute-start(bf16[8,128,128]{2,1,0:T(8,128)(2,1)S(1)} %get-tuple-element.19.own), channel_id=1, source_target_pairs={{0,8},{1,9},{2,10},{3,11},{4,12},{5,13},{6,14},{7,15},{8,16},{9,17... | collective-permute-start | bytes 786440 | tf_op jit(solution)/shard_map/ppermute | solution.py:308
  92.7 4.8 %collective-permute-start.6 = (bf16[4,128,128]{2,1,0:T(8,128)(2,1)S(1)}, bf16[4,128,128]{2,1,0:T(8,128)(2,1)}, u32[]{:S(2)}, u32[]{:S(2)}) collective-permute-start(bf16[4,128,128]{2,1,0:T(8,128)(2,1)S(1)} %get-tuple-element.22), channel_id=1, source_target_pairs={{8,2},{10,4},{11,1},{12,6},{13,3},{15,5},{16,10},{18,12},{19,9},{2... | collective-permute-start | bytes 393224 | tf_op jit(solution)/shard_map/ppermute | solution.py:308
  97.5 2.2 %collective-permute-start.4 = (bf16[2,128,128]{2,1,0:T(8,128)(2,1)}, bf16[2,128,128]{2,1,0:T(8,128)(2,1)}, u32[]{:S(2)}, u32[]{:S(2)}) collective-permute-start(bf16[2,128,128]{2,1,0:T(8,128)(2,1)} %copy-done.3), channel_id=1, source_target_pairs={{0,10},{2,12},{3,9},{4,14},{5,11},{7,13},{8,18},{10,20},{11,17},{1... | collective-permute-start | bytes 196616 | tf_op jit(solution)/shard_map/ppermute | solution.py:308
  99.7 1.3 collective-permute-start.9
  105.3 0.9 copy-done.11
  106.2 3.3 %shard_map.94 = (bf16[4,128,128]{2,1,0:T(8,128)(2,1)S(1)}, bf16[8,128,128]{2,1,0:T(8,128)(2,1)S(1)}, bf16[4,128,128]{2,1,0:T(8,128)(2,1)S(1)}, bf16[4,128,128]{2...) custom-call(s32[5]{0:T(128)S(1)} %stack.83.flags, ...), custom_call_target="tpu_custom_call" | custom-call | flops 2000000000 | bytes 4000000 | tf_op jit(solution)/shard_map/pallas_call | solution.py:249
  110.7 3.1 %copy.69 = f32[8,2,3,32,9,4]{0,5,4,3,2,1:T(4,128)} copy(f32[8,2,3,32,9,4]{3,2,5,0,4,1:T(4,128)S(1)} %bitcast.100) | data formatting | bytes 442368 | tf_op jit(solution)/shard_map/transpose | solution.py:392
  113.8 3.4 %copy.70 = f32[8,54,128]{2,1,0:T(8,128)} copy(f32[8,54,128]{0,2,1:T(8,128)} %bitcast.98) | data formatting | bytes 442368 | tf_op jit(solution)/shard_map/reshape | solution.py:393
  117.2 11.7 %all-to-all-start = ((f32[8,54,128]{2,1,0:T(8,128)}), f32[8,54,128]{2,1,0:T(8,128)S(1)}, u32[]{:S(2)}, u32[]{:S(2)}) async-start(f32[8,54,128]{2,1,0:T(8,128)} %copy.70), calls=%async_computation | async-start | bytes 458752 | tf_op jit(solution)/shard_map/all_to_all | solution.py:394
  129.0 3.2 %collective-permute-start.10 = (bf16[8,128,128]{2,1,0:T(8,128)(2,1)S(1)}, bf16[8,128,128]{2,1,0:T(8,128)(2,1)S(1)}, u32[]{:S(2)}, u32[]{:S(2)}) collective-permute-start(bf16[8,128,128]{2,1,0:T(8,128)(2,1)S(1)} %get-tuple-element.26), channel_id=1, source_target_pairs={{8,0},{9,1},{10,2},{11,3},{12,4},{13,5},{14,6},{15,7},{16,8},{17,9... | collective-permute-start | bytes 786440 | tf_op jit(solution)/shard_map/ppermute | solution.py:308
  132.9 9.4 %collective-permute-done.10 = bf16[8,128,128]{2,1,0:T(8,128)(2,1)S(1)} collective-permute-done((bf16[8,128,128]{2,1,0:T(8,128)(2,1)S(1)}, bf16[8,128,128]{2,1,0:T(8,128)(2,1)S(1)}, u32[]{:S(2)}, u32[]{:S(2)}) %collective-permute-start.10) | collective-permute-done | bytes 262176 | tf_op jit(solution)/shard_map/ppermute | solution.py:308
  143.3 9.2 %all-to-all-done = f32[8,54,128]{2,1,0:T(8,128)S(1)} async-done(((f32[8,54,128]{2,1,0:T(8,128)}), f32[8,54,128]{2,1,0:T(8,128)S(1)}, u32[]{:S(2)}, u32[]{:S(2)}) %all-to-all-start) | async-done | bytes 221216 | tf_op jit(solution)/shard_map/all_to_all | solution.py:394
  (87 shorter events, 19.6 us)
Async XLA Ops:
  2.5 18.2 %copy-start.15 = (bf16[1,2,32,864]{3,2,1,0:T(8,128)(2,1)S(1)}, bf16[1,2,32,864]{3,2,1,0:T(8,128)(2,1)}, u32[]{:S(2)}) copy-start(bf16[1,2,32,864]{3,2,1,0:T(8,128)(2,1)} %param.11) | copy-start | bytes 331780
  3.7 49.5 %collective-permute-start = (bf16[6,2,128,128]{3,2,0,1:T(8,128)(2,1)S(1)}, bf16[6,2,128,128]{3,2,0,1:T(8,128)(2,1)S(1)}, u32[]{:S(2)}, u32[]{:S(2)}) collective-permute-start(bf16[6,2,128,128]{3,2,0,1:T(8,128)(2,1)S(1)} %constant_dynamic-update-slice_fusion), channel_id=1, source_target_pairs={{0,1},{1,0},{2,3},{3,2},{4,5},{5,4},{6,7},{7,6},{8,9},{9,8},{10,11... | collective-permute-start | bytes 1179656 | tf_op jit(solution)/shard_map/ppermute | solution.py:308
  19.4 60.6 %collective-permute-start.1 = (bf16[9,128,128]{2,1,0:T(8,128)(2,1)}, bf16[9,128,128]{2,1,0:T(8,128)(2,1)S(1)}, u32[]{:S(2)}, u32[]{:S(2)}) collective-permute-start(bf16[9,128,128]{2,1,0:T(8,128)(2,1)} %pad_maximum_fusion.1), channel_id=1, source_target_pairs={{1,3},{2,0},{3,5},{4,2},{5,7},{6,4},{9,11},{10,8},{11,13},{12,10},... | collective-permute-start | bytes 884744 | tf_op jit(solution)/shard_map/ppermute | solution.py:308
  54.0 26.0 %collective-permute-start.2 = (bf16[9,128,128]{2,1,0:T(8,128)(2,1)}, bf16[9,128,128]{2,1,0:T(8,128)(2,1)S(1)}, u32[]{:S(2)}, u32[]{:S(2)}) collective-permute-start(bf16[9,128,128]{2,1,0:T(8,128)(2,1)} %pad_maximum_fusion.2), channel_id=1, source_target_pairs={{0,2},{2,4},{3,1},{4,6},{5,3},{7,5},{8,10},{10,12},{11,9},{12,14},... | collective-permute-start | bytes 884744 | tf_op jit(solution)/shard_map/ppermute | solution.py:308
  80.0 8.8 %copy-start.12 = (bf16[2,2,32,2,4,128]{5,4,3,2,1,0:T(4,128)(2,1)S(1)}, bf16[2,2,32,2,4,128]{5,4,3,2,1,0:T(4,128)(2,1)}, u32[]{:S(2)}) copy-start(bf16[2,2,32,2,4,128]{5,4,3,2,1,0:T(4,128)(2,1)} %param.10) | copy-start | bytes 786436
  80.0 8.9 %copy-start.14 = (bf16[2,32,2,4,128]{4,3,2,1,0:T(4,128)(2,1)S(1)}, bf16[2,32,2,4,128]{4,3,2,1,0:T(4,128)(2,1)}, u32[]{:S(2)}) copy-start(bf16[2,32,2,4,128]{4,3,2,1,0:T(4,128)(2,1)} %param.9) | copy-start | bytes 393220
  84.2 0.7 copy-start.4
  86.2 0.7 copy-start.10
  86.8 17.6 %collective-permute-start.5 = (bf16[16,128,128]{2,1,0:T(8,128)(2,1)S(1)}, bf16[16,128,128]{2,1,0:T(8,128)(2,1)S(1)}, u32[]{:S(2)}, u32[]{:S(2)}) collective-permute-start(bf16[16,128,128]{2,1,0:T(8,128)(2,1)S(1)} %get-tuple-element.21), channel_id=1, source_target_pairs={{8,0},{9,1},{10,2},{11,3},{12,4},{13,5},{14,6},{15,7},{16,8},{17,9... | collective-permute-start | bytes 1572872 | tf_op jit(solution)/shard_map/ppermute | solution.py:308
  88.9 15.5 %collective-permute-start.3 = (bf16[8,128,128]{2,1,0:T(8,128)(2,1)S(1)}, bf16[8,128,128]{2,1,0:T(8,128)(2,1)S(1)}, u32[]{:S(2)}, u32[]{:S(2)}) collective-permute-start(bf16[8,128,128]{2,1,0:T(8,128)(2,1)S(1)} %get-tuple-element.19.own), channel_id=1, source_target_pairs={{0,8},{1,9},{2,10},{3,11},{4,12},{5,13},{6,14},{7,15},{8,16},{9,17... | collective-permute-start | bytes 786440 | tf_op jit(solution)/shard_map/ppermute | solution.py:308
  91.3 6.2 %collective-permute-start.7 = (bf16[2,2,128,128]{3,2,1,0:T(8,128)(2,1)S(1)}, bf16[2,2,128,128]{3,2,1,0:T(8,128)(2,1)S(1)}, u32[]{:S(2)}, u32[]{:S(2)}) collective-permute-start(bf16[2,2,128,128]{3,2,1,0:T(8,128)(2,1)S(1)} %broadcast_select_fusion), channel_id=1, source_target_pairs={{112,1},{113,0},{114,3},{115,2},{116,5},{117,4},{118,7},{119,6},{3... | collective-permute-start | bytes 393224 | tf_op jit(solution)/shard_map/ppermute | solution.py:308
  92.0 7.7 %collective-permute-start.8 = (bf16[2,2,128,128]{3,2,1,0:T(8,128)(2,1)S(1)}, bf16[2,2,128,128]{3,2,1,0:T(8,128)(2,1)S(1)}, u32[]{:S(2)}, u32[]{:S(2)}) collective-permute-start(bf16[2,2,128,128]{3,2,1,0:T(8,128)(2,1)S(1)} %broadcast_select_fusion), channel_id=1, source_target_pairs={{113,2},{114,1},{115,4},{116,3},{117,6},{118,5},{393,506},{394,505... | collective-permute-start | bytes 393224 | tf_op jit(solution)/shard_map/ppermute | solution.py:308
  92.7 11.7 %collective-permute-start.6 = (bf16[4,128,128]{2,1,0:T(8,128)(2,1)S(1)}, bf16[4,128,128]{2,1,0:T(8,128)(2,1)}, u32[]{:S(2)}, u32[]{:S(2)}) collective-permute-start(bf16[4,128,128]{2,1,0:T(8,128)(2,1)S(1)} %get-tuple-element.22), channel_id=1, source_target_pairs={{8,2},{10,4},{11,1},{12,6},{13,3},{15,5},{16,10},{18,12},{19,9},{2... | collective-permute-start | bytes 393224 | tf_op jit(solution)/shard_map/ppermute | solution.py:308
  97.5 6.8 %collective-permute-start.4 = (bf16[2,128,128]{2,1,0:T(8,128)(2,1)}, bf16[2,128,128]{2,1,0:T(8,128)(2,1)}, u32[]{:S(2)}, u32[]{:S(2)}) collective-permute-start(bf16[2,128,128]{2,1,0:T(8,128)(2,1)} %copy-done.3), channel_id=1, source_target_pairs={{0,10},{2,12},{3,9},{4,14},{5,11},{7,13},{8,18},{10,20},{11,17},{1... | collective-permute-start | bytes 196616 | tf_op jit(solution)/shard_map/ppermute | solution.py:308
  99.7 4.7 %copy-start = (bf16[2,2,128,128]{3,2,1,0:T(8,128)(2,1)}, bf16[2,2,128,128]{3,2,1,0:T(8,128)(2,1)S(1)}, u32[]{:S(2)}) copy-start(bf16[2,2,128,128]{3,2,1,0:T(8,128)(2,1)S(1)} %collective-permute-done.8.sp2) | copy-start | bytes 393220
  99.7 4.6 %collective-permute-start.9 = (bf16[2,128,128]{2,1,0:T(8,128)(2,1)}, bf16[2,128,128]{2,1,0:T(8,128)(2,1)}, u32[]{:S(2)}, u32[]{:S(2)}) collective-permute-start(bf16[2,128,128]{2,1,0:T(8,128)(2,1)} %copy-done.2), channel_id=1, source_target_pairs={{504,506},{506,508},{507,505},{508,510},{509,507},{511,509}} | collective-permute-start | bytes 196616 | tf_op jit(solution)/shard_map/ppermute | solution.py:308
  101.1 0.9 copy-start.5
  102.0 0.9 copy-start.7
  102.9 0.8 copy-start.9
  104.4 0.9 copy-start.1
  105.3 0.9 copy-start.11
  113.8 28.6 %copy-start.13 = (bf16[2,2,32,2,4,128]{5,4,3,2,1,0:T(4,128)(2,1)S(1)}, bf16[2,2,32,2,4,128]{5,4,3,2,1,0:T(4,128)(2,1)}, u32[]{:S(2)}) copy-start(bf16[2,2,32,2,4,128]{5,4,3,2,1,0:T(4,128)(2,1)} %param.10) | copy-start | bytes 786436
  117.2 35.2 %all-to-all-start = ((f32[8,54,128]{2,1,0:T(8,128)}), f32[8,54,128]{2,1,0:T(8,128)S(1)}, u32[]{:S(2)}, u32[]{:S(2)}) async-start(f32[8,54,128]{2,1,0:T(8,128)} %copy.70), calls=%async_computation | async-start | bytes 458752 | tf_op jit(solution)/shard_map/all_to_all | solution.py:394
  129.0 13.3 %collective-permute-start.10 = (bf16[8,128,128]{2,1,0:T(8,128)(2,1)S(1)}, bf16[8,128,128]{2,1,0:T(8,128)(2,1)S(1)}, u32[]{:S(2)}, u32[]{:S(2)}) collective-permute-start(bf16[8,128,128]{2,1,0:T(8,128)(2,1)S(1)} %get-tuple-element.26), channel_id=1, source_target_pairs={{8,0},{9,1},{10,2},{11,3},{12,4},{13,5},{14,6},{15,7},{16,8},{17,9... | collective-permute-start | bytes 786440 | tf_op jit(solution)/shard_map/ppermute | solution.py:308
  (4 other events, 2.5 us)
where the time goes:
time: 155 us; the launch traced here: 154 us
  starting transfers between devices  48.5 us (31%)
  waiting for transfers between devices  46.2 us (30%)
  local copies, waits for them, and re-layouts  41.2 us (27%)
  other arithmetic  9.56 us (6%)
  Pallas kernels  7.46 us (5%)
    ppermute x11, waiting for transfers between devices, route(): return lax.ppermute(value, ('segment', 'slab'), pairs)  37 us
    ppermute x11, starting transfers between devices, route(): return lax.ppermute(value, ('segment', 'slab'), pairs)  36.7 us
    another operation x2, local copies, waits for them, and re-layouts, matrices(): bands = jnp.stack([rows[:, :, :, :, 3 - h:7 - h] for h in range(H)], axis=2)  12.5 us
    all_to_all x1, starting transfers between devices, local(): parts = lax.all_to_all(parts, 'slab', 0, 0, tiled=True)  11.7 us
    unnamed x39, local copies, waits for them, and re-layouts  9.86 us
    all_to_all x1, waiting for transfers between devices, local(): parts = lax.all_to_all(parts, 'slab', 0, 0, tiled=True)  9.2 us
    pallas_call x4, Pallas kernels, call(): pl.pallas_call(kernel, out_shape=tuple((jax.ShapeDtypeStruct(s, t) for s,...  7.46 us
    another operation x1, other arithmetic, matrices(): bands = jnp.stack([rows[:, :, :, :, 3 - h:7 - h] for h in range(H)], axis=2)  5.93 us
  transfers between devices with their start and end apart: 12, of which 3 were waited for; matrix products, arithmetic and copies ran while one was open for 20% of the time, Pallas kernels for 0%

commit v1 on v0

v1 whole, which is shorter than its diff:
```python
import functools

import jax
import jax.numpy as jnp
import numpy as np
from jax import lax
from jax.experimental import pallas as pl
from jax.experimental.pallas import tpu as pltpu
from jax.sharding import PartitionSpec as P

F32 = jnp.float32
BF16 = jnp.bfloat16
C = 32
H = 4
R = C * H
W = 128
SNAKE = 16


def wide(v):
    return v.astype(F32)


def silu(v):
    v = wide(v)
    return (v / (1.0 + jnp.exp(-v))).astype(BF16)


def slope(v):
    v = wide(v)
    sig = 1.0 / (1.0 + jnp.exp(-v))
    return sig * (1.0 + v * (1.0 - sig))


def conv_planes(w_ref, field, start, count, use):
    lane = lax.broadcasted_iota(jnp.int32, (R, W), 1)
    d = start
    while d < start + count:
        n = min(2, start + count - d)
        x = jnp.concatenate(
            [jnp.concatenate([field[d + k + a] for a in range(3)], axis=0) for k in range(n)], axis=1
        )
        y = jnp.dot(w_ref[...], x, preferred_element_type=F32)
        for k in range(n):
            cols = slice(k * W, (k + 1) * W)
            left = jnp.where(lane >= 1, pltpu.roll(y[:R, cols], 1, 1), 0.0)
            right = jnp.where(lane < W - 1, pltpu.roll(y[2 * R :, cols], W - 1, 1), 0.0)
            use(d + k, y[R : 2 * R, cols] + left + right)
        d += n


def mask(d, v, inner, keep):
    if d == 0:
        v = v * keep[0]
    if d == inner - 1:
        v = v * keep[1]
    return v


def forward(n, keep, w_ref, fb, fa, out_a, out_b, act_b, act_a):
    inner = n - 2
    for p in range(n):
        act_b[p] = silu(fb[p])

    def one(d, v):
        out = mask(d, wide(fa[d]) + v, inner, keep).astype(BF16)
        out_a[d] = out
        act_a[d] = silu(out)

    conv_planes(w_ref.at[0], act_b, 0, inner, one)

    def two(d, v):
        out_b[d] = (wide(fb[d + 2]) + v).astype(BF16)

    conv_planes(w_ref.at[1], act_a, 0, inner - 2, two)


def backward(n, keep, w_ref, bb, ba, db, da, rec_a, rec_b, grad_a, grad_b, act_b, act_a):
    inner = n - 2
    for p in range(n):
        act_b[p] = silu(bb[p])

    def one(d, v):
        out = mask(d, wide(ba[d]) - v, inner, keep).astype(BF16)
        rec_a[d] = out
        act_a[d] = silu(out)

    conv_planes(w_ref.at[1], act_b, 0, inner, one)

    def two(d, v):
        grad_a[d] = mask(d, wide(da[d]) + slope(bb[d + 1]) * v, inner, keep).astype(BF16)

    conv_planes(w_ref.at[3], db, 0, inner, two)

    def three(d, v):
        rec_b[d] = (wide(bb[d + 2]) - v).astype(BF16)

    conv_planes(w_ref.at[0], act_a, 0, inner - 2, three)

    def four(d, v):
        grad_b[d] = (wide(db[d + 2]) + slope(rec_a[d + 1]) * v).astype(BF16)

    conv_planes(w_ref.at[2], grad_a, 0, inner - 2, four)


class Copies:
    def __init__(self, sems):
        self.sems, self.groups, self.n = (sems, [], 0)

    def add(self, pairs, when=None):
        pairs = list(pairs)
        made = [pltpu.make_async_copy(src, dst, self.sems.at[self.n + k]) for k, (src, dst) in enumerate(pairs)]
        self.n += len(made)
        self.groups.append((when, made))

    def each(self, what):
        for when, made in self.groups:
            def run(made=made):
                for copy in made:
                    getattr(copy, what)()

            if when is None:
                run()
            else:
                pl.when(when)(run)

    def start(self):
        self.each("start")

    def wait(self):
        self.each("wait")

    def run(self):
        self.start()
        self.wait()


def at(ref, first, count):
    return ref.at[pl.ds(first, count)]


def window1(zh, b, a, nat_b, nat_a, swp_b, swp_a, near_b, near_a, far_b, far_a):
    return [
        (nat_b, at(b, 2 + 2 * zh, 2)),
        (swp_b, at(b, 4 - 2 * zh, 2)),
        (near_b, at(b, 6 - 6 * zh, 2)),
        (far_b, at(b, 6 * zh, 2)),
        (nat_a, at(a, 1 + 2 * zh, 2)),
        (swp_a, at(a, 3 - 2 * zh, 2)),
        (near_a, at(a, 5 - 5 * zh, 1)),
        (far_a, at(a, 5 * zh, 1)),
    ]


def special(zh, b, a, own, sp1, sp2):
    return [
        (own.at[1], at(b, 2, 2)),
        (sp1.at[1], at(b, 4 - 4 * zh, 2)),
        (sp2.at[1], at(b, 4 * zh, 2)),
        (own.at[0], at(a, 1, 2)),
        (at(sp1.at[0], zh, 1), at(a, 3 - 3 * zh, 1)),
        (at(sp2.at[0], 1 - zh, 1), at(a, 3 * zh, 1)),
    ]


def keeps(flags):
    return (flags[1].astype(F32), flags[2].astype(F32))


def tick1_back(flags, w_ref, nat, swp, near, far, bm, bd, h4, u4, e1p, *scratch):
    bb, ba, db, da, rec_a, rec_b, grad_a, grad_b, act_b, act_a, sems = scratch
    zh, bz = (flags[0], flags[4])
    load = Copies(sems)
    for k, (b, a) in enumerate(((bb, ba), (db, da))):
        load.add(
            window1(
                zh, b, a, nat.at[k], nat.at[2 + k], swp.at[k], swp.at[2 + k],
                at(near, 2 * k, 2), at(near, 4 + k, 1), at(far, 2 * k, 2), at(far, 4 + k, 1),
            )
        )
    load.run()
    backward(8, keeps(flags), w_ref, bb, ba, db, da, rec_a, rec_b, grad_a, grad_b, act_b, act_a)
    save = Copies(sems)
    save.add([
        (rec_b, at(bm, 0, 4)),
        (grad_b, at(bm, 4, 4)),
        (at(rec_a, 2 * bz, 4), at(bm, 8, 4)),
        (at(grad_a, 2 * bz, 4), at(bm, 12, 4)),
        (at(rec_b, 2 - 2 * bz, 2), at(bd, 0, 2)),
        (at(grad_b, 2 - 2 * bz, 2), at(bd, 2, 2)),
        (at(act_b, 1 + 2 * zh, 4), h4),
        (at(act_a, 2 * zh, 4), u4),
        (at(grad_a, 1 + 2 * zh, 2), e1p),
    ])
    save.run()


def tick1_forward(flags, w_ref, nat, swp, near, far, fm, fd, ld, y1w, *scratch):
    fb, fa, out_a, out_b, act_b, act_a, sems = scratch
    zh, fz = (flags[0], flags[3])
    load = Copies(sems)
    load.add(
        window1(
            zh, fb, fa, nat.at[0], nat.at[1], swp.at[0], swp.at[1],
            at(near, 6, 2), at(near, 8, 1), at(far, 0, 2), at(far, 2, 1),
        )
    )
    load.run()
    forward(8, keeps(flags), w_ref, fb, fa, out_a, out_b, act_b, act_a)
    save = Copies(sems)
    save.add([
        (out_b, at(fm, 0, 4)),
        (at(out_a, 2 * fz, 4), at(fm, 4, 4)),
        (at(out_b, 2 - 2 * fz, 2), fd),
        (at(out_a, 3 - zh, 1), at(ld, zh, 1)),
        (at(out_b, 3 - 3 * zh, 1), at(ld, 1 - zh, 1)),
        (out_a, y1w),
    ])
    save.run()


def tick2_back(
    scale, flags, w_ref, order, bm, bd, sp1, sp2, last_own, y1w, own, ld, dw, out, parts, *scratch
):
    bb, ba, db, da, rec_a, rec_b, grad_a, grad_b, act_b, act_a, sems = scratch
    zh, last = (flags[0], flags[4] == 1)
    main, halo = (2 - 2 * zh, 4 * zh)
    load = Copies(sems)
    load.add(
        special(zh, db, da, last_own, sp1, sp2)
        + [
            (at(y1w, zh, 5), at(bb, 1 - zh, 5)),
            (at(ld, zh, 1), at(bb, 5 * zh, 1)),
            (at(own, zh, 3), at(ba, 1 - zh, 3)),
            (at(ld, 1 - zh, 1), at(ba, 3 * zh, 1)),
        ],
        last,
    )
    load.add(
        [
            (at(bm, 0, 4), at(bb, main, 4)),
            (at(bd, 0, 2), at(bb, halo, 2)),
            (at(bm, 4, 4), at(db, main, 4)),
            (at(bd, 2, 2), at(db, halo, 2)),
            (at(bm, 8, 4), ba),
            (at(bm, 12, 4), da),
        ],
        flags[4] == 0,
    )
    load.run()
    backward(6, keeps(flags), w_ref, bb, ba, db, da, rec_a, rec_b, grad_a, grad_b, act_b, act_a)
    save = Copies(sems)
    save.add([
        (rec_b, at(out, 0, 2)),
        (at(rec_a, 1, 2), at(out, 2, 2)),
        (at(grad_a, 1, 2), at(out, 4, 2)),
        (grad_b, at(out, 6, 2)),
    ])
    save.start()
    sums = [
        dw[0] + wgrad_pair(at(grad_a, 1, 2), act_a),
        dw[1] + wgrad_pair(at(db, 2, 2), at(act_b, 1, 4)),
    ]
    sums = jnp.concatenate([(v * scale).astype(BF16) for v in sums], axis=0)
    ordered = jnp.dot(order[...], sums, preferred_element_type=F32).astype(BF16)
    parts[:, :, : 3 * C] = ordered.reshape(*parts.shape[:2], 3 * C)
    parts[:, :, 3 * C :] = jnp.zeros((*parts.shape[:2], W - 3 * C), BF16)
    save.wait()


def tick2_forward(flags, w_ref, fm, fd, sp1, sp2, first_own, out, *scratch):
    fb, fa, out_a, out_b, act_b, act_a, sems = scratch
    zh, first = (flags[0], flags[3])
    main, halo = (2 - 2 * zh, 4 * zh)
    load = Copies(sems)
    load.add(special(zh, fb, fa, first_own, sp1, sp2), first == 1)
    load.add(
        [(at(fm, 0, 4), at(fb, main, 4)), (fd, at(fb, halo, 2)), (at(fm, 4, 4), fa)],
        first == 0,
    )
    load.run()
    forward(6, keeps(flags), w_ref, fb, fa, out_a, out_b, act_b, act_a)
    out[0] = out_a[1]
    out[1] = out_a[2]
    out[2] = out_b[0]
    out[3] = out_b[1]


def wgrad_pair(g_ref, u_ref):
    lane = lax.broadcasted_iota(jnp.int32, (C, W), 1)
    zero = jnp.zeros((C, W), BF16)
    left, right = ([], [])
    for d in range(2):
        for h in range(H):
            g = wide(g_ref[d, h * C : (h + 1) * C])
            down = jnp.where(lane < W - 1, pltpu.roll(g, W - 1, 1), 0.0)
            up = jnp.where(lane >= 1, pltpu.roll(g, 1, 1), 0.0)
            left.append(jnp.concatenate([down, g, up], axis=0).astype(BF16))
            rows = []
            for a in range(3):
                for b in range(3):
                    at = h + b - 1
                    rows.append(u_ref[d + a, at * C : (at + 1) * C] if 0 <= at < H else zero)
            right.append(jnp.concatenate(rows, axis=0))
    return lax.dot_general(
        jnp.concatenate(right, axis=1),
        jnp.concatenate(left, axis=1),
        (((1,), (1,)), ((), ())),
        preferred_element_type=F32,
    )


def wgrad_kernel(e1, u4, d2, h4, out):
    out[0] = wgrad_pair(e1, u4)
    out[1] = wgrad_pair(d2, h4)


def bands_kernel(rows, out):
    lane = lax.broadcasted_iota(jnp.int32, (C, R), 1)
    for kind in range(4):
        for c in range(3):
            for a in range(3):
                tile = wide(rows[kind, c, :, a * R : (a + 1) * R])
                for h in range(H):
                    moved = tile if h == 1 else pltpu.roll(tile, ((h - 1) * C) % R, 1)
                    if h == 0:
                        moved = jnp.where(lane < 2 * C, moved, 0.0)
                    if h == 3:
                        moved = jnp.where(lane >= 2 * C, moved, 0.0)
                    at_row = (c * H + h) * C
                    out[kind, at_row : at_row + C, a * R : (a + 1) * R] = moved.astype(BF16)


VMEM = pl.BlockSpec(memory_space=pltpu.VMEM)
SMEM = pl.BlockSpec(memory_space=pltpu.SMEM)
HBM = pl.BlockSpec(memory_space=pltpu.HBM)


def call(kernel, outs, scratch, args, flops, specs, out_specs):
    return pl.pallas_call(
        kernel,
        out_shape=tuple(jax.ShapeDtypeStruct(s, t) for s, t in outs),
        in_specs=specs,
        out_specs=tuple(out_specs),
        scratch_shapes=scratch,
        compiler_params=pltpu.CompilerParams(vmem_limit_bytes=40 * 2**20),
        cost_estimate=pl.CostEstimate(flops=flops, bytes_accessed=4_000_000, transcendentals=400_000),
    )(*args)


def order_rows(slabs):
    per = C // slabs
    used = 2 * 9 * per
    rows = -(-used // 16) * 16
    out = np.zeros((slabs, rows, 2, 9, C), np.float32)
    for j in range(slabs):
        for p in range(2):
            for ab in range(9):
                for k in range(per):
                    out[j, (p * 9 + ab) * per + k, p, ab, j * per + k] = 1
    return jnp.asarray(out.reshape(slabs * rows, -1), BF16), rows


def planes(*lead):
    return pltpu.VMEM((*lead, R, W), BF16)


def shaped(*lead):
    return ((*lead, R, W), BF16)


def inside(value):
    s, _, d = value.shape[:3]
    return value.transpose(0, 2, 3, 1, 4).reshape(s, d, R, W)


def outside(value):
    s, d = value.shape[:2]
    return value.reshape(s, d, H, C, W).transpose(0, 3, 1, 2, 4)


def matrices(flat):
    k = flat.reshape(2, C, C, 3, 3, 3)
    turned = jnp.flip(k, (3, 4, 5)).transpose(0, 2, 1, 3, 4, 5)
    both = jnp.concatenate([k, turned])
    rows = both.transpose(0, 5, 1, 3, 4, 2)
    rows = jnp.pad(rows, ((0, 0), (0, 0), (0, 0), (0, 0), (0, 1), (0, 0))).reshape(4, 3, C, 3 * R)
    (out,) = call(bands_kernel, [((4, 3 * R, 3 * R), BF16)], [], (rows,), 1_000_000, [VMEM], [VMEM])
    return out


def local(fwd_in, back_out, back_grad, batch_next, loss_grad, weights):
    seg = lax.axis_index("segment")
    slab = lax.axis_index("slab")
    count = lax.axis_size("segment")
    slabs = lax.axis_size("slab")
    ny = slabs // 2
    y, zh = (slab // 2, slab % 2)
    scale = float(fwd_in.shape[3] * slabs * fwd_in.shape[4] * fwd_in.shape[5]) ** (-0.5)

    def route(value, to):
        pairs = []
        for s in range(count):
            for yy in range(ny):
                for zz in range(2):
                    target = to(s, yy, zz)
                    if target is None:
                        continue
                    ts, ty, tz = target
                    if 0 <= ts < count and 0 <= ty < ny:
                        pairs.append((s * slabs + 2 * yy + zz, ts * slabs + 2 * ty + tz))
        return lax.ppermute(value, ("segment", "slab"), pairs)

    def fwd_side(s, zz):
        return 1 - zz if s % SNAKE == SNAKE - 1 and s < count - 1 else zz

    def back_side(s, zz):
        return 1 - zz if s % SNAKE == 0 and s > 0 else zz

    fz = jnp.where((seg % SNAKE == SNAKE - 1) & (seg < count - 1), 1 - zh, zh)
    bz = jnp.where((seg % SNAKE == 0) & (seg > 0), 1 - zh, zh)
    is_first, is_last = (seg == 0, seg == count - 1)

    def swap(value):
        return route(value, lambda s, yy, zz: (s, yy, 1 - zz))

    def rim(value, high):
        n = value.shape[0] // 2
        return jnp.concatenate([value[:n].reshape(2 * n, R, W), jnp.where(high, value[n:, 1], value[n:, 0])])

    nat_b = jnp.stack([inside(v[0, k : k + 1])[0] for k, v in ((0, back_out), (1, back_grad), (1, back_out), (0, back_grad))])
    swp_b = swap(nat_b)
    nat_f = inside(fwd_in[0])[::-1]
    swp_f = swap(nat_f)
    near = route(
        jnp.concatenate([rim(nat_b, zh == 1), rim(nat_f, zh == 1)]), lambda s, yy, zz: (s, yy - 1 + 2 * zz, zz)
    )

    from_first, from_last = (14 % count, (count - 15) % count)
    first_own, last_own = (inside(batch_next), inside(loss_grad[0]))
    ends = jnp.where(seg == from_first, first_own, last_own)

    def end_of(s):
        return 0 if s == from_first else count - 1 if s == from_last else -1

    sp1 = route(ends, lambda s, yy, zz: (end_of(s), yy, 1 - zz))
    sp2 = route(ends, lambda s, yy, zz: (end_of(s), yy + (1 if zz == 1 else -1), 1 - zz))
    mats = matrices(weights[0])

    def as_flags(*values):
        return jnp.stack([jnp.asarray(v).astype(jnp.int32) for v in values])

    flags1 = as_flags(zh, y > 0, y < ny - 1, fz, bz)
    flags2 = as_flags(zh, (y > 0) | (zh == 1), (y < ny - 1) | (zh == 0), is_first, is_last)
    order, rows = order_rows(slabs)

    swp_b, near, sp1, sp2, mats = lax.optimization_barrier((swp_b, near, sp1, sp2, mats))

    def onward(value):
        return route(rim(value, zh == 0), lambda s, yy, zz: (s, yy + 1 - 2 * zz, zz))

    far_b = onward(swp_b)
    sems = pltpu.SemaphoreType.DMA((20,))
    bm, bd, h4, u4, e1p = call(
        tick1_back,
        [shaped(16), shaped(4), shaped(4), shaped(4), shaped(2)],
        [planes(8), planes(6), planes(8), planes(6), planes(6), planes(4), planes(6), planes(4), planes(8), planes(6), sems],
        (flags1, mats, nat_b, swp_b, near, far_b),
        2_000_000_000,
        [SMEM, VMEM] + [HBM] * 4,
        [HBM] * 5,
    )

    def fwd_diag(s, yy, zz):
        r = fwd_side(s, zz)
        return (s + 1, yy + 1 - 2 * r, r)

    def back_diag(s, yy, zz):
        r = back_side(s, zz)
        return (s - 1, yy + 1 - 2 * r, r)

    bm2 = route(bm, lambda s, yy, zz: (s - 1, yy, back_side(s, zz)))
    bd2 = route(bd, back_diag)
    (dw,) = call(
        wgrad_kernel, [((2, 9 * C, 3 * C), F32)], [], (e1p, u4, nat_b[1], h4), 300_000_000, [VMEM] * 4, [VMEM]
    )

    swp_f, bm = lax.optimization_barrier((swp_f, bm))
    far_f = onward(swp_f)
    fm, fd, ld, y1w = call(
        tick1_forward,
        [shaped(8), shaped(2), shaped(2), shaped(6)],
        [planes(8), planes(6), planes(6), planes(4), planes(8), planes(6), sems],
        (flags1, mats, nat_f, swp_f, near, far_f),
        1_000_000_000,
        [SMEM, VMEM] + [HBM] * 4,
        [HBM] * 4,
    )
    ld2 = route(ld, lambda s, yy, zz: (s if s == count - 1 else -1, yy + 1 - 2 * zz, zz))
    fd2 = route(fd, fwd_diag)
    fm2 = route(fm, lambda s, yy, zz: (s + 1, yy, fwd_side(s, zz)))

    out_b, parts = call(
        functools.partial(tick2_back, scale),
        [shaped(8), ((slabs, rows, W), BF16)],
        [planes(6), planes(4), planes(6), planes(4), planes(4), planes(2), planes(4), planes(2), planes(6), planes(4), sems],
        (flags2, mats, order, bm2, bd2, sp1, sp2, last_own, y1w, fm, ld2, dw),
        1_500_000_000,
        [SMEM, VMEM, VMEM] + [HBM] * 8 + [VMEM],
        [HBM, VMEM],
    )
    back = route(out_b, lambda s, yy, zz: (s - 1, yy, zz))
    parts = lax.all_to_all(parts, "slab", 0, 0, tiled=True)

    fm2, out_b = lax.optimization_barrier((fm2, out_b))
    (out_f,) = call(
        tick2_forward,
        [shaped(4)],
        [planes(6), planes(4), planes(4), planes(2), planes(6), planes(4), sems],
        (flags2, mats, fm2, fd2, sp1, sp2, first_own),
        700_000_000,
        [SMEM, VMEM] + [HBM] * 5,
        [VMEM],
    )

    total = jnp.sum(wide(parts), axis=0)[: 2 * 9 * (C // slabs), : 3 * C]
    total = total.reshape(2, 9, C // slabs, 3, C).transpose(0, 4, 2, 1, 3).reshape(1, 2, C, -1)

    fwd_out = outside(out_f.reshape(2, 2, R, W))
    back = outside(back.reshape(4, 2, R, W))
    acts = jnp.where(is_last, fwd_out, back[:2])
    grads = jnp.where(is_last, loss_grad[1], back[2:])
    return (fwd_out[None], acts[None], grads[None], total)


def solution(mesh):
    placed = (
        P("segment", None, None, "slab", None, None),
        P("segment", None, None, "slab", None, None),
        P("segment", None, None, "slab", None, None),
        P(None, None, "slab", None, None),
        P(None, None, None, "slab", None, None),
        P("segment", None, None, None),
    )
    return jax.shard_map(
        local,
        mesh=mesh,
        in_specs=placed,
        out_specs=(
            P("segment", None, None, "slab", None, None),
            P("segment", None, None, "slab", None, None),
            P("segment", None, None, "slab", None, None),
            P("segment", None, None, "slab"),
        ),
        check_vma=False,
    )
```

time: 155 us -> 133 us (0.86)
  the two profiles are of different devices: /device:TPU:36 before, /device:TPU:62 now
where the time goes in v1:
time: 133 us; the launch traced here: 132 us
  starting transfers between devices  59 us (44%)
  waiting for transfers between devices  28.7 us (22%)
  local copies, waits for them, and re-layouts  21.1 us (16%)
  Pallas kernels  16.3 us (12%)
  other arithmetic  5.18 us (4%)
  between operations  1.39 us (1%)
    ppermute x13, starting transfers between devices, route(): return lax.ppermute(value, ('segment', 'slab'), pairs)  47.1 us
    ppermute x13, waiting for transfers between devices, route(): return lax.ppermute(value, ('segment', 'slab'), pairs)  28.7 us
    pallas_call x6, Pallas kernels, call(): pl.pallas_call(kernel, out_shape=tuple((jax.ShapeDtypeStruct(s, t) for s,...  16.3 us
    all_to_all x1, starting transfers between devices, local(): parts = lax.all_to_all(parts, 'slab', 0, 0, tiled=True)  11.9 us
    unnamed x47, local copies, waits for them, and re-layouts  10.9 us
    transpose x10, local copies, waits for them, and re-layouts, inside(): return value.transpose(0, 2, 3, 1, 4).reshape(s, d, R, W)  2.9 us
  transfers between devices with their start and end apart: 14, of which 4 were waited for; matrix products, arithmetic and copies ran while one was open for 8% of the time, Pallas kernels for 9%

profile of v1, /device:TPU:62, one launch (start us, length us, event | category | flops | bytes accessed | tf_op | source)
XLA Modules:
  0.0 131.7 jit_solution(17816150530894809725)
XLA Ops:
  5.3 2.7 %collective-permute-start.1 = (bf16[9,128,128]{2,1,0:T(8,128)(2,1)}, bf16[9,128,128]{2,1,0:T(8,128)(2,1)S(1)}, u32[]{:S(2)}, u32[]{:S(2)}) collective-permute-start(bf16[9,128,128]{2,1,0:T(8,128)(2,1)} %pad_maximum_fusion), channel_id=1, source_target_pairs={{1,3},{2,0},{3,5},{4,2},{5,7},{6,4},{9,11},{10,8},{11,13},{12,10},... | collective-permute-start | bytes 884744 | tf_op jit(solution)/shard_map/ppermute | solution.py:412
  8.7 13.4 %collective-permute-start = (bf16[4,2,128,128]{3,2,0,1:T(8,128)(2,1)}, bf16[4,2,128,128]{3,2,0,1:T(8,128)(2,1)}, u32[]{:S(2)}, u32[]{:S(2)}) collective-permute-start(bf16[4,2,128,128]{3,2,0,1:T(8,128)(2,1)} %pad_maximum_fusion.1), channel_id=1, source_target_pairs={{0,1},{1,0},{2,3},{3,2},{4,5},{5,4},{6,7},{7,6},{8,9},{9,8},{10,11... | collective-permute-start | bytes 786440 | tf_op jit(solution)/shard_map/ppermute | solution.py:412
  26.1 1.1 maximum_bitcast_fusion
  27.2 1.1 copy.46
  30.1 14.8 %collective-permute-done = bf16[4,2,128,128]{3,2,0,1:T(8,128)(2,1)} collective-permute-done((bf16[4,2,128,128]{3,2,0,1:T(8,128)(2,1)}, bf16[4,2,128,128]{3,2,0,1:T(8,128)(2,1)}, u32[]{:S(2)}, u32[]{:S(2)}) %collective-permute-start) | collective-permute-done | bytes 262176 | tf_op jit(solution)/shard_map/ppermute | solution.py:412
  46.8 1.3 collective-permute-start.5
  48.1 16.3 %collective-permute-start.4 = (bf16[2,2,128,128]{3,2,1,0:T(8,128)(2,1)S(1)}, bf16[2,2,128,128]{3,2,1,0:T(8,128)(2,1)S(1)}, u32[]{:S(2)}, u32[]{:S(2)}) collective-permute-start(bf16[2,2,128,128]{3,2,1,0:T(8,128)(2,1)S(1)} %rev.8.nat), channel_id=1, source_target_pairs={{0,1},{1,0},{2,3},{3,2},{4,5},{5,4},{6,7},{7,6},{8,9},{9,8},{10,11... | collective-permute-start | bytes 393224 | tf_op jit(solution)/shard_map/ppermute | solution.py:412
  64.4 1.0 copy.39.nat
  65.5 1.0 copy.40.swp
  66.5 4.7 %shard_map.103 = (bf16[16,128,128]{2,1,0:T(8,128)(2,1)S(1)}, bf16[4,128,128]{2,1,0:T(8,128)(2,1)}, bf16[4,128,128]{2,1,0:T(8,128)(2,1)S(1)}, bf16[4,128,128]{2,1,0:T(8,128)(2,1)S(1)}, bf16[2,128,128]{2,1,0:T(8,128)(2,1)S(1)}) custom-call(s32[5]{0:T(128)S(1)} %stack.78.flags, bf16[4,384,384]{2,1,0:T(8,128)(2,1)S(1)} %shard_map.102.w_ref, ...), custom_call_target="tpu_custom_call" | custom-call | flops 2000000000 | bytes 4000000 | tf_op jit(solution)/shard_map/pallas_call | solution.py:340
  71.9 1.9 %collective-permute-start.8 = (bf16[16,128,128]{2,1,0:T(8,128)(2,1)S(1)}, bf16[16,128,128]{2,1,0:T(8,128)(2,1)S(1)}, u32[]{:S(2)}, u32[]{:S(2)}) collective-permute-start(bf16[16,128,128]{2,1,0:T(8,128)(2,1)S(1)} %get-tuple-element.25), channel_id=1, source_target_pairs={{8,0},{9,1},{10,2},{11,3},{12,4},{13,5},{14,6},{15,7},{16,8},{17,9... | collective-permute-start | bytes 1572872 | tf_op jit(solution)/shard_map/ppermute | solution.py:412
  73.8 1.3 collective-permute-start.6
  75.1 1.4 %collective-permute-start.9 = (bf16[4,128,128]{2,1,0:T(8,128)(2,1)}, bf16[4,128,128]{2,1,0:T(8,128)(2,1)}, u32[]{:S(2)}, u32[]{:S(2)}) collective-permute-start(bf16[4,128,128]{2,1,0:T(8,128)(2,1)} %get-tuple-element.28), channel_id=1, source_target_pairs={{8,2},{10,4},{11,1},{12,6},{13,3},{15,5},{16,10},{18,12},{19,9},{2... | collective-permute-start | bytes 393224 | tf_op jit(solution)/shard_map/ppermute | solution.py:412
  76.6 4.3 %collective-permute-done.6.far = bf16[3,128,128]{2,1,0:T(8,128)(2,1)S(1)} collective-permute-done((bf16[3,128,128]{2,1,0:T(8,128)(2,1)S(1)}, bf16[3,128,128]{2,1,0:T(8,128)(2,1)S(1)}, u32[]{:S(2)}, u32[]{:S(2)}) %collective-permute-start.6) | collective-permute-done | bytes 98336 | tf_op jit(solution)/shard_map/ppermute | solution.py:412
  80.9 3.5 %shard_map.104 = (bf16[8,128,128]{2,1,0:T(8,128)(2,1)S(1)}, bf16[2,128,128]{2,1,0:T(8,128)(2,1)S(1)}, bf16[2,128,128]{2,1,0:T(8,128)(2,1)}, bf16[6,128,128]{2,1,0:T(8,128)(2,1)S(1)}) custom-call(s32[5]{0:T(128)S(1)} %stack.78.flags, bf16[4,384,384]{2,1,0:T(8,128)(2,1)S(1)} %shard_map.102.w_ref, bf16[2,2,128,128]{3,2,1,0:T(8,128)(2,1)S(1)} %rev.8.nat, ...), custom_call_target="tpu_custom_call" | custom-call | flops 1000000000 | bytes 4000000 | tf_op jit(solution)/shard_map/pallas_call | solution.py:340
  91.4 1.1 copy-done.7
  93.5 5.0 %shard_map.106 = (bf16[8,128,128]{2,1,0:T(8,128)(2,1)S(1)}, bf16[8,80,128]{2,1,0:T(8,128)(2,1)}) custom-call(s32[5]{0:T(128)S(1)} %stack.68.flags, bf16[4,384,384]{2,1,0:T(8,128)(2,1)S(1)} %shard_map.102.w_ref, bf16[640,576]{1,0:T(8,128)(2,1)S(1)} %copy-done.7, bf16[16,128,128]{2,1,0:T(8,128)(2,1)S(1)} %collective-permute-done.8.bm, ...), custom_call_target="tpu_custom_call" | custom-call | flops 1500000000 | bytes 4000000 | tf_op jit(solution)/shard_map/pallas_call | solution.py:340
  98.5 11.9 %all-to-all-start = ((bf16[8,80,128]{2,1,0:T(8,128)(2,1)}), bf16[8,80,128]{2,1,0:T(8,128)(2,1)S(1)}, u32[]{:S(2)}, u32[]{:S(2)}) async-start(bf16[8,80,128]{2,1,0:T(8,128)(2,1)} %get-tuple-element.39), calls=%async_computation | async-start | bytes 327680 | tf_op jit(solution)/shard_map/all_to_all | solution.py:513
  110.4 1.9 %collective-permute-start.7 = (bf16[8,128,128]{2,1,0:T(8,128)(2,1)S(1)}, bf16[8,128,128]{2,1,0:T(8,128)(2,1)S(1)}, u32[]{:S(2)}, u32[]{:S(2)}) collective-permute-start(bf16[8,128,128]{2,1,0:T(8,128)(2,1)S(1)} %copy-done.1), channel_id=1, source_target_pairs={{0,8},{1,9},{2,10},{3,11},{4,12},{5,13},{6,14},{7,15},{8,16},{9,17... | collective-permute-start | bytes 786440 | tf_op jit(solution)/shard_map/ppermute | solution.py:412
  112.3 3.6 %collective-permute-start.12 = (bf16[8,128,128]{2,1,0:T(8,128)(2,1)S(1)}, bf16[8,128,128]{2,1,0:T(8,128)(2,1)S(1)}, u32[]{:S(2)}, u32[]{:S(2)}) collective-permute-start(bf16[8,128,128]{2,1,0:T(8,128)(2,1)S(1)} %get-tuple-element.36), channel_id=1, source_target_pairs={{8,0},{9,1},{10,2},{11,3},{12,4},{13,5},{14,6},{15,7},{16,8},{17,9... | collective-permute-start | bytes 786440 | tf_op jit(solution)/shard_map/ppermute | solution.py:412
  116.0 1.3 collective-permute-start.11
  117.3 8.3 %collective-permute-done.7.fm = bf16[8,128,128]{2,1,0:T(8,128)(2,1)S(1)} collective-permute-done((bf16[8,128,128]{2,1,0:T(8,128)(2,1)S(1)}, bf16[8,128,128]{2,1,0:T(8,128)(2,1)S(1)}, u32[]{:S(2)}, u32[]{:S(2)}) %collective-permute-start.7) | collective-permute-done | bytes 262176 | tf_op jit(solution)/shard_map/ppermute | solution.py:412
  125.6 1.1 collective-permute-done.11.fd
  126.8 2.3 %shard_map.107 = bf16[4,128,128]{2,1,0:T(8,128)(2,1)S(1)} custom-call(s32[5]{0:T(128)S(1)} %stack.68.flags, bf16[4,384,384]{2,1,0:T(8,128)(2,1)S(1)} %shard_map.102.w_ref, bf16[8,128,128]{2,1,0:T(8,128)(2,1)S(1)} %collective-permute-done.7.fm, bf16[2,128,128]{2,1,0:T(8,128)(2,1)S(1)} %collective-permute-done.11.fd, ...), custom_call_target="tpu_custom_call" | custom-call | flops 700000000 | bytes 4000000 | tf_op jit(solution)/shard_map/pallas_call | solution.py:340
  (100 shorter events, 23.7 us)
Async XLA Ops:
  4.4 17.8 %copy-start.18 = (bf16[2,2,32,2,4,128]{5,4,3,2,1,0:T(4,128)(2,1)S(1)}, bf16[2,2,32,2,4,128]{5,4,3,2,1,0:T(4,128)(2,1)}, u32[]{:S(2)}) copy-start(bf16[2,2,32,2,4,128]{5,4,3,2,1,0:T(4,128)(2,1)} %param.11) | copy-start | bytes 786436
  4.5 17.8 %copy-start.20 = (bf16[2,32,2,4,128]{4,3,2,1,0:T(4,128)(2,1)S(1)}, bf16[2,32,2,4,128]{4,3,2,1,0:T(4,128)(2,1)}, u32[]{:S(2)}) copy-start(bf16[2,32,2,4,128]{4,3,2,1,0:T(4,128)(2,1)} %param.10) | copy-start | bytes 393220
  4.6 19.8 %copy-start.21 = (bf16[1,2,32,864]{3,2,1,0:T(8,128)(2,1)S(1)}, bf16[1,2,32,864]{3,2,1,0:T(8,128)(2,1)}, u32[]{:S(2)}) copy-start(bf16[1,2,32,864]{3,2,1,0:T(8,128)(2,1)} %param.12) | copy-start | bytes 331780
  5.3 39.6 %collective-permute-start.1 = (bf16[9,128,128]{2,1,0:T(8,128)(2,1)}, bf16[9,128,128]{2,1,0:T(8,128)(2,1)S(1)}, u32[]{:S(2)}, u32[]{:S(2)}) collective-permute-start(bf16[9,128,128]{2,1,0:T(8,128)(2,1)} %pad_maximum_fusion), channel_id=1, source_target_pairs={{1,3},{2,0},{3,5},{4,2},{5,7},{6,4},{9,11},{10,8},{11,13},{12,10},... | collective-permute-start | bytes 884744 | tf_op jit(solution)/shard_map/ppermute | solution.py:412
  8.7 36.2 %collective-permute-start = (bf16[4,2,128,128]{3,2,0,1:T(8,128)(2,1)}, bf16[4,2,128,128]{3,2,0,1:T(8,128)(2,1)}, u32[]{:S(2)}, u32[]{:S(2)}) collective-permute-start(bf16[4,2,128,128]{3,2,0,1:T(8,128)(2,1)} %pad_maximum_fusion.1), channel_id=1, source_target_pairs={{0,1},{1,0},{2,3},{3,2},{4,5},{5,4},{6,7},{7,6},{8,9},{9,8},{10,11... | collective-permute-start | bytes 786440 | tf_op jit(solution)/shard_map/ppermute | solution.py:412
  23.0 7.0 %collective-permute-start.2 = (bf16[2,2,128,128]{3,2,1,0:T(8,128)(2,1)}, bf16[2,2,128,128]{3,2,1,0:T(8,128)(2,1)S(1)}, u32[]{:S(2)}, u32[]{:S(2)}) collective-permute-start(bf16[2,2,128,128]{3,2,1,0:T(8,128)(2,1)} %broadcast_select_fusion), channel_id=1, source_target_pairs={{112,1},{113,0},{114,3},{115,2},{116,5},{117,4},{118,7},{119,6},{3... | collective-permute-start | bytes 393224 | tf_op jit(solution)/shard_map/ppermute | solution.py:412
  23.7 6.4 %collective-permute-start.3 = (bf16[2,2,128,128]{3,2,1,0:T(8,128)(2,1)}, bf16[2,2,128,128]{3,2,1,0:T(8,128)(2,1)S(1)}, u32[]{:S(2)}, u32[]{:S(2)}) collective-permute-start(bf16[2,2,128,128]{3,2,1,0:T(8,128)(2,1)} %broadcast_select_fusion), channel_id=1, source_target_pairs={{113,2},{114,1},{115,4},{116,3},{117,6},{118,5},{393,506},{394,505... | collective-permute-start | bytes 393224 | tf_op jit(solution)/shard_map/ppermute | solution.py:412
  29.7 18.4 %copy-start.17 = (bf16[2,2,4,32,128]{4,3,2,1,0:T(8,128)(2,1)S(1)}, bf16[2,2,4,32,128]{4,3,2,1,0:T(8,128)(2,1)}, u32[]{:S(2)}) copy-start(bf16[2,2,4,32,128]{4,3,2,1,0:T(8,128)(2,1)} %copy-done.16) | copy-start | bytes 393220
  30.0 16.7 %copy-start.2 = (bf16[2,2,128,128]{3,2,1,0:T(8,128)(2,1)}, bf16[2,2,128,128]{3,2,1,0:T(8,128)(2,1)S(1)}, u32[]{:S(2)}) copy-start(bf16[2,2,128,128]{3,2,1,0:T(8,128)(2,1)S(1)} %collective-permute-done.3.sp2) | copy-start | bytes 393220
  46.8 19.7 %collective-permute-start.5 = (bf16[6,128,128]{2,1,0:T(8,128)(2,1)S(1)}, bf16[6,128,128]{2,1,0:T(8,128)(2,1)S(1)}, u32[]{:S(2)}, u32[]{:S(2)}) collective-permute-start(bf16[6,128,128]{2,1,0:T(8,128)(2,1)S(1)} %pad_maximum_fusion.2), channel_id=1, source_target_pairs={{0,2},{2,4},{3,1},{4,6},{5,3},{7,5},{8,10},{10,12},{11,9},{12,14},... | collective-permute-start | bytes 589832 | tf_op jit(solution)/shard_map/ppermute | solution.py:412
  48.1 25.7 %collective-permute-start.4 = (bf16[2,2,128,128]{3,2,1,0:T(8,128)(2,1)S(1)}, bf16[2,2,128,128]{3,2,1,0:T(8,128)(2,1)S(1)}, u32[]{:S(2)}, u32[]{:S(2)}) collective-permute-start(bf16[2,2,128,128]{3,2,1,0:T(8,128)(2,1)S(1)} %rev.8.nat), channel_id=1, source_target_pairs={{0,1},{1,0},{2,3},{3,2},{4,5},{5,4},{6,7},{7,6},{8,9},{9,8},{10,11... | collective-permute-start | bytes 393224 | tf_op jit(solution)/shard_map/ppermute | solution.py:412
  71.9 12.6 %copy-start.8 = (bf16[4,128,128]{2,1,0:T(8,128)(2,1)}, bf16[4,128,128]{2,1,0:T(8,128)(2,1)S(1)}, u32[]{:S(2)}) copy-start(bf16[4,128,128]{2,1,0:T(8,128)(2,1)S(1)} %get-tuple-element.35.h4) | copy-start | bytes 393220
  71.9 12.6 %copy-start.10 = (bf16[4,128,128]{2,1,0:T(8,128)(2,1)}, bf16[4,128,128]{2,1,0:T(8,128)(2,1)S(1)}, u32[]{:S(2)}) copy-start(bf16[4,128,128]{2,1,0:T(8,128)(2,1)S(1)} %get-tuple-element.34.u4) | copy-start | bytes 393220
  71.9 18.6 %collective-permute-start.8 = (bf16[16,128,128]{2,1,0:T(8,128)(2,1)S(1)}, bf16[16,128,128]{2,1,0:T(8,128)(2,1)S(1)}, u32[]{:S(2)}, u32[]{:S(2)}) collective-permute-start(bf16[16,128,128]{2,1,0:T(8,128)(2,1)S(1)} %get-tuple-element.25), channel_id=1, source_target_pairs={{8,0},{9,1},{10,2},{11,3},{12,4},{13,5},{14,6},{15,7},{16,8},{17,9... | collective-permute-start | bytes 1572872 | tf_op jit(solution)/shard_map/ppermute | solution.py:412
  73.8 7.1 %collective-permute-start.6 = (bf16[3,128,128]{2,1,0:T(8,128)(2,1)S(1)}, bf16[3,128,128]{2,1,0:T(8,128)(2,1)S(1)}, u32[]{:S(2)}, u32[]{:S(2)}) collective-permute-start(bf16[3,128,128]{2,1,0:T(8,128)(2,1)S(1)} %pad_maximum_fusion.4), channel_id=1, source_target_pairs={{0,2},{2,4},{3,1},{4,6},{5,3},{7,5},{8,10},{10,12},{11,9},{12,14},... | collective-permute-start | bytes 294920 | tf_op jit(solution)/shard_map/ppermute | solution.py:412
  75.1 15.3 %copy-start.3 = (bf16[2,2,128,128]{3,2,1,0:T(8,128)(2,1)S(1)}, bf16[2,2,128,128]{3,2,1,0:T(8,128)(2,1)}, u32[]{:S(2)}) copy-start(bf16[2,2,128,128]{3,2,1,0:T(8,128)(2,1)} %copy-done.2) | copy-start | bytes 393220
  75.1 15.3 %collective-permute-start.9 = (bf16[4,128,128]{2,1,0:T(8,128)(2,1)}, bf16[4,128,128]{2,1,0:T(8,128)(2,1)}, u32[]{:S(2)}, u32[]{:S(2)}) collective-permute-start(bf16[4,128,128]{2,1,0:T(8,128)(2,1)} %get-tuple-element.28), channel_id=1, source_target_pairs={{8,2},{10,4},{11,1},{12,6},{13,3},{15,5},{16,10},{18,12},{19,9},{2... | collective-permute-start | bytes 393224 | tf_op jit(solution)/shard_map/ppermute | solution.py:412
  86.5 4.0 %collective-permute-start.10 = (bf16[2,128,128]{2,1,0:T(8,128)(2,1)}, bf16[2,128,128]{2,1,0:T(8,128)(2,1)S(1)}, u32[]{:S(2)}, u32[]{:S(2)}) collective-permute-start(bf16[2,128,128]{2,1,0:T(8,128)(2,1)} %get-tuple-element.32), channel_id=1, source_target_pairs={{504,506},{506,508},{507,505},{508,510},{509,507},{511,509}} | collective-permute-start | bytes 196616 | tf_op jit(solution)/shard_map/ppermute | solution.py:412
  93.5 22.5 %copy-start.6 = (bf16[2,128,128]{2,1,0:T(8,128)(2,1)S(1)}, bf16[2,128,128]{2,1,0:T(8,128)(2,1)}, u32[]{:S(2)}) copy-start(bf16[2,128,128]{2,1,0:T(8,128)(2,1)} %copy-done.5) | copy-start | bytes 196612
  93.5 33.3 %copy-start.4 = (bf16[2,2,128,128]{3,2,1,0:T(8,128)(2,1)S(1)}, bf16[2,2,128,128]{3,2,1,0:T(8,128)(2,1)}, u32[]{:S(2)}) copy-start(bf16[2,2,128,128]{3,2,1,0:T(8,128)(2,1)} %copy-done.2) | copy-start | bytes 393220
  98.5 32.3 %all-to-all-start = ((bf16[8,80,128]{2,1,0:T(8,128)(2,1)}), bf16[8,80,128]{2,1,0:T(8,128)(2,1)S(1)}, u32[]{:S(2)}, u32[]{:S(2)}) async-start(bf16[8,80,128]{2,1,0:T(8,128)(2,1)} %get-tuple-element.39), calls=%async_computation | async-start | bytes 327680 | tf_op jit(solution)/shard_map/all_to_all | solution.py:513
  110.4 15.2 %collective-permute-start.7 = (bf16[8,128,128]{2,1,0:T(8,128)(2,1)S(1)}, bf16[8,128,128]{2,1,0:T(8,128)(2,1)S(1)}, u32[]{:S(2)}, u32[]{:S(2)}) collective-permute-start(bf16[8,128,128]{2,1,0:T(8,128)(2,1)S(1)} %copy-done.1), channel_id=1, source_target_pairs={{0,8},{1,9},{2,10},{3,11},{4,12},{5,13},{6,14},{7,15},{8,16},{9,17... | collective-permute-start | bytes 786440 | tf_op jit(solution)/shard_map/ppermute | solution.py:412
  112.3 17.4 %collective-permute-start.12 = (bf16[8,128,128]{2,1,0:T(8,128)(2,1)S(1)}, bf16[8,128,128]{2,1,0:T(8,128)(2,1)S(1)}, u32[]{:S(2)}, u32[]{:S(2)}) collective-permute-start(bf16[8,128,128]{2,1,0:T(8,128)(2,1)S(1)} %get-tuple-element.36), channel_id=1, source_target_pairs={{8,0},{9,1},{10,2},{11,3},{12,4},{13,5},{14,6},{15,7},{16,8},{17,9... | collective-permute-start | bytes 786440 | tf_op jit(solution)/shard_map/ppermute | solution.py:412
  116.0 10.8 %collective-permute-start.11 = (bf16[2,128,128]{2,1,0:T(8,128)(2,1)S(1)}, bf16[2,128,128]{2,1,0:T(8,128)(2,1)S(1)}, u32[]{:S(2)}, u32[]{:S(2)}) collective-permute-start(bf16[2,128,128]{2,1,0:T(8,128)(2,1)S(1)} %copy-done.6), channel_id=1, source_target_pairs={{0,10},{2,12},{3,9},{4,14},{5,11},{7,13},{8,18},{10,20},{11,17},{1... | collective-permute-start | bytes 196616 | tf_op jit(solution)/shard_map/ppermute | solution.py:412
  (12 other events, 15.2 us)

commit v2 on v1

--- a/solution.py
+++ b/solution.py
@@ -2,7 +2,6 @@
 
 import jax
 import jax.numpy as jnp
-import numpy as np
 from jax import lax
 from jax.experimental import pallas as pl
 from jax.experimental.pallas import tpu as pltpu
@@ -154,10 +153,10 @@
 
 def special(zh, b, a, own, sp1, sp2):
     return [
-        (own.at[1], at(b, 2, 2)),
+        (own[1], at(b, 2, 2)),
         (sp1.at[1], at(b, 4 - 4 * zh, 2)),
         (sp2.at[1], at(b, 4 * zh, 2)),
-        (own.at[0], at(a, 1, 2)),
+        (own[0], at(a, 1, 2)),
         (at(sp1.at[0], zh, 1), at(a, 3 - 3 * zh, 1)),
         (at(sp2.at[0], 1 - zh, 1), at(a, 3 * zh, 1)),
     ]
@@ -167,15 +166,15 @@
     return (flags[1].astype(F32), flags[2].astype(F32))
 
 
-def tick1_back(flags, w_ref, nat, swp, near, far, bm, bd, h4, u4, e1p, *scratch):
+def tick1_back(flags, w_ref, nat, swp, near, far, bm, bd, dw, *scratch):
     bb, ba, db, da, rec_a, rec_b, grad_a, grad_b, act_b, act_a, sems = scratch
     zh, bz = (flags[0], flags[4])
     load = Copies(sems)
     for k, (b, a) in enumerate(((bb, ba), (db, da))):
         load.add(
             window1(
-                zh, b, a, nat.at[k], nat.at[2 + k], swp.at[k], swp.at[2 + k],
-                at(near, 2 * k, 2), at(near, 4 + k, 1), at(far, 2 * k, 2), at(far, 4 + k, 1),
+                zh, b, a, at(nat, 2 * k, 2), at(nat, 4 + 2 * k, 2), at(swp, 2 * k, 2), at(swp, 4 + 2 * k, 2),
+                at(near, 2 * k, 2), at(near, 4 + k, 1), at(far, 2 * k, 2), at(far, 5 + 2 * k - zh, 1),
             )
         )
     load.run()
@@ -188,21 +187,21 @@
         (at(grad_a, 2 * bz, 4), at(bm, 12, 4)),
         (at(rec_b, 2 - 2 * bz, 2), at(bd, 0, 2)),
         (at(grad_b, 2 - 2 * bz, 2), at(bd, 2, 2)),
-        (at(act_b, 1 + 2 * zh, 4), h4),
-        (at(act_a, 2 * zh, 4), u4),
-        (at(grad_a, 1 + 2 * zh, 2), e1p),
     ])
-    save.run()
-
-
-def tick1_forward(flags, w_ref, nat, swp, near, far, fm, fd, ld, y1w, *scratch):
+    save.start()
+    dw[0] = wgrad_pair(at(grad_a, 1 + 2 * zh, 2), at(act_a, 2 * zh, 4))
+    dw[1] = wgrad_pair(at(db, 2 + 2 * zh, 2), at(act_b, 1 + 2 * zh, 4))
+    save.wait()
+
+
+def tick1_forward(flags, w_ref, nat, swp, near, far, last_own, fm, fd, ld, y1w, *scratch):
     fb, fa, out_a, out_b, act_b, act_a, sems = scratch
     zh, fz = (flags[0], flags[3])
     load = Copies(sems)
     load.add(
         window1(
-            zh, fb, fa, nat.at[0], nat.at[1], swp.at[0], swp.at[1],
-            at(near, 6, 2), at(near, 8, 1), at(far, 0, 2), at(far, 2, 1),
+            zh, fb, fa, at(nat, 0, 2), at(nat, 2, 2), at(swp, 0, 2), at(swp, 2, 2),
+            at(near, 6, 2), at(near, 8, 1), at(far, 0, 2), at(far, 3 - zh, 1),
         )
     )
     load.run()
@@ -214,20 +213,22 @@
         (at(out_b, 2 - 2 * fz, 2), fd),
         (at(out_a, 3 - zh, 1), at(ld, zh, 1)),
         (at(out_b, 3 - 3 * zh, 1), at(ld, 1 - zh, 1)),
-        (out_a, y1w),
+        (out_a, at(y1w, 0, 6)),
+        (last_own.at[0], at(y1w, 6, 2)),
+        (last_own.at[1], at(y1w, 8, 2)),
     ])
     save.run()
 
 
 def tick2_back(
-    scale, flags, w_ref, order, bm, bd, sp1, sp2, last_own, y1w, own, ld, dw, out, parts, *scratch
+    scale, flags, w_ref, bm, bd, sp1, sp2, y1w, own, ld, dw, out, parts, *scratch
 ):
     bb, ba, db, da, rec_a, rec_b, grad_a, grad_b, act_b, act_a, sems = scratch
     zh, last = (flags[0], flags[4] == 1)
     main, halo = (2 - 2 * zh, 4 * zh)
     load = Copies(sems)
     load.add(
-        special(zh, db, da, last_own, sp1, sp2)
+        special(zh, db, da, (at(y1w, 6, 2), at(y1w, 8, 2)), sp1, sp2)
         + [
             (at(y1w, zh, 5), at(bb, 1 - zh, 5)),
             (at(ld, zh, 1), at(bb, 5 * zh, 1)),
@@ -247,25 +248,21 @@
         ],
         flags[4] == 0,
     )
-    load.run()
+    load.start()
+    order, back_order = (slab_order(parts.shape[0]), to_outside())
+    load.wait()
     backward(6, keeps(flags), w_ref, bb, ba, db, da, rec_a, rec_b, grad_a, grad_b, act_b, act_a)
-    save = Copies(sems)
-    save.add([
-        (rec_b, at(out, 0, 2)),
-        (at(rec_a, 1, 2), at(out, 2, 2)),
-        (at(grad_a, 1, 2), at(out, 4, 2)),
-        (grad_b, at(out, 6, 2)),
-    ])
-    save.start()
+    pieces = [rec_b[...], rec_a[1:3], grad_a[1:3], grad_b[...]]
+    for k, v in enumerate(reorder(back_order, [p.reshape(2 * R, W) for p in pieces])):
+        out[k] = v
     sums = [
         dw[0] + wgrad_pair(at(grad_a, 1, 2), act_a),
         dw[1] + wgrad_pair(at(db, 2, 2), at(act_b, 1, 4)),
     ]
     sums = jnp.concatenate([(v * scale).astype(BF16) for v in sums], axis=0)
-    ordered = jnp.dot(order[...], sums, preferred_element_type=F32).astype(BF16)
+    ordered = jnp.dot(order, sums, preferred_element_type=F32).astype(BF16)
     parts[:, :, : 3 * C] = ordered.reshape(*parts.shape[:2], 3 * C)
     parts[:, :, 3 * C :] = jnp.zeros((*parts.shape[:2], W - 3 * C), BF16)
-    save.wait()
 
 
 def tick2_forward(flags, w_ref, fm, fd, sp1, sp2, first_own, out, *scratch):
@@ -273,17 +270,15 @@
     zh, first = (flags[0], flags[3])
     main, halo = (2 - 2 * zh, 4 * zh)
     load = Copies(sems)
-    load.add(special(zh, fb, fa, first_own, sp1, sp2), first == 1)
+    load.add(special(zh, fb, fa, (first_own.at[0], first_own.at[1]), sp1, sp2), first == 1)
     load.add(
         [(at(fm, 0, 4), at(fb, main, 4)), (fd, at(fb, halo, 2)), (at(fm, 4, 4), fa)],
         first == 0,
     )
     load.run()
     forward(6, keeps(flags), w_ref, fb, fa, out_a, out_b, act_b, act_a)
-    out[0] = out_a[1]
-    out[1] = out_a[2]
-    out[2] = out_b[0]
-    out[3] = out_b[1]
+    for k, v in enumerate(reorder(to_outside(), [p.reshape(2 * R, W) for p in (out_a[1:3], out_b[...])])):
+        out[k] = v
 
 
 def wgrad_pair(g_ref, u_ref):
@@ -310,11 +305,6 @@
     )
 
 
-def wgrad_kernel(e1, u4, d2, h4, out):
-    out[0] = wgrad_pair(e1, u4)
-    out[1] = wgrad_pair(d2, h4)
-
-
 def bands_kernel(rows, out):
     lane = lax.broadcasted_iota(jnp.int32, (C, R), 1)
     for kind in range(4):
@@ -336,29 +326,28 @@
 HBM = pl.BlockSpec(memory_space=pltpu.HBM)
 
 
-def call(kernel, outs, scratch, args, flops, specs, out_specs):
+def call(kernel, outs, scratch, args, flops, specs, out_specs, mib=16):
     return pl.pallas_call(
         kernel,
         out_shape=tuple(jax.ShapeDtypeStruct(s, t) for s, t in outs),
         in_specs=specs,
         out_specs=tuple(out_specs),
         scratch_shapes=scratch,
-        compiler_params=pltpu.CompilerParams(vmem_limit_bytes=40 * 2**20),
+        compiler_params=pltpu.CompilerParams(vmem_limit_bytes=mib * 2**20),
         cost_estimate=pl.CostEstimate(flops=flops, bytes_accessed=4_000_000, transcendentals=400_000),
     )(*args)
 
 
-def order_rows(slabs):
+def slab_rows(slabs):
+    return -(-2 * 9 * C // (16 * slabs)) * 16
+
+
+def slab_order(slabs):
     per = C // slabs
-    used = 2 * 9 * per
-    rows = -(-used // 16) * 16
-    out = np.zeros((slabs, rows, 2, 9, C), np.float32)
-    for j in range(slabs):
-        for p in range(2):
-            for ab in range(9):
-                for k in range(per):
-                    out[j, (p * 9 + ab) * per + k, p, ab, j * per + k] = 1
-    return jnp.asarray(out.reshape(slabs * rows, -1), BF16), rows
+    low, rows = (per.bit_length() - 1, slab_rows(slabs))
+    return one_hot(
+        slabs * rows, 2 * 9 * C, lambda n: ((n & (C - 1)) >> low) * rows + (n >> 5) * per + (n & (per - 1))
+    )
 
 
 def planes(*lead):
@@ -369,14 +358,63 @@
     return ((*lead, R, W), BF16)
 
 
-def inside(value):
-    s, _, d = value.shape[:3]
-    return value.transpose(0, 2, 3, 1, 4).reshape(s, d, R, W)
-
-
-def outside(value):
-    s, d = value.shape[:2]
-    return value.reshape(s, d, H, C, W).transpose(0, 3, 1, 2, 4)
+def flat_rows(value):
+    return value.reshape(value.shape[0], -1, W)
+
+
+def one_hot(rows, cols, target):
+    row = lax.broadcasted_iota(jnp.int32, (rows, cols), 0)
+    col = lax.broadcasted_iota(jnp.int32, (rows, cols), 1)
+    return jnp.where(row == target(col), 1.0, 0.0).astype(BF16)
+
+
+def to_inside():
+    return one_hot(2 * R, 2 * R, lambda n: (n & 7) * C + (n >> 3))
+
+
+def to_outside():
+    return one_hot(2 * R, 2 * R, lambda n: (n & (C - 1)) * 8 + (n >> 5))
+
+
+def reorder(matrix, pieces):
+    both = jnp.dot(matrix, jnp.concatenate(pieces, axis=1), preferred_element_type=F32).astype(BF16)
+    return [both[:, k * W : (k + 1) * W] for k in range(len(pieces))]
+
+
+def prepare_kernel(flags, fwd_hbm, acts_hbm, grads_hbm, nat_b, nat_f, near, fwd, acts, grads, sems):
+    zh = flags[0]
+    load = Copies(sems)
+    load.add([(fwd_hbm, fwd), (acts_hbm, acts), (grads_hbm, grads)])
+    load.start()
+    order = to_inside()
+    load.wait()
+    streams = reorder(order, [acts[0], grads[1], acts[1], grads[0], fwd[1], fwd[0]])
+    for k, v in enumerate(streams):
+        ref, at_k = (nat_b, k) if k < 4 else (nat_f, k - 4)
+        ref[2 * at_k] = v[:R]
+        ref[2 * at_k + 1] = v[R:]
+    for k, src in ((0, 0), (2, 1), (6, 4)):
+        near[k] = streams[src][:R]
+        near[k + 1] = streams[src][R:]
+    for k, ref, src in ((4, nat_b, 4), (5, nat_b, 6), (8, nat_f, 2)):
+        near[k] = ref[src + zh]
+
+
+def prepare_ends_kernel(flags, batch, loss, first_own, last_own, ends):
+    x1, x2, d1, d2 = reorder(to_inside(), [batch[0], batch[1], loss[0], loss[1]])
+    for ref, pair in ((first_own, (x1, x2)), (last_own, (d1, d2))):
+        for k in range(2):
+            ref[k, 0] = pair[k][:R]
+            ref[k, 1] = pair[k][R:]
+    first = flags[5] == 1
+
+    @pl.when(first)
+    def _():
+        ends[...] = first_own[...]
+
+    @pl.when(jnp.logical_not(first))
+    def _():
+        ends[...] = last_own[...]
 
 
 def matrices(flat):
@@ -424,21 +462,34 @@
     def swap(value):
         return route(value, lambda s, yy, zz: (s, yy, 1 - zz))
 
-    def rim(value, high):
-        n = value.shape[0] // 2
-        return jnp.concatenate([value[:n].reshape(2 * n, R, W), jnp.where(high, value[n:, 1], value[n:, 0])])
-
-    nat_b = jnp.stack([inside(v[0, k : k + 1])[0] for k, v in ((0, back_out), (1, back_grad), (1, back_out), (0, back_grad))])
+    def as_flags(*values):
+        return jnp.stack([jnp.asarray(v).astype(jnp.int32) for v in values])
+
+    from_first, from_last = (14 % count, (count - 15) % count)
+    flags1 = as_flags(zh, y > 0, y < ny - 1, fz, bz, seg == from_first)
+    flags2 = as_flags(zh, (y > 0) | (zh == 1), (y < ny - 1) | (zh == 0), is_first, is_last)
+    nat_b, nat_f, near = call(
+        prepare_kernel,
+        [shaped(8), shaped(4), shaped(9)],
+        [pltpu.VMEM((2, 2 * R, W), BF16)] * 3 + [pltpu.SemaphoreType.DMA((3,))],
+        (flags1, flat_rows(fwd_in[0]), flat_rows(back_out[0]), flat_rows(back_grad[0])),
+        100_000_000,
+        [SMEM] + [HBM] * 3,
+        [VMEM] * 3,
+        58,
+    )
     swp_b = swap(nat_b)
-    nat_f = inside(fwd_in[0])[::-1]
     swp_f = swap(nat_f)
-    near = route(
-        jnp.concatenate([rim(nat_b, zh == 1), rim(nat_f, zh == 1)]), lambda s, yy, zz: (s, yy - 1 + 2 * zz, zz)
-    )
-
-    from_first, from_last = (14 % count, (count - 15) % count)
-    first_own, last_own = (inside(batch_next), inside(loss_grad[0]))
-    ends = jnp.where(seg == from_first, first_own, last_own)
+    near = route(near, lambda s, yy, zz: (s, yy - 1 + 2 * zz, zz))
+    first_own, last_own, ends = call(
+        prepare_ends_kernel,
+        [shaped(2, 2)] * 3,
+        [],
+        (flags1, flat_rows(batch_next), flat_rows(loss_grad[0])),
+        100_000_000,
+        [SMEM] + [VMEM] * 2,
+        [VMEM] * 3,
+    )
 
     def end_of(s):
         return 0 if s == from_first else count - 1 if s == from_last else -1
@@ -447,28 +498,22 @@
     sp2 = route(ends, lambda s, yy, zz: (end_of(s), yy + (1 if zz == 1 else -1), 1 - zz))
     mats = matrices(weights[0])
 
-    def as_flags(*values):
-        return jnp.stack([jnp.asarray(v).astype(jnp.int32) for v in values])
-
-    flags1 = as_flags(zh, y > 0, y < ny - 1, fz, bz)
-    flags2 = as_flags(zh, (y > 0) | (zh == 1), (y < ny - 1) | (zh == 0), is_first, is_last)
-    order, rows = order_rows(slabs)
+    sems = pltpu.SemaphoreType.DMA((20,))
 
     swp_b, near, sp1, sp2, mats = lax.optimization_barrier((swp_b, near, sp1, sp2, mats))
 
     def onward(value):
-        return route(rim(value, zh == 0), lambda s, yy, zz: (s, yy + 1 - 2 * zz, zz))
+        return route(value, lambda s, yy, zz: (s, yy + 1 - 2 * zz, zz))
 
     far_b = onward(swp_b)
-    sems = pltpu.SemaphoreType.DMA((20,))
-    bm, bd, h4, u4, e1p = call(
+    bm, bd, dw = call(
         tick1_back,
-        [shaped(16), shaped(4), shaped(4), shaped(4), shaped(2)],
+        [shaped(16), shaped(4), ((2, 9 * C, 3 * C), F32)],
         [planes(8), planes(6), planes(8), planes(6), planes(6), planes(4), planes(6), planes(4), planes(8), planes(6), sems],
         (flags1, mats, nat_b, swp_b, near, far_b),
         2_000_000_000,
         [SMEM, VMEM] + [HBM] * 4,
-        [HBM] * 5,
+        [HBM, HBM, VMEM],
     )
 
     def fwd_diag(s, yy, zz):
@@ -481,33 +526,30 @@
 
     bm2 = route(bm, lambda s, yy, zz: (s - 1, yy, back_side(s, zz)))
     bd2 = route(bd, back_diag)
-    (dw,) = call(
-        wgrad_kernel, [((2, 9 * C, 3 * C), F32)], [], (e1p, u4, nat_b[1], h4), 300_000_000, [VMEM] * 4, [VMEM]
-    )
-
     swp_f, bm = lax.optimization_barrier((swp_f, bm))
     far_f = onward(swp_f)
     fm, fd, ld, y1w = call(
         tick1_forward,
-        [shaped(8), shaped(2), shaped(2), shaped(6)],
+        [shaped(8), shaped(2), shaped(2), shaped(10)],
         [planes(8), planes(6), planes(6), planes(4), planes(8), planes(6), sems],
-        (flags1, mats, nat_f, swp_f, near, far_f),
+        (flags1, mats, nat_f, swp_f, near, far_f, last_own),
         1_000_000_000,
-        [SMEM, VMEM] + [HBM] * 4,
+        [SMEM, VMEM] + [HBM] * 5,
         [HBM] * 4,
     )
     ld2 = route(ld, lambda s, yy, zz: (s if s == count - 1 else -1, yy + 1 - 2 * zz, zz))
     fd2 = route(fd, fwd_diag)
     fm2 = route(fm, lambda s, yy, zz: (s + 1, yy, fwd_side(s, zz)))
 
+    bm2, bd2, fm2, fd2, ld2 = lax.optimization_barrier((bm2, bd2, fm2, fd2, ld2))
     out_b, parts = call(
         functools.partial(tick2_back, scale),
-        [shaped(8), ((slabs, rows, W), BF16)],
+        [((4, 2 * R, W), BF16), ((slabs, slab_rows(slabs), W), BF16)],
         [planes(6), planes(4), planes(6), planes(4), planes(4), planes(2), planes(4), planes(2), planes(6), planes(4), sems],
-        (flags2, mats, order, bm2, bd2, sp1, sp2, last_own, y1w, fm, ld2, dw),
+        (flags2, mats, bm2, bd2, sp1, sp2, y1w, fm, ld2, dw),
         1_500_000_000,
-        [SMEM, VMEM, VMEM] + [HBM] * 8 + [VMEM],
-        [HBM, VMEM],
+        [SMEM, VMEM] + [HBM] * 7 + [VMEM],
+        [VMEM, VMEM],
     )
     back = route(out_b, lambda s, yy, zz: (s - 1, yy, zz))
     parts = lax.all_to_all(parts, "slab", 0, 0, tiled=True)
@@ -515,7 +557,7 @@
     fm2, out_b = lax.optimization_barrier((fm2, out_b))
     (out_f,) = call(
         tick2_forward,
-        [shaped(4)],
+        [((2, 2 * R, W), BF16)],
         [planes(6), planes(4), planes(4), planes(2), planes(6), planes(4), sems],
         (flags2, mats, fm2, fd2, sp1, sp2, first_own),
         700_000_000,
@@ -526,11 +568,9 @@
     total = jnp.sum(wide(parts), axis=0)[: 2 * 9 * (C // slabs), : 3 * C]
     total = total.reshape(2, 9, C // slabs, 3, C).transpose(0, 4, 2, 1, 3).reshape(1, 2, C, -1)
 
-    fwd_out = outside(out_f.reshape(2, 2, R, W))
-    back = outside(back.reshape(4, 2, R, W))
-    acts = jnp.where(is_last, fwd_out, back[:2])
-    grads = jnp.where(is_last, loss_grad[1], back[2:])
-    return (fwd_out[None], acts[None], grads[None], total)
+    acts = jnp.where(is_last, out_f, back[:2])
+    grads = jnp.where(is_last, flat_rows(loss_grad[1]), back[2:])
+    return (*(v.reshape(fwd_in.shape) for v in (out_f, acts, grads)), total)
 
 
 def solution(mesh):

time: 133 us -> 128 us (0.962)
  the two profiles are of different devices: /device:TPU:62 before, /device:TPU:36 now
where the time goes in v2:
time: 128 us; the launch traced here: 127 us
  starting transfers between devices  61.5 us (48%)
  waiting for transfers between devices  29 us (23%)
  Pallas kernels  19.9 us (16%)
  local copies, waits for them, and re-layouts  13.9 us (11%)
  other arithmetic  1.9 us (1%)
    ppermute x13, starting transfers between devices, route(): return lax.ppermute(value, ('segment', 'slab'), pairs)  50.4 us
    pallas_call x7, Pallas kernels, call(): pl.pallas_call(kernel, out_shape=tuple((jax.ShapeDtypeStruct(s, t) for s,...  19.9 us
    ppermute x13, waiting for transfers between devices, route(): return lax.ppermute(value, ('segment', 'slab'), pairs)  19.5 us
    all_to_all x1, starting transfers between devices, local(): parts = lax.all_to_all(parts, 'slab', 0, 0, tiled=True)  11.1 us
    all_to_all x1, waiting for transfers between devices, local(): parts = lax.all_to_all(parts, 'slab', 0, 0, tiled=True)  9.48 us
    unnamed x31, local copies, waits for them, and re-layouts  7.68 us
  transfers between devices with their start and end apart: 14, of which 6 were waited for; matrix products, arithmetic and copies ran while one was open for 8% of the time, Pallas kernels for 10%

profile of v2, /device:TPU:36, one launch (start us, length us, event | category | flops | bytes accessed | tf_op | source)
XLA Modules:
  0.0 127.2 jit_solution(9084160055203638176)
XLA Ops:
  1.4 3.0 %shard_map.93 = (bf16[8,128,128]{2,1,0:T(8,128)(2,1)}, bf16[4,128,128]{2,1,0:T(8,128)(2,1)}, bf16[9,128,128]{2,1,0:T(8,128)(2,1)}) custom-call(s32[6]{0:T(128)} %stack.76.flags, bf16[2,256,128]{2,1,0:T(8,128)(2,1)} %bitcast.36, bf16[2,256,128]{2,1,0:T(8,128)(2,1)} %bitcast.37, bf16[2,256,128]{2,1,0:T(8,128)(2,1)} %bitcast.38), custom_call_target="tpu_custom_call" | custom-call | flops 100000000 | bytes 4000000 | tf_op jit(solution)/shard_map/pallas_call | solution.py:330
  4.3 14.8 %collective-permute-start = (bf16[8,128,128]{2,1,0:T(8,128)(2,1)}, bf16[8,128,128]{2,1,0:T(8,128)(2,1)S(1)}, u32[]{:S(2)}, u32[]{:S(2)}) collective-permute-start(bf16[8,128,128]{2,1,0:T(8,128)(2,1)} %get-tuple-element.31.nat), channel_id=1, source_target_pairs={{0,1},{1,0},{2,3},{3,2},{4,5},{5,4},{6,7},{7,6},{8,9},{9,8},{10,11... | collective-permute-start | bytes 786440 | tf_op jit(solution)/shard_map/ppermute | solution.py:450
  19.2 1.3 %collective-permute-start.1 = (bf16[9,128,128]{2,1,0:T(8,128)(2,1)}, bf16[9,128,128]{2,1,0:T(8,128)(2,1)S(1)}, u32[]{:S(2)}, u32[]{:S(2)}) collective-permute-start(bf16[9,128,128]{2,1,0:T(8,128)(2,1)} %get-tuple-element.32), channel_id=1, source_target_pairs={{1,3},{2,0},{3,5},{4,2},{5,7},{6,4},{9,11},{10,8},{11,13},{12,10},... | collective-permute-start | bytes 884744 | tf_op jit(solution)/shard_map/ppermute | solution.py:450
  20.5 1.7 %fusion = (bf16[1,2,32,2,4,128]{5,4,3,2,1,0:T(4,128)(2,1)}, bf16[1,2,32,2,4,128]{5,4,3,2,1,0:T(4,128)(2,1)S(1)}) fusion(bf16[2,2,32,2,4,128]{5,4,3,2,1,0:T(4,128)(2,1)} %param.10), kind=kLoop, calls=%fused_computation.5 | loop fusion | bytes 524288 | tf_op jit(solution)/shard_map/slice | solution.py:572
  27.9 2.2 %copy.17 = bf16[4,3,32,3,3,32]{5,4,3,2,1,0:T(4,128)(2,1)} copy(bf16[4,3,32,3,3,32]{2,0,1,4,3,5:T(4,128)(2,1)S(1)} %maximum_bitcast_fusion) | data formatting | bytes 442368
  30.1 2.0 %pad.4.clone = bf16[4,3,32,3,4,32]{5,4,3,2,1,0:T(4,128)(2,1)S(1)} pad(bf16[4,3,32,3,3,32]{5,4,3,2,1,0:T(4,128)(2,1)} %copy.17, bf16[]{:T(256)} %constant.56.clone.1), padding=0_0x0_0x0_0x0_0x0_1x0_0 | pad | bytes 516098 | tf_op jit(solution)/shard_map/jit(_pad)/pad | solution.py:425
  33.1 9.7 %collective-permute-done.swp = bf16[8,128,128]{2,1,0:T(8,128)(2,1)S(1)} collective-permute-done((bf16[8,128,128]{2,1,0:T(8,128)(2,1)}, bf16[8,128,128]{2,1,0:T(8,128)(2,1)S(1)}, u32[]{:S(2)}, u32[]{:S(2)}) %collective-permute-start) | collective-permute-done | bytes 262176 | tf_op jit(solution)/shard_map/ppermute | solution.py:450
  42.8 3.5 %collective-permute-start.4 = (bf16[8,128,128]{2,1,0:T(8,128)(2,1)S(1)}, bf16[8,128,128]{2,1,0:T(8,128)(2,1)S(1)}, u32[]{:S(2)}, u32[]{:S(2)}) collective-permute-start(bf16[8,128,128]{2,1,0:T(8,128)(2,1)S(1)} %collective-permute-done.swp), channel_id=1, source_target_pairs={{0,2},{2,4},{3,1},{4,6},{5,3},{7,5},{8,10},{10,12},{11,9},{12,14},... | collective-permute-start | bytes 786440 | tf_op jit(solution)/shard_map/ppermute | solution.py:450
  46.3 10.1 %collective-permute-start.7 = (bf16[4,128,128]{2,1,0:T(8,128)(2,1)S(1)}, bf16[4,128,128]{2,1,0:T(8,128)(2,1)S(1)}, u32[]{:S(2)}, u32[]{:S(2)}) collective-permute-start(bf16[4,128,128]{2,1,0:T(8,128)(2,1)S(1)} %copy-done.3), channel_id=1, source_target_pairs={{0,1},{1,0},{2,3},{3,2},{4,5},{5,4},{6,7},{7,6},{8,9},{9,8},{10,11... | collective-permute-start | bytes 393224 | tf_op jit(solution)/shard_map/ppermute | solution.py:450
  56.4 4.8 %shard_map.96 = (bf16[16,128,128]{2,1,0:T(8,128)(2,1)S(1)}, bf16[4,128,128]{2,1,0:T(8,128)(2,1)}, f32[2,288,96]{2,1,0:T(8,128)S(1)}) custom-call(s32[6]{0:T(128)S(1)} %copy-done, bf16[4,384,384]{2,1,0:T(8,128)(2,1)S(1)} %shard_map.95.w_ref, bf16[8,128,128]{2,1,0:T(8,128)(2,1)S(1)} %copy-done.1, bf16[8,128,128]{2,1,0:T(8,128)(2,1)S(1)} %collective-permute-done.swp, ...), custom_call_target="tpu_custom_call" | custom-call | flops 2000000000 | bytes 4000000 | tf_op jit(solution)/shard_map/pallas_call | solution.py:330
  61.9 1.9 %collective-permute-start.5 = (bf16[16,128,128]{2,1,0:T(8,128)(2,1)S(1)}, bf16[16,128,128]{2,1,0:T(8,128)(2,1)S(1)}, u32[]{:S(2)}, u32[]{:S(2)}) collective-permute-start(bf16[16,128,128]{2,1,0:T(8,128)(2,1)S(1)} %get-tuple-element.37), channel_id=1, source_target_pairs={{8,0},{9,1},{10,2},{11,3},{12,4},{13,5},{14,6},{15,7},{16,8},{17,9... | collective-permute-start | bytes 1572872 | tf_op jit(solution)/shard_map/ppermute | solution.py:450
  64.5 3.9 %collective-permute-start.8 = (bf16[4,128,128]{2,1,0:T(8,128)(2,1)S(1)}, bf16[4,128,128]{2,1,0:T(8,128)(2,1)S(1)}, u32[]{:S(2)}, u32[]{:S(2)}) collective-permute-start(bf16[4,128,128]{2,1,0:T(8,128)(2,1)S(1)} %collective-permute-done.7.swp), channel_id=1, source_target_pairs={{0,2},{2,4},{3,1},{4,6},{5,3},{7,5},{8,10},{10,12},{11,9},{12,14},... | collective-permute-start | bytes 393224 | tf_op jit(solution)/shard_map/ppermute | solution.py:450
  68.4 3.4 %collective-permute-done.8.far = bf16[4,128,128]{2,1,0:T(8,128)(2,1)S(1)} collective-permute-done((bf16[4,128,128]{2,1,0:T(8,128)(2,1)S(1)}, bf16[4,128,128]{2,1,0:T(8,128)(2,1)S(1)}, u32[]{:S(2)}, u32[]{:S(2)}) %collective-permute-start.8) | collective-permute-done | bytes 131104 | tf_op jit(solution)/shard_map/ppermute | solution.py:450
  71.8 3.4 %shard_map.97 = (bf16[8,128,128]{2,1,0:T(8,128)(2,1)S(1)}, bf16[2,128,128]{2,1,0:T(8,128)(2,1)}, bf16[2,128,128]{2,1,0:T(8,128)(2,1)S(1)}, bf16[10,128,128]{2,1,0:T(8,128)(2,1)S(1)}) custom-call(s32[6]{0:T(128)S(1)} %copy-done, bf16[4,384,384]{2,1,0:T(8,128)(2,1)S(1)} %shard_map.95.w_ref, bf16[4,128,128]{2,1,0:T(8,128)(2,1)S(1)} %copy-done.3, ...), custom_call_target="tpu_custom_call" | custom-call | flops 1000000000 | bytes 4000000 | tf_op jit(solution)/shard_map/pallas_call | solution.py:330
  76.0 1.9 %collective-permute-start.9 = (bf16[8,128,128]{2,1,0:T(8,128)(2,1)S(1)}, bf16[8,128,128]{2,1,0:T(8,128)(2,1)S(1)}, u32[]{:S(2)}, u32[]{:S(2)}) collective-permute-start(bf16[8,128,128]{2,1,0:T(8,128)(2,1)S(1)} %get-tuple-element.42.own), channel_id=1, source_target_pairs={{0,8},{1,9},{2,10},{3,11},{4,12},{5,13},{6,14},{7,15},{8,16},{9,17... | collective-permute-start | bytes 786440 | tf_op jit(solution)/shard_map/ppermute | solution.py:450
  77.9 5.6 %collective-permute-start.6 = (bf16[4,128,128]{2,1,0:T(8,128)(2,1)}, bf16[4,128,128]{2,1,0:T(8,128)(2,1)S(1)}, u32[]{:S(2)}, u32[]{:S(2)}) collective-permute-start(bf16[4,128,128]{2,1,0:T(8,128)(2,1)} %get-tuple-element.38), channel_id=1, source_target_pairs={{8,2},{10,4},{11,1},{12,6},{13,3},{15,5},{16,10},{18,12},{19,9},{2... | collective-permute-start | bytes 393224 | tf_op jit(solution)/shard_map/ppermute | solution.py:450
  83.5 3.5 %collective-permute-start.10 = (bf16[2,128,128]{2,1,0:T(8,128)(2,1)}, bf16[2,128,128]{2,1,0:T(8,128)(2,1)S(1)}, u32[]{:S(2)}, u32[]{:S(2)}) collective-permute-start(bf16[2,128,128]{2,1,0:T(8,128)(2,1)} %get-tuple-element.43), channel_id=1, source_target_pairs={{0,10},{2,12},{3,9},{4,14},{5,11},{7,13},{8,18},{10,20},{11,17},{1... | collective-permute-start | bytes 196616 | tf_op jit(solution)/shard_map/ppermute | solution.py:450
  87.7 2.4 %collective-permute-done.10.fd = bf16[2,128,128]{2,1,0:T(8,128)(2,1)S(1)} collective-permute-done((bf16[2,128,128]{2,1,0:T(8,128)(2,1)}, bf16[2,128,128]{2,1,0:T(8,128)(2,1)S(1)}, u32[]{:S(2)}, u32[]{:S(2)}) %collective-permute-start.10) | collective-permute-done | bytes 65568 | tf_op jit(solution)/shard_map/ppermute | solution.py:450
  92.1 4.6 %shard_map.98 = (bf16[4,256,128]{2,1,0:T(8,128)(2,1)S(1)}, bf16[8,80,128]{2,1,0:T(8,128)(2,1)}) custom-call(s32[5]{0:T(128)S(1)} %stack.67.flags, bf16[4,384,384]{2,1,0:T(8,128)(2,1)S(1)} %shard_map.95.w_ref, bf16[16,128,128]{2,1,0:T(8,128)(2,1)S(1)} %collective-permute-done.5.bm, bf16[4,128,128]{2,1,0:T(8,128)(2,1)S(1)} %collective-permute-done.6.bd, ...), custom_call_target="tpu_custom_call" | custom-call | flops 1500000000 | bytes 4000000 | tf_op jit(solution)/shard_map/pallas_call | solution.py:330
  96.7 11.1 %all-to-all-start = ((bf16[8,80,128]{2,1,0:T(8,128)(2,1)}), bf16[8,80,128]{2,1,0:T(8,128)(2,1)S(1)}, u32[]{:S(2)}, u32[]{:S(2)}) async-start(bf16[8,80,128]{2,1,0:T(8,128)(2,1)} %get-tuple-element.57), calls=%async_computation | async-start | bytes 327680 | tf_op jit(solution)/shard_map/all_to_all | solution.py:555
  107.8 1.9 %collective-permute-start.12 = (bf16[4,256,128]{2,1,0:T(8,128)(2,1)S(1)}, bf16[4,256,128]{2,1,0:T(8,128)(2,1)S(1)}, u32[]{:S(2)}, u32[]{:S(2)}) collective-permute-start(bf16[4,256,128]{2,1,0:T(8,128)(2,1)S(1)} %get-tuple-element.53), channel_id=1, source_target_pairs={{8,0},{9,1},{10,2},{11,3},{12,4},{13,5},{14,6},{15,7},{16,8},{17,9... | collective-permute-start | bytes 786440 | tf_op jit(solution)/shard_map/ppermute | solution.py:450
  109.7 3.1 %shard_map.99 = bf16[2,256,128]{2,1,0:T(8,128)(2,1)} custom-call(s32[5]{0:T(128)S(1)} %stack.67.flags, bf16[4,384,384]{2,1,0:T(8,128)(2,1)S(1)} %shard_map.95.w_ref, bf16[8,128,128]{2,1,0:T(8,128)(2,1)S(1)} %collective-permute-done.9.fm, bf16[2,128,128]{2,1,0:T(8,128)(2,1)S(1)} %collective-permute-done.10.fd, ...), custom_call_target="tpu_custom_call" | custom-call | flops 700000000 | bytes 4000000 | tf_op jit(solution)/shard_map/pallas_call | solution.py:330
  112.8 3.3 %collective-permute-done.12 = bf16[4,256,128]{2,1,0:T(8,128)(2,1)S(1)} collective-permute-done((bf16[4,256,128]{2,1,0:T(8,128)(2,1)S(1)}, bf16[4,256,128]{2,1,0:T(8,128)(2,1)S(1)}, u32[]{:S(2)}, u32[]{:S(2)}) %collective-permute-start.12) | collective-permute-done | bytes 262176 | tf_op jit(solution)/shard_map/ppermute | solution.py:450
  116.8 9.5 %all-to-all-done = bf16[8,80,128]{2,1,0:T(8,128)(2,1)S(1)} async-done(((bf16[8,80,128]{2,1,0:T(8,128)(2,1)}), bf16[8,80,128]{2,1,0:T(8,128)(2,1)S(1)}, u32[]{:S(2)}, u32[]{:S(2)}) %all-to-all-start) | async-done | bytes 163872 | tf_op jit(solution)/shard_map/all_to_all | solution.py:555
  (55 shorter events, 13.7 us)
Async XLA Ops:
  0.6 21.6 %copy-start.2 = (bf16[2,32,2,4,128]{4,3,2,1,0:T(4,128)(2,1)S(1)}, bf16[2,32,2,4,128]{4,3,2,1,0:T(4,128)(2,1)}, u32[]{:S(2)}) copy-start(bf16[2,32,2,4,128]{4,3,2,1,0:T(4,128)(2,1)} %param.9) | copy-start | bytes 393220
  0.6 24.3 %copy-start.13 = (bf16[1,2,32,864]{3,2,1,0:T(8,128)(2,1)S(1)}, bf16[1,2,32,864]{3,2,1,0:T(8,128)(2,1)}, u32[]{:S(2)}) copy-start(bf16[1,2,32,864]{3,2,1,0:T(8,128)(2,1)} %param.11) | copy-start | bytes 331780
  1.4 20.8 %copy-start = (s32[6]{0:T(128)S(1)}, s32[6]{0:T(128)}, u32[]{:S(2)}) copy-start(s32[6]{0:T(128)} %stack.76.flags) | copy-start | bytes 76
  4.3 38.4 %collective-permute-start = (bf16[8,128,128]{2,1,0:T(8,128)(2,1)}, bf16[8,128,128]{2,1,0:T(8,128)(2,1)S(1)}, u32[]{:S(2)}, u32[]{:S(2)}) collective-permute-start(bf16[8,128,128]{2,1,0:T(8,128)(2,1)} %get-tuple-element.31.nat), channel_id=1, source_target_pairs={{0,1},{1,0},{2,3},{3,2},{4,5},{5,4},{6,7},{7,6},{8,9},{9,8},{10,11... | collective-permute-start | bytes 786440 | tf_op jit(solution)/shard_map/ppermute | solution.py:450
  19.2 23.6 %collective-permute-start.1 = (bf16[9,128,128]{2,1,0:T(8,128)(2,1)}, bf16[9,128,128]{2,1,0:T(8,128)(2,1)S(1)}, u32[]{:S(2)}, u32[]{:S(2)}) collective-permute-start(bf16[9,128,128]{2,1,0:T(8,128)(2,1)} %get-tuple-element.32), channel_id=1, source_target_pairs={{1,3},{2,0},{3,5},{4,2},{5,7},{6,4},{9,11},{10,8},{11,13},{12,10},... | collective-permute-start | bytes 884744 | tf_op jit(solution)/shard_map/ppermute | solution.py:450
  23.6 4.2 %copy-start.6 = (bf16[2,2,128,128]{3,2,1,0:T(8,128)(2,1)}, bf16[2,2,128,128]{3,2,1,0:T(8,128)(2,1)S(1)}, u32[]{:S(2)}) copy-start(bf16[2,2,128,128]{3,2,1,0:T(8,128)(2,1)S(1)} %get-tuple-element.41.last_own) | copy-start | bytes 393220
  23.6 9.4 %collective-permute-start.3 = (bf16[2,2,128,128]{3,2,1,0:T(8,128)(2,1)S(1)}, bf16[2,2,128,128]{3,2,1,0:T(8,128)(2,1)S(1)}, u32[]{:S(2)}, u32[]{:S(2)}) collective-permute-start(bf16[2,2,128,128]{3,2,1,0:T(8,128)(2,1)S(1)} %get-tuple-element.33), channel_id=1, source_target_pairs={{113,2},{114,1},{115,4},{116,3},{117,6},{118,5},{393,506},{394,505... | collective-permute-start | bytes 393224 | tf_op jit(solution)/shard_map/ppermute | solution.py:450
  24.3 8.7 %collective-permute-start.2 = (bf16[2,2,128,128]{3,2,1,0:T(8,128)(2,1)S(1)}, bf16[2,2,128,128]{3,2,1,0:T(8,128)(2,1)S(1)}, u32[]{:S(2)}, u32[]{:S(2)}) collective-permute-start(bf16[2,2,128,128]{3,2,1,0:T(8,128)(2,1)S(1)} %get-tuple-element.33), channel_id=1, source_target_pairs={{112,1},{113,0},{114,3},{115,2},{116,5},{117,4},{118,7},{119,6},{3... | collective-permute-start | bytes 393224 | tf_op jit(solution)/shard_map/ppermute | solution.py:450
  32.1 14.2 %copy-start.3 = (bf16[4,128,128]{2,1,0:T(8,128)(2,1)S(1)}, bf16[4,128,128]{2,1,0:T(8,128)(2,1)}, u32[]{:S(2)}) copy-start(bf16[4,128,128]{2,1,0:T(8,128)(2,1)} %get-tuple-element.39.nat) | copy-start | bytes 393220
  32.1 24.4 %copy-start.1 = (bf16[8,128,128]{2,1,0:T(8,128)(2,1)S(1)}, bf16[8,128,128]{2,1,0:T(8,128)(2,1)}, u32[]{:S(2)}) copy-start(bf16[8,128,128]{2,1,0:T(8,128)(2,1)} %get-tuple-element.31.nat) | copy-start | bytes 786436
  42.8 13.7 %collective-permute-start.4 = (bf16[8,128,128]{2,1,0:T(8,128)(2,1)S(1)}, bf16[8,128,128]{2,1,0:T(8,128)(2,1)S(1)}, u32[]{:S(2)}, u32[]{:S(2)}) collective-permute-start(bf16[8,128,128]{2,1,0:T(8,128)(2,1)S(1)} %collective-permute-done.swp), channel_id=1, source_target_pairs={{0,2},{2,4},{3,1},{4,6},{5,3},{7,5},{8,10},{10,12},{11,9},{12,14},... | collective-permute-start | bytes 786440 | tf_op jit(solution)/shard_map/ppermute | solution.py:450
  46.3 25.5 %copy-start.7 = (bf16[2,2,128,128]{3,2,1,0:T(8,128)(2,1)S(1)}, bf16[2,2,128,128]{3,2,1,0:T(8,128)(2,1)}, u32[]{:S(2)}) copy-start(bf16[2,2,128,128]{3,2,1,0:T(8,128)(2,1)} %copy-done.6) | copy-start | bytes 393220
  46.3 18.3 %collective-permute-start.7 = (bf16[4,128,128]{2,1,0:T(8,128)(2,1)S(1)}, bf16[4,128,128]{2,1,0:T(8,128)(2,1)S(1)}, u32[]{:S(2)}, u32[]{:S(2)}) collective-permute-start(bf16[4,128,128]{2,1,0:T(8,128)(2,1)S(1)} %copy-done.3), channel_id=1, source_target_pairs={{0,1},{1,0},{2,3},{3,2},{4,5},{5,4},{6,7},{7,6},{8,9},{9,8},{10,11... | collective-permute-start | bytes 393224 | tf_op jit(solution)/shard_map/ppermute | solution.py:450
  61.9 28.2 %collective-permute-start.5 = (bf16[16,128,128]{2,1,0:T(8,128)(2,1)S(1)}, bf16[16,128,128]{2,1,0:T(8,128)(2,1)S(1)}, u32[]{:S(2)}, u32[]{:S(2)}) collective-permute-start(bf16[16,128,128]{2,1,0:T(8,128)(2,1)S(1)} %get-tuple-element.37), channel_id=1, source_target_pairs={{8,0},{9,1},{10,2},{11,3},{12,4},{13,5},{14,6},{15,7},{16,8},{17,9... | collective-permute-start | bytes 1572872 | tf_op jit(solution)/shard_map/ppermute | solution.py:450
  64.5 7.3 %collective-permute-start.8 = (bf16[4,128,128]{2,1,0:T(8,128)(2,1)S(1)}, bf16[4,128,128]{2,1,0:T(8,128)(2,1)S(1)}, u32[]{:S(2)}, u32[]{:S(2)}) collective-permute-start(bf16[4,128,128]{2,1,0:T(8,128)(2,1)S(1)} %collective-permute-done.7.swp), channel_id=1, source_target_pairs={{0,2},{2,4},{3,1},{4,6},{5,3},{7,5},{8,10},{10,12},{11,9},{12,14},... | collective-permute-start | bytes 393224 | tf_op jit(solution)/shard_map/ppermute | solution.py:450
  76.0 14.2 %collective-permute-start.9 = (bf16[8,128,128]{2,1,0:T(8,128)(2,1)S(1)}, bf16[8,128,128]{2,1,0:T(8,128)(2,1)S(1)}, u32[]{:S(2)}, u32[]{:S(2)}) collective-permute-start(bf16[8,128,128]{2,1,0:T(8,128)(2,1)S(1)} %get-tuple-element.42.own), channel_id=1, source_target_pairs={{0,8},{1,9},{2,10},{3,11},{4,12},{5,13},{6,14},{7,15},{8,16},{9,17... | collective-permute-start | bytes 786440 | tf_op jit(solution)/shard_map/ppermute | solution.py:450
  77.9 9.8 %collective-permute-start.6 = (bf16[4,128,128]{2,1,0:T(8,128)(2,1)}, bf16[4,128,128]{2,1,0:T(8,128)(2,1)S(1)}, u32[]{:S(2)}, u32[]{:S(2)}) collective-permute-start(bf16[4,128,128]{2,1,0:T(8,128)(2,1)} %get-tuple-element.38), channel_id=1, source_target_pairs={{8,2},{10,4},{11,1},{12,6},{13,3},{15,5},{16,10},{18,12},{19,9},{2... | collective-permute-start | bytes 393224 | tf_op jit(solution)/shard_map/ppermute | solution.py:450
  83.5 6.7 %collective-permute-start.10 = (bf16[2,128,128]{2,1,0:T(8,128)(2,1)}, bf16[2,128,128]{2,1,0:T(8,128)(2,1)S(1)}, u32[]{:S(2)}, u32[]{:S(2)}) collective-permute-start(bf16[2,128,128]{2,1,0:T(8,128)(2,1)} %get-tuple-element.43), channel_id=1, source_target_pairs={{0,10},{2,12},{3,9},{4,14},{5,11},{7,13},{8,18},{10,20},{11,17},{1... | collective-permute-start | bytes 196616 | tf_op jit(solution)/shard_map/ppermute | solution.py:450
  86.9 3.2 %collective-permute-start.11 = (bf16[2,128,128]{2,1,0:T(8,128)(2,1)S(1)}, bf16[2,128,128]{2,1,0:T(8,128)(2,1)S(1)}, u32[]{:S(2)}, u32[]{:S(2)}) collective-permute-start(bf16[2,128,128]{2,1,0:T(8,128)(2,1)S(1)} %get-tuple-element.44), channel_id=1, source_target_pairs={{504,506},{506,508},{507,505},{508,510},{509,507},{511,509}} | collective-permute-start | bytes 196616 | tf_op jit(solution)/shard_map/ppermute | solution.py:450
  90.1 1.0 copy-start.9
  92.1 17.6 %copy-start.5 = (bf16[2,2,128,128]{3,2,1,0:T(8,128)(2,1)S(1)}, bf16[2,2,128,128]{3,2,1,0:T(8,128)(2,1)}, u32[]{:S(2)}) copy-start(bf16[2,2,128,128]{3,2,1,0:T(8,128)(2,1)} %copy-done.4) | copy-start | bytes 393220
  96.7 29.6 %all-to-all-start = ((bf16[8,80,128]{2,1,0:T(8,128)(2,1)}), bf16[8,80,128]{2,1,0:T(8,128)(2,1)S(1)}, u32[]{:S(2)}, u32[]{:S(2)}) async-start(bf16[8,80,128]{2,1,0:T(8,128)(2,1)} %get-tuple-element.57), calls=%async_computation | async-start | bytes 327680 | tf_op jit(solution)/shard_map/all_to_all | solution.py:555
  107.8 8.3 %collective-permute-start.12 = (bf16[4,256,128]{2,1,0:T(8,128)(2,1)S(1)}, bf16[4,256,128]{2,1,0:T(8,128)(2,1)S(1)}, u32[]{:S(2)}, u32[]{:S(2)}) collective-permute-start(bf16[4,256,128]{2,1,0:T(8,128)(2,1)S(1)} %get-tuple-element.53), channel_id=1, source_target_pairs={{8,0},{9,1},{10,2},{11,3},{12,4},{13,5},{14,6},{15,7},{16,8},{17,9... | collective-permute-start | bytes 786440 | tf_op jit(solution)/shard_map/ppermute | solution.py:450
  109.7 6.4 %copy-start.12 = (bf16[1,2,32,2,4,128]{5,4,3,2,1,0:T(4,128)(2,1)S(1)}, bf16[1,2,32,2,4,128]{5,4,3,2,1,0:T(4,128)(2,1)}, u32[]{:S(2)}) copy-start(bf16[1,2,32,2,4,128]{5,4,3,2,1,0:T(4,128)(2,1)} %get-tuple-element.64) | copy-start | bytes 393220
  (4 other events, 3.0 us)

commit v3 on v2

--- a/solution.py
+++ b/solution.py
@@ -33,19 +33,17 @@
 
 def conv_planes(w_ref, field, start, count, use):
     lane = lax.broadcasted_iota(jnp.int32, (R, W), 1)
-    d = start
-    while d < start + count:
-        n = min(2, start + count - d)
+    for d in range(0, count, 2):
+        n = min(2, count - d)
         x = jnp.concatenate(
-            [jnp.concatenate([field[d + k + a] for a in range(3)], axis=0) for k in range(n)], axis=1
+            [jnp.concatenate([field[start + d + k + a] for a in range(3)], axis=0) for k in range(n)], axis=1
         )
         y = jnp.dot(w_ref[...], x, preferred_element_type=F32)
         for k in range(n):
             cols = slice(k * W, (k + 1) * W)
             left = jnp.where(lane >= 1, pltpu.roll(y[:R, cols], 1, 1), 0.0)
             right = jnp.where(lane < W - 1, pltpu.roll(y[2 * R :, cols], W - 1, 1), 0.0)
-            use(d + k, y[R : 2 * R, cols] + left + right)
-        d += n
+            use(start + d + k, y[R : 2 * R, cols] + left + right)
 
 
 def mask(d, v, inner, keep):
@@ -74,8 +72,8 @@
     conv_planes(w_ref.at[1], act_a, 0, inner - 2, two)
 
 
-def backward(n, keep, w_ref, bb, ba, db, da, rec_a, rec_b, grad_a, grad_b, act_b, act_a):
-    inner = n - 2
+def backward(keep, w_ref, bb, ba, db, da, rec_a, rec_b, grad_a, grad_b, act_b, act_a, first, count):
+    n, inner = (8, 6)
     for p in range(n):
         act_b[p] = silu(bb[p])
 
@@ -94,12 +92,12 @@
     def three(d, v):
         rec_b[d] = (wide(bb[d + 2]) - v).astype(BF16)
 
-    conv_planes(w_ref.at[0], act_a, 0, inner - 2, three)
+    conv_planes(w_ref.at[0], act_a, first, count, three)
 
     def four(d, v):
         grad_b[d] = (wide(db[d + 2]) + slope(rec_a[d + 1]) * v).astype(BF16)
 
-    conv_planes(w_ref.at[2], grad_a, 0, inner - 2, four)
+    conv_planes(w_ref.at[2], grad_a, first, count, four)
 
 
 class Copies:
@@ -166,42 +164,50 @@
     return (flags[1].astype(F32), flags[2].astype(F32))
 
 
-def tick1_back(flags, w_ref, nat, swp, near, far, bm, bd, dw, *scratch):
+def weight_sums(db, grad_a, act_b, act_a):
+    return (
+        wgrad_pair(at(grad_a, 1, 4), act_a),
+        wgrad_pair(at(db, 2, 4), at(act_b, 1, 6)),
+    )
+
+
+def tick1_back(flags, w_ref, nat, swp, near, far, bm, bl, bh, dw, *scratch):
     bb, ba, db, da, rec_a, rec_b, grad_a, grad_b, act_b, act_a, sems = scratch
-    zh, bz = (flags[0], flags[4])
+    zh = flags[0]
     load = Copies(sems)
     for k, (b, a) in enumerate(((bb, ba), (db, da))):
         load.add(
             window1(
                 zh, b, a, at(nat, 2 * k, 2), at(nat, 4 + 2 * k, 2), at(swp, 2 * k, 2), at(swp, 4 + 2 * k, 2),
-                at(near, 2 * k, 2), at(near, 4 + k, 1), at(far, 2 * k, 2), at(far, 5 + 2 * k - zh, 1),
+                at(near, 2 * k, 2), at(near, 4 + 2 * k + zh, 1), at(far, 2 * k, 2), at(far, 5 + 2 * k - zh, 1),
             )
         )
     load.run()
-    backward(8, keeps(flags), w_ref, bb, ba, db, da, rec_a, rec_b, grad_a, grad_b, act_b, act_a)
+    backward(keeps(flags), w_ref, bb, ba, db, da, rec_a, rec_b, grad_a, grad_b, act_b, act_a, 0, 4)
     save = Copies(sems)
     save.add([
         (rec_b, at(bm, 0, 4)),
         (grad_b, at(bm, 4, 4)),
-        (at(rec_a, 2 * bz, 4), at(bm, 8, 4)),
-        (at(grad_a, 2 * bz, 4), at(bm, 12, 4)),
-        (at(rec_b, 2 - 2 * bz, 2), at(bd, 0, 2)),
-        (at(grad_b, 2 - 2 * bz, 2), at(bd, 2, 2)),
+        (rec_a, at(bm, 8, 6)),
+        (grad_a, at(bm, 14, 6)),
+        (at(rec_b, 2, 2), at(bl, 0, 2)),
+        (at(grad_b, 2, 2), at(bl, 2, 2)),
+        (at(rec_b, 0, 2), at(bh, 0, 2)),
+        (at(grad_b, 0, 2), at(bh, 2, 2)),
     ])
     save.start()
-    dw[0] = wgrad_pair(at(grad_a, 1 + 2 * zh, 2), at(act_a, 2 * zh, 4))
-    dw[1] = wgrad_pair(at(db, 2 + 2 * zh, 2), at(act_b, 1 + 2 * zh, 4))
+    dw[0], dw[1] = weight_sums(db, grad_a, act_b, act_a)
     save.wait()
 
 
-def tick1_forward(flags, w_ref, nat, swp, near, far, last_own, fm, fd, ld, y1w, *scratch):
+def tick1_forward(flags, w_ref, nat, swp, near, far, last_own, fm, fd, ll, lh, y1w, *scratch):
     fb, fa, out_a, out_b, act_b, act_a, sems = scratch
     zh, fz = (flags[0], flags[3])
     load = Copies(sems)
     load.add(
         window1(
-            zh, fb, fa, at(nat, 0, 2), at(nat, 2, 2), at(swp, 0, 2), at(swp, 2, 2),
-            at(near, 6, 2), at(near, 8, 1), at(far, 0, 2), at(far, 3 - zh, 1),
+            zh, fb, fa, at(nat.at[0], 0, 2), at(nat.at[0], 2, 2), at(swp, 0, 2), at(swp, 2, 2),
+            at(near, 8, 2), at(near, 10 + zh, 1), at(far, 0, 2), at(far, 3 - zh, 1),
         )
     )
     load.run()
@@ -211,8 +217,10 @@
         (out_b, at(fm, 0, 4)),
         (at(out_a, 2 * fz, 4), at(fm, 4, 4)),
         (at(out_b, 2 - 2 * fz, 2), fd),
-        (at(out_a, 3 - zh, 1), at(ld, zh, 1)),
-        (at(out_b, 3 - 3 * zh, 1), at(ld, 1 - zh, 1)),
+        (at(out_a, 3, 1), at(ll, 0, 1)),
+        (at(out_b, 3, 1), at(ll, 1, 1)),
+        (at(out_a, 2, 1), at(lh, 0, 1)),
+        (at(out_b, 0, 1), at(lh, 1, 1)),
         (out_a, at(y1w, 0, 6)),
         (last_own.at[0], at(y1w, 6, 2)),
         (last_own.at[1], at(y1w, 8, 2)),
@@ -221,44 +229,48 @@
 
 
 def tick2_back(
-    scale, flags, w_ref, bm, bd, sp1, sp2, y1w, own, ld, dw, out, parts, *scratch
+    scale, flags, w_ref, bm, bl, bh, sp1, sp2, sp3, y1w, own, ll, lh, dw, out, parts, *scratch
 ):
     bb, ba, db, da, rec_a, rec_b, grad_a, grad_b, act_b, act_a, sems = scratch
-    zh, last = (flags[0], flags[4] == 1)
-    main, halo = (2 - 2 * zh, 4 * zh)
+    zh = flags[0]
     load = Copies(sems)
     load.add(
-        special(zh, db, da, (at(y1w, 6, 2), at(y1w, 8, 2)), sp1, sp2)
+        window1(
+            zh, db, da, at(y1w, 8, 2), at(y1w, 6, 2), sp1.at[1], sp1.at[0],
+            sp3.at[1], at(sp3.at[0], zh, 1), sp2.at[1], at(sp2.at[0], 1 - zh, 1),
+        )
         + [
-            (at(y1w, zh, 5), at(bb, 1 - zh, 5)),
-            (at(ld, zh, 1), at(bb, 5 * zh, 1)),
-            (at(own, zh, 3), at(ba, 1 - zh, 3)),
-            (at(ld, 1 - zh, 1), at(ba, 3 * zh, 1)),
+            (at(y1w, 0, 6), at(bb, 1, 6)),
+            (at(ll, 0, 1), at(bb, 0, 1)),
+            (at(lh, 0, 1), at(bb, 7, 1)),
+            (at(own, 0, 4), at(ba, 1, 4)),
+            (at(ll, 1, 1), at(ba, 0, 1)),
+            (at(lh, 1, 1), at(ba, 5, 1)),
         ],
-        last,
+        flags[6] == 1,
     )
     load.add(
         [
-            (at(bm, 0, 4), at(bb, main, 4)),
-            (at(bd, 0, 2), at(bb, halo, 2)),
-            (at(bm, 4, 4), at(db, main, 4)),
-            (at(bd, 2, 2), at(db, halo, 2)),
-            (at(bm, 8, 4), ba),
-            (at(bm, 12, 4), da),
+            (at(bl, 0, 2), at(bb, 0, 2)),
+            (at(bm, 0, 4), at(bb, 2, 4)),
+            (at(bh, 0, 2), at(bb, 6, 2)),
+            (at(bl, 2, 2), at(db, 0, 2)),
+            (at(bm, 4, 4), at(db, 2, 4)),
+            (at(bh, 2, 2), at(db, 6, 2)),
+            (at(bm, 8, 6), ba),
+            (at(bm, 14, 6), da),
         ],
-        flags[4] == 0,
+        flags[6] == 0,
     )
     load.start()
-    order, back_order = (slab_order(parts.shape[0]), to_outside())
+    order, back_order = (slab_order(2 * parts.shape[0], zh), to_outside())
     load.wait()
-    backward(6, keeps(flags), w_ref, bb, ba, db, da, rec_a, rec_b, grad_a, grad_b, act_b, act_a)
-    pieces = [rec_b[...], rec_a[1:3], grad_a[1:3], grad_b[...]]
+    backward(keeps(flags), w_ref, bb, ba, db, da, rec_a, rec_b, grad_a, grad_b, act_b, act_a, 2 * zh, 2)
+    own_a, own_b = (pl.ds(1 + 2 * zh, 2), pl.ds(2 * zh, 2))
+    pieces = [rec_b[own_b], rec_a[own_a], grad_a[own_a], grad_b[own_b]]
     for k, v in enumerate(reorder(back_order, [p.reshape(2 * R, W) for p in pieces])):
         out[k] = v
-    sums = [
-        dw[0] + wgrad_pair(at(grad_a, 1, 2), act_a),
-        dw[1] + wgrad_pair(at(db, 2, 2), at(act_b, 1, 4)),
-    ]
+    sums = [dw[k] + v for k, v in enumerate(weight_sums(db, grad_a, act_b, act_a))]
     sums = jnp.concatenate([(v * scale).astype(BF16) for v in sums], axis=0)
     ordered = jnp.dot(order, sums, preferred_element_type=F32).astype(BF16)
     parts[:, :, : 3 * C] = ordered.reshape(*parts.shape[:2], 3 * C)
@@ -285,7 +297,7 @@
     lane = lax.broadcasted_iota(jnp.int32, (C, W), 1)
     zero = jnp.zeros((C, W), BF16)
     left, right = ([], [])
-    for d in range(2):
+    for d in range(g_ref.shape[0]):
         for h in range(H):
             g = wide(g_ref[d, h * C : (h + 1) * C])
             down = jnp.where(lane < W - 1, pltpu.roll(g, W - 1, 1), 0.0)
@@ -342,12 +354,16 @@
     return -(-2 * 9 * C // (16 * slabs)) * 16
 
 
-def slab_order(slabs):
+def slab_order(slabs, zh):
     per = C // slabs
     low, rows = (per.bit_length() - 1, slab_rows(slabs))
-    return one_hot(
-        slabs * rows, 2 * 9 * C, lambda n: ((n & (C - 1)) >> low) * rows + (n >> 5) * per + (n & (per - 1))
-    )
+
+    def target(n):
+        slab = (n & (C - 1)) >> low
+        row = (slab >> 1) * rows + (n >> 5) * per + (n & (per - 1))
+        return jnp.where((slab & 1) == zh, row, -1)
+
+    return one_hot(slabs // 2 * rows, 2 * 9 * C, target)
 
 
 def planes(*lead):
@@ -381,8 +397,7 @@
     return [both[:, k * W : (k + 1) * W] for k in range(len(pieces))]
 
 
-def prepare_kernel(flags, fwd_hbm, acts_hbm, grads_hbm, nat_b, nat_f, near, fwd, acts, grads, sems):
-    zh = flags[0]
+def prepare_kernel(fwd_hbm, acts_hbm, grads_hbm, nat_b, nat_f, near, fwd, acts, grads, sems):
     load = Copies(sems)
     load.add([(fwd_hbm, fwd), (acts_hbm, acts), (grads_hbm, grads)])
     load.start()
@@ -390,14 +405,13 @@
     load.wait()
     streams = reorder(order, [acts[0], grads[1], acts[1], grads[0], fwd[1], fwd[0]])
     for k, v in enumerate(streams):
-        ref, at_k = (nat_b, k) if k < 4 else (nat_f, k - 4)
-        ref[2 * at_k] = v[:R]
-        ref[2 * at_k + 1] = v[R:]
-    for k, src in ((0, 0), (2, 1), (6, 4)):
-        near[k] = streams[src][:R]
-        near[k + 1] = streams[src][R:]
-    for k, ref, src in ((4, nat_b, 4), (5, nat_b, 6), (8, nat_f, 2)):
-        near[k] = ref[src + zh]
+        for half, plane in enumerate((v[:R], v[R:])):
+            near[2 * k + half] = plane
+            if k < 4:
+                nat_b[2 * k + half] = plane
+            else:
+                for copy in range(2):
+                    nat_f[copy, 2 * (k - 4) + half] = plane
 
 
 def prepare_ends_kernel(flags, batch, loss, first_own, last_own, ends):
@@ -456,7 +470,6 @@
         return 1 - zz if s % SNAKE == 0 and s > 0 else zz
 
     fz = jnp.where((seg % SNAKE == SNAKE - 1) & (seg < count - 1), 1 - zh, zh)
-    bz = jnp.where((seg % SNAKE == 0) & (seg > 0), 1 - zh, zh)
     is_first, is_last = (seg == 0, seg == count - 1)
 
     def swap(value):
@@ -466,20 +479,21 @@
         return jnp.stack([jnp.asarray(v).astype(jnp.int32) for v in values])
 
     from_first, from_last = (14 % count, (count - 15) % count)
-    flags1 = as_flags(zh, y > 0, y < ny - 1, fz, bz, seg == from_first)
+    flags1 = as_flags(zh, y > 0, y < ny - 1, fz, 0, seg == from_first, is_last)
     flags2 = as_flags(zh, (y > 0) | (zh == 1), (y < ny - 1) | (zh == 0), is_first, is_last)
     nat_b, nat_f, near = call(
         prepare_kernel,
-        [shaped(8), shaped(4), shaped(9)],
+        [shaped(8), shaped(2, 4), shaped(12)],
         [pltpu.VMEM((2, 2 * R, W), BF16)] * 3 + [pltpu.SemaphoreType.DMA((3,))],
-        (flags1, flat_rows(fwd_in[0]), flat_rows(back_out[0]), flat_rows(back_grad[0])),
+        (flat_rows(fwd_in[0]), flat_rows(back_out[0]), flat_rows(back_grad[0])),
         100_000_000,
-        [SMEM] + [HBM] * 3,
+        [HBM] * 3,
         [VMEM] * 3,
         58,
     )
     swp_b = swap(nat_b)
-    swp_f = swap(nat_f)
+    pairs = [[2 * k, 2 * k + 1] for k in range(ny)]
+    all_f = lax.all_to_all(nat_f, "slab", 0, 0, axis_index_groups=pairs, tiled=True)
     near = route(near, lambda s, yy, zz: (s, yy - 1 + 2 * zz, zz))
     first_own, last_own, ends = call(
         prepare_ends_kernel,
@@ -496,63 +510,66 @@
 
     sp1 = route(ends, lambda s, yy, zz: (end_of(s), yy, 1 - zz))
     sp2 = route(ends, lambda s, yy, zz: (end_of(s), yy + (1 if zz == 1 else -1), 1 - zz))
+    sp3 = route(last_own, lambda s, yy, zz: (count - 1 if s == count - 2 else -1, yy - 1 + 2 * zz, zz))
     mats = matrices(weights[0])
 
-    sems = pltpu.SemaphoreType.DMA((20,))
-
-    swp_b, near, sp1, sp2, mats = lax.optimization_barrier((swp_b, near, sp1, sp2, mats))
+    sems = pltpu.SemaphoreType.DMA((24,))
+
+    swp_b, near, sp1, sp2, sp3, mats = lax.optimization_barrier((swp_b, near, sp1, sp2, sp3, mats))
 
     def onward(value):
         return route(value, lambda s, yy, zz: (s, yy + 1 - 2 * zz, zz))
 
     far_b = onward(swp_b)
-    bm, bd, dw = call(
+    bm, bl, bh, dw = call(
         tick1_back,
-        [shaped(16), shaped(4), ((2, 9 * C, 3 * C), F32)],
+        [shaped(20), shaped(4), shaped(4), ((2, 9 * C, 3 * C), F32)],
         [planes(8), planes(6), planes(8), planes(6), planes(6), planes(4), planes(6), planes(4), planes(8), planes(6), sems],
         (flags1, mats, nat_b, swp_b, near, far_b),
         2_000_000_000,
         [SMEM, VMEM] + [HBM] * 4,
-        [HBM, HBM, VMEM],
+        [HBM, HBM, HBM, VMEM],
     )
 
     def fwd_diag(s, yy, zz):
         r = fwd_side(s, zz)
         return (s + 1, yy + 1 - 2 * r, r)
 
-    def back_diag(s, yy, zz):
-        r = back_side(s, zz)
-        return (s - 1, yy + 1 - 2 * r, r)
-
     bm2 = route(bm, lambda s, yy, zz: (s - 1, yy, back_side(s, zz)))
-    bd2 = route(bd, back_diag)
-    swp_f, bm = lax.optimization_barrier((swp_f, bm))
+    bl2 = route(bl, lambda s, yy, zz: (s - 1, yy + 1, back_side(s, zz)))
+    bh2 = route(bh, lambda s, yy, zz: (s - 1, yy - 1, back_side(s, zz)))
+
+    all_f, bm = lax.optimization_barrier((all_f, bm))
+    swp_f = jnp.where(zh == 0, all_f[1], all_f[0])
     far_f = onward(swp_f)
-    fm, fd, ld, y1w = call(
+    far_f, bl2, bh2 = lax.optimization_barrier((far_f, bl2, bh2))
+    fm, fd, ll, lh, y1w = call(
         tick1_forward,
-        [shaped(8), shaped(2), shaped(2), shaped(10)],
+        [shaped(8), shaped(2), shaped(2), shaped(2), shaped(10)],
         [planes(8), planes(6), planes(6), planes(4), planes(8), planes(6), sems],
         (flags1, mats, nat_f, swp_f, near, far_f, last_own),
         1_000_000_000,
         [SMEM, VMEM] + [HBM] * 5,
-        [HBM] * 4,
-    )
-    ld2 = route(ld, lambda s, yy, zz: (s if s == count - 1 else -1, yy + 1 - 2 * zz, zz))
+        [HBM] * 5,
+    )
+    ll2 = route(ll, lambda s, yy, zz: (s if s == count - 1 else -1, yy + 1, zz))
+    lh2 = route(lh, lambda s, yy, zz: (s if s == count - 1 else -1, yy - 1, zz))
     fd2 = route(fd, fwd_diag)
     fm2 = route(fm, lambda s, yy, zz: (s + 1, yy, fwd_side(s, zz)))
 
-    bm2, bd2, fm2, fd2, ld2 = lax.optimization_barrier((bm2, bd2, fm2, fd2, ld2))
+    bm2, bl2, bh2, fm2, fd2, ll2, lh2 = lax.optimization_barrier((bm2, bl2, bh2, fm2, fd2, ll2, lh2))
     out_b, parts = call(
         functools.partial(tick2_back, scale),
-        [((4, 2 * R, W), BF16), ((slabs, slab_rows(slabs), W), BF16)],
-        [planes(6), planes(4), planes(6), planes(4), planes(4), planes(2), planes(4), planes(2), planes(6), planes(4), sems],
-        (flags2, mats, bm2, bd2, sp1, sp2, y1w, fm, ld2, dw),
+        [((4, 2 * R, W), BF16), ((ny, slab_rows(slabs), W), BF16)],
+        [planes(8), planes(6), planes(8), planes(6), planes(6), planes(4), planes(6), planes(4), planes(8), planes(6), sems],
+        (flags1, mats, bm2, bl2, bh2, sp1, sp2, sp3, y1w, fm, ll2, lh2, dw),
         1_500_000_000,
-        [SMEM, VMEM] + [HBM] * 7 + [VMEM],
+        [SMEM, VMEM] + [HBM] * 10 + [VMEM],
         [VMEM, VMEM],
     )
     back = route(out_b, lambda s, yy, zz: (s - 1, yy, zz))
-    parts = lax.all_to_all(parts, "slab", 0, 0, tiled=True)
+    columns = [[2 * k + j for k in range(ny)] for j in range(2)]
+    parts = lax.all_to_all(parts, "slab", 0, 0, axis_index_groups=columns, tiled=True)
 
     fm2, out_b = lax.optimization_barrier((fm2, out_b))
     (out_f,) = call(

time: 128 us -> 126 us (0.984)
  the two profiles are of different devices: /device:TPU:36 before, /device:TPU:2 now
where the time goes in v3:
time: 126 us
  starting transfers between devices  70.6 us (56%)
  Pallas kernels  21.3 us (17%)
  waiting for transfers between devices  18.2 us (14%)
  local copies, waits for them, and re-layouts  11.6 us (9%)
  other arithmetic  2.87 us (2%)
    ppermute x15, starting transfers between devices, route(): return lax.ppermute(value, ('segment', 'slab'), pairs)  60.7 us
    pallas_call x7, Pallas kernels, call(): pl.pallas_call(kernel, out_shape=tuple((jax.ShapeDtypeStruct(s, t) for s,...  21.3 us
    ppermute x15, waiting for transfers between devices, route(): return lax.ppermute(value, ('segment', 'slab'), pairs)  15.6 us
    unnamed x29, local copies, waits for them, and re-layouts  6.62 us
    all_to_all x1, starting transfers between devices, local(): lax.all_to_all(parts, 'slab', 0, 0, axis_index_groups=columns, tiled=True)  5.78 us
    all_to_all x1, starting transfers between devices, local(): lax.all_to_all(nat_f, 'slab', 0, 0, axis_index_groups=pairs, tiled=True)  4.12 us
    all_to_all x1, waiting for transfers between devices, local(): lax.all_to_all(parts, 'slab', 0, 0, axis_index_groups=columns, tiled=True)  2.59 us
  transfers between devices with their start and end apart: 17, of which 6 were waited for; matrix products, arithmetic and copies ran while one was open for 9% of the time, Pallas kernels for 11%

profile of v3, /device:TPU:2, one launch (start us, length us, event | category | flops | bytes accessed | tf_op | source)
XLA Modules:
  0.0 125.7 jit_solution(13950237421113070240)
XLA Ops:
  0.7 2.3 %shard_map.93 = (bf16[8,128,128]{2,1,0:T(8,128)(2,1)}, bf16[2,4,128,128]{3,2,1,0:T(8,128)(2,1)}, bf16[12,128,128]{2,1,0:T(8,128)(2,1)}) custom-call(bf16[2,256,128]{2,1,0:T(8,128)(2,1)} %bitcast.37, bf16[2,256,128]{2,1,0:T(8,128)(2,1)} %bitcast.38, bf16[2,256,128]{2,1,0:T(8,128)(2,1)} %bitcast.39), custom_call_target="tpu_custom_call" | custom-call | flops 100000000 | bytes 4000000 | tf_op jit(solution)/shard_map/pallas_call | solution.py:342
  3.0 15.7 %collective-permute-start = (bf16[8,128,128]{2,1,0:T(8,128)(2,1)}, bf16[8,128,128]{2,1,0:T(8,128)(2,1)S(1)}, u32[]{:S(2)}, u32[]{:S(2)}) collective-permute-start(bf16[8,128,128]{2,1,0:T(8,128)(2,1)} %get-tuple-element.39.nat), channel_id=1, source_target_pairs={{0,1},{1,0},{2,3},{3,2},{4,5},{5,4},{6,7},{7,6},{8,9},{9,8},{10,11... | collective-permute-start | bytes 786440 | tf_op jit(solution)/shard_map/ppermute | solution.py:464
  18.7 1.3 %collective-permute-start.1 = (bf16[12,128,128]{2,1,0:T(8,128)(2,1)}, bf16[12,128,128]{2,1,0:T(8,128)(2,1)S(1)}, u32[]{:S(2)}, u32[]{:S(2)}) collective-permute-start(bf16[12,128,128]{2,1,0:T(8,128)(2,1)} %get-tuple-element.40), channel_id=1, source_target_pairs={{1,3},{2,0},{3,5},{4,2},{5,7},{6,4},{9,11},{10,8},{11,13},{12,10},... | collective-permute-start | bytes 1179656 | tf_op jit(solution)/shard_map/ppermute | solution.py:464
  24.0 4.1 %all-to-all-start = ((bf16[2,4,128,128]{3,2,1,0:T(8,128)(2,1)}), bf16[2,4,128,128]{3,2,1,0:T(8,128)(2,1)}, u32[]{:S(2)}, u32[]{:S(2)}) async-start(bf16[2,4,128,128]{3,2,1,0:T(8,128)(2,1)} %get-tuple-element.47.nat), calls=%async_computation | async-start | bytes 524288 | tf_op jit(solution)/shard_map/all_to_all | solution.py:496
  31.0 2.2 %copy.17 = bf16[4,3,32,3,3,32]{5,4,3,2,1,0:T(4,128)(2,1)} copy(bf16[4,3,32,3,3,32]{2,0,1,4,3,5:T(4,128)(2,1)S(1)} %maximum_bitcast_fusion) | data formatting | bytes 442368
  33.3 2.0 %pad.4.clone = bf16[4,3,32,3,4,32]{5,4,3,2,1,0:T(4,128)(2,1)S(1)} pad(bf16[4,3,32,3,3,32]{5,4,3,2,1,0:T(4,128)(2,1)} %copy.17, bf16[]{:T(256)} %constant.56.clone.1), padding=0_0x0_0x0_0x0_0x0_1x0_0 | pad | bytes 516098 | tf_op jit(solution)/shard_map/jit(_pad)/pad | solution.py:439
  36.3 4.6 %collective-permute-start.5 = (bf16[8,128,128]{2,1,0:T(8,128)(2,1)S(1)}, bf16[8,128,128]{2,1,0:T(8,128)(2,1)S(1)}, u32[]{:S(2)}, u32[]{:S(2)}) collective-permute-start(bf16[8,128,128]{2,1,0:T(8,128)(2,1)S(1)} %collective-permute-done.swp), channel_id=1, source_target_pairs={{0,2},{2,4},{3,1},{4,6},{5,3},{7,5},{8,10},{10,12},{11,9},{12,14},... | collective-permute-start | bytes 786440 | tf_op jit(solution)/shard_map/ppermute | solution.py:464
  40.8 5.0 %collective-permute-done.5.far = bf16[8,128,128]{2,1,0:T(8,128)(2,1)S(1)} collective-permute-done((bf16[8,128,128]{2,1,0:T(8,128)(2,1)S(1)}, bf16[8,128,128]{2,1,0:T(8,128)(2,1)S(1)}, u32[]{:S(2)}, u32[]{:S(2)}) %collective-permute-start.5) | collective-permute-done | bytes 262176 | tf_op jit(solution)/shard_map/ppermute | solution.py:464
  45.8 5.5 %shard_map.96 = (bf16[20,128,128]{2,1,0:T(8,128)(2,1)S(1)}, bf16[4,128,128]{2,1,0:T(8,128)(2,1)S(1)}, bf16[4,128,128]{2,1,0:T(8,128)(2,1)S(1)}, f32[2,288,96]{2,1,0:T(8,128)S(1)}) custom-call(s32[7]{0:T(128)S(1)} %stack.73.flags, bf16[4,384,384]{2,1,0:T(8,128)(2,1)S(1)} %shard_map.95.w_ref, bf16[8,128,128]{2,1,0:T(8,128)(2,1)S(1)} %copy-done, ...), custom_call_target="tpu_custom_call" | custom-call | flops 2000000000 | bytes 4000000 | tf_op jit(solution)/shard_map/pallas_call | solution.py:342
  53.4 8.3 %collective-permute-start.6 = (bf16[20,128,128]{2,1,0:T(8,128)(2,1)S(1)}, bf16[20,128,128]{2,1,0:T(8,128)(2,1)S(1)}, u32[]{:S(2)}, u32[]{:S(2)}) collective-permute-start(bf16[20,128,128]{2,1,0:T(8,128)(2,1)S(1)} %get-tuple-element.46), channel_id=1, source_target_pairs={{8,0},{9,1},{10,2},{11,3},{12,4},{13,5},{14,6},{15,7},{16,8},{17,9... | collective-permute-start | bytes 1966088 | tf_op jit(solution)/shard_map/ppermute | solution.py:464
  62.7 3.5 %collective-permute-start.7 = (bf16[4,128,128]{2,1,0:T(8,128)(2,1)S(1)}, bf16[4,128,128]{2,1,0:T(8,128)(2,1)S(1)}, u32[]{:S(2)}, u32[]{:S(2)}) collective-permute-start(bf16[4,128,128]{2,1,0:T(8,128)(2,1)S(1)} %select_bitcast_fusion.swp), channel_id=1, source_target_pairs={{0,2},{2,4},{3,1},{4,6},{5,3},{7,5},{8,10},{10,12},{11,9},{12,14},... | collective-permute-start | bytes 393224 | tf_op jit(solution)/shard_map/ppermute | solution.py:464
  66.2 9.1 %collective-permute-start.8 = (bf16[4,128,128]{2,1,0:T(8,128)(2,1)}, bf16[4,128,128]{2,1,0:T(8,128)(2,1)S(1)}, u32[]{:S(2)}, u32[]{:S(2)}) collective-permute-start(bf16[4,128,128]{2,1,0:T(8,128)(2,1)} %copy-done.7), channel_id=1, source_target_pairs={{8,2},{9,3},{10,4},{11,5},{12,6},{13,7},{16,10},{17,11},{18,12},{1... | collective-permute-start | bytes 393224 | tf_op jit(solution)/shard_map/ppermute | solution.py:464
  75.2 1.4 %collective-permute-start.9 = (bf16[4,128,128]{2,1,0:T(8,128)(2,1)}, bf16[4,128,128]{2,1,0:T(8,128)(2,1)S(1)}, u32[]{:S(2)}, u32[]{:S(2)}) collective-permute-start(bf16[4,128,128]{2,1,0:T(8,128)(2,1)} %copy-done.6), channel_id=1, source_target_pairs={{10,0},{11,1},{12,2},{13,3},{14,4},{15,5},{18,8},{19,9},{20,10},{2... | collective-permute-start | bytes 393224 | tf_op jit(solution)/shard_map/ppermute | solution.py:464
  76.7 1.4 %collective-permute-done.8.bl = bf16[4,128,128]{2,1,0:T(8,128)(2,1)S(1)} collective-permute-done((bf16[4,128,128]{2,1,0:T(8,128)(2,1)}, bf16[4,128,128]{2,1,0:T(8,128)(2,1)S(1)}, u32[]{:S(2)}, u32[]{:S(2)}) %collective-permute-start.8) | collective-permute-done | bytes 131104 | tf_op jit(solution)/shard_map/ppermute | solution.py:464
  78.0 5.2 %collective-permute-done.9.bh = bf16[4,128,128]{2,1,0:T(8,128)(2,1)S(1)} collective-permute-done((bf16[4,128,128]{2,1,0:T(8,128)(2,1)}, bf16[4,128,128]{2,1,0:T(8,128)(2,1)S(1)}, u32[]{:S(2)}, u32[]{:S(2)}) %collective-permute-start.9) | collective-permute-done | bytes 131104 | tf_op jit(solution)/shard_map/ppermute | solution.py:464
  84.2 4.1 %shard_map.97 = (bf16[8,128,128]{2,1,0:T(8,128)(2,1)S(1)}, bf16[2,128,128]{2,1,0:T(8,128)(2,1)S(1)}, bf16[2,128,128]{2,1,0:T(8,128)(2,1)S(1)}, bf16[2,128,128]{2,1,0:T(8,128)(2,1)S(1)}, bf16[10,128,128]{2,1,0:T(8,128)(2,1)S(1)}) custom-call(s32[7]{0:T(128)S(1)} %stack.73.flags, bf16[4,384,384]{2,1,0:T(8,128)(2,1)S(1)} %shard_map.95.w_ref, ...), custom_call_target="tpu_custom_call" | custom-call | flops 1000000000 | bytes 4000000 | tf_op jit(solution)/shard_map/pallas_call | solution.py:342
  88.3 1.9 %collective-permute-start.10 = (bf16[8,128,128]{2,1,0:T(8,128)(2,1)S(1)}, bf16[8,128,128]{2,1,0:T(8,128)(2,1)S(1)}, u32[]{:S(2)}, u32[]{:S(2)}) collective-permute-start(bf16[8,128,128]{2,1,0:T(8,128)(2,1)S(1)} %get-tuple-element.54.own), channel_id=1, source_target_pairs={{0,8},{1,9},{2,10},{3,11},{4,12},{5,13},{6,14},{7,15},{8,16},{9,17... | collective-permute-start | bytes 786440 | tf_op jit(solution)/shard_map/ppermute | solution.py:464
  90.2 2.5 %collective-permute-start.11 = (bf16[2,128,128]{2,1,0:T(8,128)(2,1)S(1)}, bf16[2,128,128]{2,1,0:T(8,128)(2,1)S(1)}, u32[]{:S(2)}, u32[]{:S(2)}) collective-permute-start(bf16[2,128,128]{2,1,0:T(8,128)(2,1)S(1)} %get-tuple-element.55), channel_id=1, source_target_pairs={{0,10},{2,12},{3,9},{4,14},{5,11},{7,13},{8,18},{10,20},{11,17},{1... | collective-permute-start | bytes 196616 | tf_op jit(solution)/shard_map/ppermute | solution.py:464
  94.6 3.5 %collective-permute-done.10.fm = bf16[8,128,128]{2,1,0:T(8,128)(2,1)S(1)} collective-permute-done((bf16[8,128,128]{2,1,0:T(8,128)(2,1)S(1)}, bf16[8,128,128]{2,1,0:T(8,128)(2,1)S(1)}, u32[]{:S(2)}, u32[]{:S(2)}) %collective-permute-start.10) | collective-permute-done | bytes 262176 | tf_op jit(solution)/shard_map/ppermute | solution.py:464
  98.1 5.3 %shard_map.98 = (bf16[4,256,128]{2,1,0:T(8,128)(2,1)S(1)}, bf16[4,80,128]{2,1,0:T(8,128)(2,1)}) custom-call(s32[7]{0:T(128)S(1)} %stack.73.flags, bf16[4,384,384]{2,1,0:T(8,128)(2,1)S(1)} %shard_map.95.w_ref, bf16[20,128,128]{2,1,0:T(8,128)(2,1)S(1)} %collective-permute-done.6.bm, bf16[4,128,128]{2,1,0:T(8,128)(2,1)S(1)} %collective-permute-done.8.bl, ...), custom_call_target="tpu_custom_call" | custom-call | flops 1500000000 | bytes 4000000 | tf_op jit(solution)/shard_map/pallas_call | solution.py:342
  103.3 9.0 %collective-permute-start.14 = (bf16[4,256,128]{2,1,0:T(8,128)(2,1)S(1)}, bf16[4,256,128]{2,1,0:T(8,128)(2,1)S(1)}, u32[]{:S(2)}, u32[]{:S(2)}) collective-permute-start(bf16[4,256,128]{2,1,0:T(8,128)(2,1)S(1)} %get-tuple-element.69), channel_id=1, source_target_pairs={{8,0},{9,1},{10,2},{11,3},{12,4},{13,5},{14,6},{15,7},{16,8},{17,9... | collective-permute-start | bytes 786440 | tf_op jit(solution)/shard_map/ppermute | solution.py:464
  112.5 5.8 %all-to-all-start.1 = ((bf16[4,80,128]{2,1,0:T(8,128)(2,1)}), bf16[4,80,128]{2,1,0:T(8,128)(2,1)S(1)}, u32[]{:S(2)}, u32[]{:S(2)}) async-start(bf16[4,80,128]{2,1,0:T(8,128)(2,1)} %get-tuple-element.73), calls=%async_computation.1 | async-start | bytes 163840 | tf_op jit(solution)/shard_map/all_to_all | solution.py:572
  118.3 3.1 %shard_map.99 = bf16[2,256,128]{2,1,0:T(8,128)(2,1)} custom-call(s32[5]{0:T(128)S(1)} %stack.65.flags, bf16[4,384,384]{2,1,0:T(8,128)(2,1)S(1)} %shard_map.95.w_ref, bf16[8,128,128]{2,1,0:T(8,128)(2,1)S(1)} %collective-permute-done.10.fm, bf16[2,128,128]{2,1,0:T(8,128)(2,1)S(1)} %collective-permute-done.11.fd, ...), custom_call_target="tpu_custom_call" | custom-call | flops 700000000 | bytes 4000000 | tf_op jit(solution)/shard_map/pallas_call | solution.py:342
  121.4 2.6 %all-to-all-done.1 = bf16[4,80,128]{2,1,0:T(8,128)(2,1)S(1)} async-done(((bf16[4,80,128]{2,1,0:T(8,128)(2,1)}), bf16[4,80,128]{2,1,0:T(8,128)(2,1)S(1)}, u32[]{:S(2)}, u32[]{:S(2)}) %all-to-all-start.1) | async-done | bytes 81952 | tf_op jit(solution)/shard_map/all_to_all | solution.py:572
  (60 shorter events, 15.3 us)
Async XLA Ops:
  0.6 20.6 %copy-start.1 = (bf16[2,32,2,4,128]{4,3,2,1,0:T(4,128)(2,1)S(1)}, bf16[2,32,2,4,128]{4,3,2,1,0:T(4,128)(2,1)}, u32[]{:S(2)}) copy-start(bf16[2,32,2,4,128]{4,3,2,1,0:T(4,128)(2,1)} %param.9) | copy-start | bytes 393220
  0.6 27.5 %copy-start.12 = (bf16[1,2,32,864]{3,2,1,0:T(8,128)(2,1)S(1)}, bf16[1,2,32,864]{3,2,1,0:T(8,128)(2,1)}, u32[]{:S(2)}) copy-start(bf16[1,2,32,864]{3,2,1,0:T(8,128)(2,1)} %param.11) | copy-start | bytes 331780
  3.0 33.3 %collective-permute-start = (bf16[8,128,128]{2,1,0:T(8,128)(2,1)}, bf16[8,128,128]{2,1,0:T(8,128)(2,1)S(1)}, u32[]{:S(2)}, u32[]{:S(2)}) collective-permute-start(bf16[8,128,128]{2,1,0:T(8,128)(2,1)} %get-tuple-element.39.nat), channel_id=1, source_target_pairs={{0,1},{1,0},{2,3},{3,2},{4,5},{5,4},{6,7},{7,6},{8,9},{9,8},{10,11... | collective-permute-start | bytes 786440 | tf_op jit(solution)/shard_map/ppermute | solution.py:464
  18.7 17.6 %collective-permute-start.1 = (bf16[12,128,128]{2,1,0:T(8,128)(2,1)}, bf16[12,128,128]{2,1,0:T(8,128)(2,1)S(1)}, u32[]{:S(2)}, u32[]{:S(2)}) collective-permute-start(bf16[12,128,128]{2,1,0:T(8,128)(2,1)} %get-tuple-element.40), channel_id=1, source_target_pairs={{1,3},{2,0},{3,5},{4,2},{5,7},{6,4},{9,11},{10,8},{11,13},{12,10},... | collective-permute-start | bytes 1179656 | tf_op jit(solution)/shard_map/ppermute | solution.py:464
  22.0 14.2 %collective-permute-start.2 = (bf16[2,2,128,128]{3,2,1,0:T(8,128)(2,1)S(1)}, bf16[2,2,128,128]{3,2,1,0:T(8,128)(2,1)S(1)}, u32[]{:S(2)}, u32[]{:S(2)}) collective-permute-start(bf16[2,2,128,128]{3,2,1,0:T(8,128)(2,1)S(1)} %get-tuple-element.41), channel_id=1, source_target_pairs={{112,1},{113,0},{114,3},{115,2},{116,5},{117,4},{118,7},{119,6},{3... | collective-permute-start | bytes 393224 | tf_op jit(solution)/shard_map/ppermute | solution.py:464
  22.7 13.5 %collective-permute-start.3 = (bf16[2,2,128,128]{3,2,1,0:T(8,128)(2,1)S(1)}, bf16[2,2,128,128]{3,2,1,0:T(8,128)(2,1)S(1)}, u32[]{:S(2)}, u32[]{:S(2)}) collective-permute-start(bf16[2,2,128,128]{3,2,1,0:T(8,128)(2,1)S(1)} %get-tuple-element.41), channel_id=1, source_target_pairs={{113,2},{114,1},{115,4},{116,3},{117,6},{118,5},{393,506},{394,505... | collective-permute-start | bytes 393224 | tf_op jit(solution)/shard_map/ppermute | solution.py:464
  23.4 12.9 %collective-permute-start.4 = (bf16[2,2,128,128]{3,2,1,0:T(8,128)(2,1)S(1)}, bf16[2,2,128,128]{3,2,1,0:T(8,128)(2,1)S(1)}, u32[]{:S(2)}, u32[]{:S(2)}) collective-permute-start(bf16[2,2,128,128]{3,2,1,0:T(8,128)(2,1)S(1)} %get-tuple-element.42.last_own), channel_id=1, source_target_pairs={{497,507},{498,504},{499,509},{500,506},{501,511},{502,508}} | collective-permute-start | bytes 393224 | tf_op jit(solution)/shard_map/ppermute | solution.py:464
  24.0 37.7 %all-to-all-start = ((bf16[2,4,128,128]{3,2,1,0:T(8,128)(2,1)}), bf16[2,4,128,128]{3,2,1,0:T(8,128)(2,1)}, u32[]{:S(2)}, u32[]{:S(2)}) async-start(bf16[2,4,128,128]{3,2,1,0:T(8,128)(2,1)} %get-tuple-element.47.nat), calls=%async_computation | async-start | bytes 524288 | tf_op jit(solution)/shard_map/all_to_all | solution.py:496
  35.2 10.6 %copy-start = (bf16[8,128,128]{2,1,0:T(8,128)(2,1)S(1)}, bf16[8,128,128]{2,1,0:T(8,128)(2,1)}, u32[]{:S(2)}) copy-start(bf16[8,128,128]{2,1,0:T(8,128)(2,1)} %get-tuple-element.39.nat) | copy-start | bytes 786436
  36.2 15.1 %copy-start.2 = (bf16[2,2,128,128]{3,2,1,0:T(8,128)(2,1)}, bf16[2,2,128,128]{3,2,1,0:T(8,128)(2,1)S(1)}, u32[]{:S(2)}) copy-start(bf16[2,2,128,128]{3,2,1,0:T(8,128)(2,1)S(1)} %collective-permute-done.4.sp3) | copy-start | bytes 393220
  36.3 9.5 %collective-permute-start.5 = (bf16[8,128,128]{2,1,0:T(8,128)(2,1)S(1)}, bf16[8,128,128]{2,1,0:T(8,128)(2,1)S(1)}, u32[]{:S(2)}, u32[]{:S(2)}) collective-permute-start(bf16[8,128,128]{2,1,0:T(8,128)(2,1)S(1)} %collective-permute-done.swp), channel_id=1, source_target_pairs={{0,2},{2,4},{3,1},{4,6},{5,3},{7,5},{8,10},{10,12},{11,9},{12,14},... | collective-permute-start | bytes 786440 | tf_op jit(solution)/shard_map/ppermute | solution.py:464
  53.4 44.7 %collective-permute-start.6 = (bf16[20,128,128]{2,1,0:T(8,128)(2,1)S(1)}, bf16[20,128,128]{2,1,0:T(8,128)(2,1)S(1)}, u32[]{:S(2)}, u32[]{:S(2)}) collective-permute-start(bf16[20,128,128]{2,1,0:T(8,128)(2,1)S(1)} %get-tuple-element.46), channel_id=1, source_target_pairs={{8,0},{9,1},{10,2},{11,3},{12,4},{13,5},{14,6},{15,7},{16,8},{17,9... | collective-permute-start | bytes 1966088 | tf_op jit(solution)/shard_map/ppermute | solution.py:464
  62.7 14.0 %collective-permute-start.7 = (bf16[4,128,128]{2,1,0:T(8,128)(2,1)S(1)}, bf16[4,128,128]{2,1,0:T(8,128)(2,1)S(1)}, u32[]{:S(2)}, u32[]{:S(2)}) collective-permute-start(bf16[4,128,128]{2,1,0:T(8,128)(2,1)S(1)} %select_bitcast_fusion.swp), channel_id=1, source_target_pairs={{0,2},{2,4},{3,1},{4,6},{5,3},{7,5},{8,10},{10,12},{11,9},{12,14},... | collective-permute-start | bytes 393224 | tf_op jit(solution)/shard_map/ppermute | solution.py:464
  66.2 11.9 %collective-permute-start.8 = (bf16[4,128,128]{2,1,0:T(8,128)(2,1)}, bf16[4,128,128]{2,1,0:T(8,128)(2,1)S(1)}, u32[]{:S(2)}, u32[]{:S(2)}) collective-permute-start(bf16[4,128,128]{2,1,0:T(8,128)(2,1)} %copy-done.7), channel_id=1, source_target_pairs={{8,2},{9,3},{10,4},{11,5},{12,6},{13,7},{16,10},{17,11},{18,12},{1... | collective-permute-start | bytes 393224 | tf_op jit(solution)/shard_map/ppermute | solution.py:464
  75.2 22.8 %copy-start.3 = (bf16[2,2,128,128]{3,2,1,0:T(8,128)(2,1)S(1)}, bf16[2,2,128,128]{3,2,1,0:T(8,128)(2,1)}, u32[]{:S(2)}) copy-start(bf16[2,2,128,128]{3,2,1,0:T(8,128)(2,1)} %copy-done.2) | copy-start | bytes 393220
  75.2 8.0 %collective-permute-start.9 = (bf16[4,128,128]{2,1,0:T(8,128)(2,1)}, bf16[4,128,128]{2,1,0:T(8,128)(2,1)S(1)}, u32[]{:S(2)}, u32[]{:S(2)}) collective-permute-start(bf16[4,128,128]{2,1,0:T(8,128)(2,1)} %copy-done.6), channel_id=1, source_target_pairs={{10,0},{11,1},{12,2},{13,3},{14,4},{15,5},{18,8},{19,9},{20,10},{2... | collective-permute-start | bytes 393224 | tf_op jit(solution)/shard_map/ppermute | solution.py:464
  84.2 13.9 %copy-start.11 = (f32[2,288,96]{2,1,0:T(8,128)S(1)}, f32[2,288,96]{2,1,0:T(8,128)}, u32[]{:S(2)}) copy-start(f32[2,288,96]{2,1,0:T(8,128)} %copy-done.10) | copy-start | bytes 663556
  88.3 9.8 %collective-permute-start.10 = (bf16[8,128,128]{2,1,0:T(8,128)(2,1)S(1)}, bf16[8,128,128]{2,1,0:T(8,128)(2,1)S(1)}, u32[]{:S(2)}, u32[]{:S(2)}) collective-permute-start(bf16[8,128,128]{2,1,0:T(8,128)(2,1)S(1)} %get-tuple-element.54.own), channel_id=1, source_target_pairs={{0,8},{1,9},{2,10},{3,11},{4,12},{5,13},{6,14},{7,15},{8,16},{9,17... | collective-permute-start | bytes 786440 | tf_op jit(solution)/shard_map/ppermute | solution.py:464
  90.2 4.4 %collective-permute-start.11 = (bf16[2,128,128]{2,1,0:T(8,128)(2,1)S(1)}, bf16[2,128,128]{2,1,0:T(8,128)(2,1)S(1)}, u32[]{:S(2)}, u32[]{:S(2)}) collective-permute-start(bf16[2,128,128]{2,1,0:T(8,128)(2,1)S(1)} %get-tuple-element.55), channel_id=1, source_target_pairs={{0,10},{2,12},{3,9},{4,14},{5,11},{7,13},{8,18},{10,20},{11,17},{1... | collective-permute-start | bytes 196616 | tf_op jit(solution)/shard_map/ppermute | solution.py:464
  92.7 1.9 %collective-permute-start.12 = (bf16[2,128,128]{2,1,0:T(8,128)(2,1)S(1)}, bf16[2,128,128]{2,1,0:T(8,128)(2,1)S(1)}, u32[]{:S(2)}, u32[]{:S(2)}) collective-permute-start(bf16[2,128,128]{2,1,0:T(8,128)(2,1)S(1)} %get-tuple-element.56), channel_id=1, source_target_pairs={{504,506},{505,507},{506,508},{507,509},{508,510},{509,511}} | collective-permute-start | bytes 196616 | tf_op jit(solution)/shard_map/ppermute | solution.py:464
  93.4 1.2 collective-permute-start.13
  98.1 20.2 %copy-start.9 = (bf16[2,2,128,128]{3,2,1,0:T(8,128)(2,1)S(1)}, bf16[2,2,128,128]{3,2,1,0:T(8,128)(2,1)}, u32[]{:S(2)}) copy-start(bf16[2,2,128,128]{3,2,1,0:T(8,128)(2,1)} %copy-done.8) | copy-start | bytes 393220
  103.3 21.6 %collective-permute-start.14 = (bf16[4,256,128]{2,1,0:T(8,128)(2,1)S(1)}, bf16[4,256,128]{2,1,0:T(8,128)(2,1)S(1)}, u32[]{:S(2)}, u32[]{:S(2)}) collective-permute-start(bf16[4,256,128]{2,1,0:T(8,128)(2,1)S(1)} %get-tuple-element.69), channel_id=1, source_target_pairs={{8,0},{9,1},{10,2},{11,3},{12,4},{13,5},{14,6},{15,7},{16,8},{17,9... | collective-permute-start | bytes 786440 | tf_op jit(solution)/shard_map/ppermute | solution.py:464
  112.5 11.5 %all-to-all-start.1 = ((bf16[4,80,128]{2,1,0:T(8,128)(2,1)}), bf16[4,80,128]{2,1,0:T(8,128)(2,1)S(1)}, u32[]{:S(2)}, u32[]{:S(2)}) async-start(bf16[4,80,128]{2,1,0:T(8,128)(2,1)} %get-tuple-element.73), calls=%async_computation.1 | async-start | bytes 163840 | tf_op jit(solution)/shard_map/all_to_all | solution.py:572
  (6 other events, 18.7 us)

commit v4 on v3

--- a/solution.py
+++ b/solution.py
@@ -100,36 +100,10 @@
     conv_planes(w_ref.at[2], grad_a, first, count, four)
 
 
-class Copies:
-    def __init__(self, sems):
-        self.sems, self.groups, self.n = (sems, [], 0)
-
-    def add(self, pairs, when=None):
-        pairs = list(pairs)
-        made = [pltpu.make_async_copy(src, dst, self.sems.at[self.n + k]) for k, (src, dst) in enumerate(pairs)]
-        self.n += len(made)
-        self.groups.append((when, made))
-
-    def each(self, what):
-        for when, made in self.groups:
-            def run(made=made):
-                for copy in made:
-                    getattr(copy, what)()
-
-            if when is None:
-                run()
-            else:
-                pl.when(when)(run)
-
-    def start(self):
-        self.each("start")
-
-    def wait(self):
-        self.each("wait")
-
-    def run(self):
-        self.start()
-        self.wait()
+def move(pairs):
+    for src, dst in pairs:
+        for k in range(dst.shape[0]):
+            dst[k] = src[k]
 
 
 def at(ref, first, count):
@@ -171,21 +145,21 @@
     )
 
 
+def tick1_window(zh, b, a, b_at, a_at, nat, swp, near, far):
+    move(
+        window1(
+            zh, b, a, at(nat, b_at, 2), at(nat, a_at, 2), at(swp, b_at, 2), at(swp, a_at, 2),
+            at(near, b_at, 2), at(near, a_at + zh, 1), at(far, b_at, 2), at(far, a_at + 1 - zh, 1),
+        )
+    )
+
+
 def tick1_back(flags, w_ref, nat, swp, near, far, bm, bl, bh, dw, *scratch):
-    bb, ba, db, da, rec_a, rec_b, grad_a, grad_b, act_b, act_a, sems = scratch
-    zh = flags[0]
-    load = Copies(sems)
+    bb, ba, db, da, rec_a, rec_b, grad_a, grad_b, act_b, act_a = scratch
     for k, (b, a) in enumerate(((bb, ba), (db, da))):
-        load.add(
-            window1(
-                zh, b, a, at(nat, 2 * k, 2), at(nat, 4 + 2 * k, 2), at(swp, 2 * k, 2), at(swp, 4 + 2 * k, 2),
-                at(near, 2 * k, 2), at(near, 4 + 2 * k + zh, 1), at(far, 2 * k, 2), at(far, 5 + 2 * k - zh, 1),
-            )
-        )
-    load.run()
+        tick1_window(flags[0], b, a, 2 * k, 4 + 2 * k, nat, swp, near, far)
     backward(keeps(flags), w_ref, bb, ba, db, da, rec_a, rec_b, grad_a, grad_b, act_b, act_a, 0, 4)
-    save = Copies(sems)
-    save.add([
+    move([
         (rec_b, at(bm, 0, 4)),
         (grad_b, at(bm, 4, 4)),
         (rec_a, at(bm, 8, 6)),
@@ -195,25 +169,15 @@
         (at(rec_b, 0, 2), at(bh, 0, 2)),
         (at(grad_b, 0, 2), at(bh, 2, 2)),
     ])
-    save.start()
     dw[0], dw[1] = weight_sums(db, grad_a, act_b, act_a)
-    save.wait()
 
 
 def tick1_forward(flags, w_ref, nat, swp, near, far, last_own, fm, fd, ll, lh, y1w, *scratch):
-    fb, fa, out_a, out_b, act_b, act_a, sems = scratch
-    zh, fz = (flags[0], flags[3])
-    load = Copies(sems)
-    load.add(
-        window1(
-            zh, fb, fa, at(nat.at[0], 0, 2), at(nat.at[0], 2, 2), at(swp, 0, 2), at(swp, 2, 2),
-            at(near, 8, 2), at(near, 10 + zh, 1), at(far, 0, 2), at(far, 3 - zh, 1),
-        )
-    )
-    load.run()
+    fb, fa, out_a, out_b, act_b, act_a = scratch
+    fz = flags[3]
+    tick1_window(flags[0], fb, fa, 8, 10, nat, swp, near, far)
     forward(8, keeps(flags), w_ref, fb, fa, out_a, out_b, act_b, act_a)
-    save = Copies(sems)
-    save.add([
+    move([
         (out_b, at(fm, 0, 4)),
         (at(out_a, 2 * fz, 4), at(fm, 4, 4)),
         (at(out_b, 2 - 2 * fz, 2), fd),
@@ -225,32 +189,32 @@
         (last_own.at[0], at(y1w, 6, 2)),
         (last_own.at[1], at(y1w, 8, 2)),
     ])
-    save.run()
 
 
 def tick2_back(
     scale, flags, w_ref, bm, bl, bh, sp1, sp2, sp3, y1w, own, ll, lh, dw, out, parts, *scratch
 ):
-    bb, ba, db, da, rec_a, rec_b, grad_a, grad_b, act_b, act_a, sems = scratch
+    bb, ba, db, da, rec_a, rec_b, grad_a, grad_b, act_b, act_a = scratch
     zh = flags[0]
-    load = Copies(sems)
-    load.add(
-        window1(
+
+    @pl.when(flags[6] == 1)
+    def _():
+        move(window1(
             zh, db, da, at(y1w, 8, 2), at(y1w, 6, 2), sp1.at[1], sp1.at[0],
             sp3.at[1], at(sp3.at[0], zh, 1), sp2.at[1], at(sp2.at[0], 1 - zh, 1),
-        )
-        + [
+        ))
+        move([
             (at(y1w, 0, 6), at(bb, 1, 6)),
             (at(ll, 0, 1), at(bb, 0, 1)),
             (at(lh, 0, 1), at(bb, 7, 1)),
             (at(own, 0, 4), at(ba, 1, 4)),
             (at(ll, 1, 1), at(ba, 0, 1)),
             (at(lh, 1, 1), at(ba, 5, 1)),
-        ],
-        flags[6] == 1,
-    )
-    load.add(
-        [
+        ])
+
+    @pl.when(flags[6] == 0)
+    def _():
+        move([
             (at(bl, 0, 2), at(bb, 0, 2)),
             (at(bm, 0, 4), at(bb, 2, 4)),
             (at(bh, 0, 2), at(bb, 6, 2)),
@@ -259,12 +223,9 @@
             (at(bh, 2, 2), at(db, 6, 2)),
             (at(bm, 8, 6), ba),
             (at(bm, 14, 6), da),
-        ],
-        flags[6] == 0,
-    )
-    load.start()
+        ])
+
     order, back_order = (slab_order(2 * parts.shape[0], zh), to_outside())
-    load.wait()
     backward(keeps(flags), w_ref, bb, ba, db, da, rec_a, rec_b, grad_a, grad_b, act_b, act_a, 2 * zh, 2)
     own_a, own_b = (pl.ds(1 + 2 * zh, 2), pl.ds(2 * zh, 2))
     pieces = [rec_b[own_b], rec_a[own_a], grad_a[own_a], grad_b[own_b]]
@@ -278,16 +239,17 @@
 
 
 def tick2_forward(flags, w_ref, fm, fd, sp1, sp2, first_own, out, *scratch):
-    fb, fa, out_a, out_b, act_b, act_a, sems = scratch
+    fb, fa, out_a, out_b, act_b, act_a = scratch
     zh, first = (flags[0], flags[3])
-    main, halo = (2 - 2 * zh, 4 * zh)
-    load = Copies(sems)
-    load.add(special(zh, fb, fa, (first_own.at[0], first_own.at[1]), sp1, sp2), first == 1)
-    load.add(
-        [(at(fm, 0, 4), at(fb, main, 4)), (fd, at(fb, halo, 2)), (at(fm, 4, 4), fa)],
-        first == 0,
-    )
-    load.run()
+
+    @pl.when(first == 1)
+    def _():
+        move(special(zh, fb, fa, (first_own.at[0], first_own.at[1]), sp1, sp2))
+
+    @pl.when(first == 0)
+    def _():
+        move([(at(fm, 0, 4), at(fb, 2 - 2 * zh, 4)), (fd, at(fb, 4 * zh, 2)), (at(fm, 4, 4), fa)])
+
     forward(6, keeps(flags), w_ref, fb, fa, out_a, out_b, act_b, act_a)
     for k, v in enumerate(reorder(to_outside(), [p.reshape(2 * R, W) for p in (out_a[1:3], out_b[...])])):
         out[k] = v
@@ -397,21 +359,18 @@
     return [both[:, k * W : (k + 1) * W] for k in range(len(pieces))]
 
 
-def prepare_kernel(fwd_hbm, acts_hbm, grads_hbm, nat_b, nat_f, near, fwd, acts, grads, sems):
-    load = Copies(sems)
-    load.add([(fwd_hbm, fwd), (acts_hbm, acts), (grads_hbm, grads)])
-    load.start()
+def prepare_kernel(fwd_hbm, acts_hbm, grads_hbm, nat, fwd, acts, grads, sems):
+    pairs = ((fwd_hbm, fwd), (acts_hbm, acts), (grads_hbm, grads))
+    copies = [pltpu.make_async_copy(src, dst, sems.at[k]) for k, (src, dst) in enumerate(pairs)]
+    for copy in copies:
+        copy.start()
     order = to_inside()
-    load.wait()
+    for copy in copies:
+        copy.wait()
     streams = reorder(order, [acts[0], grads[1], acts[1], grads[0], fwd[1], fwd[0]])
     for k, v in enumerate(streams):
-        for half, plane in enumerate((v[:R], v[R:])):
-            near[2 * k + half] = plane
-            if k < 4:
-                nat_b[2 * k + half] = plane
-            else:
-                for copy in range(2):
-                    nat_f[copy, 2 * (k - 4) + half] = plane
+        nat[2 * k] = v[:R]
+        nat[2 * k + 1] = v[R:]
 
 
 def prepare_ends_kernel(flags, batch, loss, first_own, last_own, ends):
@@ -481,20 +440,17 @@
     from_first, from_last = (14 % count, (count - 15) % count)
     flags1 = as_flags(zh, y > 0, y < ny - 1, fz, 0, seg == from_first, is_last)
     flags2 = as_flags(zh, (y > 0) | (zh == 1), (y < ny - 1) | (zh == 0), is_first, is_last)
-    nat_b, nat_f, near = call(
+    (nat,) = call(
         prepare_kernel,
-        [shaped(8), shaped(2, 4), shaped(12)],
+        [shaped(12)],
         [pltpu.VMEM((2, 2 * R, W), BF16)] * 3 + [pltpu.SemaphoreType.DMA((3,))],
         (flat_rows(fwd_in[0]), flat_rows(back_out[0]), flat_rows(back_grad[0])),
         100_000_000,
         [HBM] * 3,
-        [VMEM] * 3,
+        [VMEM],
         58,
     )
-    swp_b = swap(nat_b)
-    pairs = [[2 * k, 2 * k + 1] for k in range(ny)]
-    all_f = lax.all_to_all(nat_f, "slab", 0, 0, axis_index_groups=pairs, tiled=True)
-    near = route(near, lambda s, yy, zz: (s, yy - 1 + 2 * zz, zz))
+    swp = swap(nat)
     first_own, last_own, ends = call(
         prepare_ends_kernel,
         [shaped(2, 2)] * 3,
@@ -505,6 +461,9 @@
         [VMEM] * 3,
     )
 
+    own_planes, ends = lax.optimization_barrier((nat, ends))
+    near = route(own_planes, lambda s, yy, zz: (s, yy - 1 + 2 * zz, zz))
+
     def end_of(s):
         return 0 if s == from_first else count - 1 if s == from_last else -1
 
@@ -513,22 +472,18 @@
     sp3 = route(last_own, lambda s, yy, zz: (count - 1 if s == count - 2 else -1, yy - 1 + 2 * zz, zz))
     mats = matrices(weights[0])
 
-    sems = pltpu.SemaphoreType.DMA((24,))
-
-    swp_b, near, sp1, sp2, sp3, mats = lax.optimization_barrier((swp_b, near, sp1, sp2, sp3, mats))
-
-    def onward(value):
-        return route(value, lambda s, yy, zz: (s, yy + 1 - 2 * zz, zz))
-
-    far_b = onward(swp_b)
+
+    swp, near, sp1, sp2, sp3, mats = lax.optimization_barrier((swp, near, sp1, sp2, sp3, mats))
+
+    far = route(swp, lambda s, yy, zz: (s, yy + 1 - 2 * zz, zz))
     bm, bl, bh, dw = call(
         tick1_back,
         [shaped(20), shaped(4), shaped(4), ((2, 9 * C, 3 * C), F32)],
-        [planes(8), planes(6), planes(8), planes(6), planes(6), planes(4), planes(6), planes(4), planes(8), planes(6), sems],
-        (flags1, mats, nat_b, swp_b, near, far_b),
+        [planes(8), planes(6), planes(8), planes(6), planes(6), planes(4), planes(6), planes(4), planes(8), planes(6)],
+        (flags1, mats, nat, swp, near, far),
         2_000_000_000,
-        [SMEM, VMEM] + [HBM] * 4,
-        [HBM, HBM, HBM, VMEM],
+        [SMEM] + [VMEM] * 5,
+        [VMEM] * 4,
     )
 
     def fwd_diag(s, yy, zz):
@@ -539,18 +494,14 @@
     bl2 = route(bl, lambda s, yy, zz: (s - 1, yy + 1, back_side(s, zz)))
     bh2 = route(bh, lambda s, yy, zz: (s - 1, yy - 1, back_side(s, zz)))
 
-    all_f, bm = lax.optimization_barrier((all_f, bm))
-    swp_f = jnp.where(zh == 0, all_f[1], all_f[0])
-    far_f = onward(swp_f)
-    far_f, bl2, bh2 = lax.optimization_barrier((far_f, bl2, bh2))
     fm, fd, ll, lh, y1w = call(
         tick1_forward,
         [shaped(8), shaped(2), shaped(2), shaped(2), shaped(10)],
-        [planes(8), planes(6), planes(6), planes(4), planes(8), planes(6), sems],
-        (flags1, mats, nat_f, swp_f, near, far_f, last_own),
+        [planes(8), planes(6), planes(6), planes(4), planes(8), planes(6)],
+        (flags1, mats, nat, swp, near, far, last_own),
         1_000_000_000,
-        [SMEM, VMEM] + [HBM] * 5,
-        [HBM] * 5,
+        [SMEM] + [VMEM] * 6,
+        [VMEM] * 5,
     )
     ll2 = route(ll, lambda s, yy, zz: (s if s == count - 1 else -1, yy + 1, zz))
     lh2 = route(lh, lambda s, yy, zz: (s if s == count - 1 else -1, yy - 1, zz))
@@ -561,10 +512,10 @@
     out_b, parts = call(
         functools.partial(tick2_back, scale),
         [((4, 2 * R, W), BF16), ((ny, slab_rows(slabs), W), BF16)],
-        [planes(8), planes(6), planes(8), planes(6), planes(6), planes(4), planes(6), planes(4), planes(8), planes(6), sems],
+        [planes(8), planes(6), planes(8), planes(6), planes(6), planes(4), planes(6), planes(4), planes(8), planes(6)],
         (flags1, mats, bm2, bl2, bh2, sp1, sp2, sp3, y1w, fm, ll2, lh2, dw),
         1_500_000_000,
-        [SMEM, VMEM] + [HBM] * 10 + [VMEM],
+        [SMEM] + [VMEM] * 12,
         [VMEM, VMEM],
     )
     back = route(out_b, lambda s, yy, zz: (s - 1, yy, zz))
@@ -575,10 +526,10 @@
     (out_f,) = call(
         tick2_forward,
         [((2, 2 * R, W), BF16)],
-        [planes(6), planes(4), planes(4), planes(2), planes(6), planes(4), sems],
+        [planes(6), planes(4), planes(4), planes(2), planes(6), planes(4)],
         (flags2, mats, fm2, fd2, sp1, sp2, first_own),
         700_000_000,
-        [SMEM, VMEM] + [HBM] * 5,
+        [SMEM] + [VMEM] * 6,
         [VMEM],
     )
 

time: 126 us -> 120 us (0.952)
  the two profiles are of different devices: /device:TPU:2 before, /device:TPU:6 now
where the time goes in v4:
time: 120 us
  starting transfers between devices  76.4 us (64%)
  waiting for transfers between devices  14.3 us (12%)
  Pallas kernels  13.9 us (12%)
  local copies, waits for them, and re-layouts  11.5 us (10%)
  other arithmetic  2.81 us (2%)
    ppermute x14, starting transfers between devices, route(): return lax.ppermute(value, ('segment', 'slab'), pairs)  72.8 us
    pallas_call x7, Pallas kernels, call(): pl.pallas_call(kernel, out_shape=tuple((jax.ShapeDtypeStruct(s, t) for s,...  13.9 us
    ppermute x14, waiting for transfers between devices, route(): return lax.ppermute(value, ('segment', 'slab'), pairs)  11.1 us
    unnamed x11, local copies, waits for them, and re-layouts  5.83 us
    all_to_all x1, starting transfers between devices, local(): lax.all_to_all(parts, 'slab', 0, 0, axis_index_groups=columns, tiled=True)  3.59 us
    all_to_all x1, waiting for transfers between devices, local(): lax.all_to_all(parts, 'slab', 0, 0, axis_index_groups=columns, tiled=True)  3.23 us
  transfers between devices with their start and end apart: 15, of which 5 were waited for; matrix products, arithmetic and copies ran while one was open for 9% of the time, Pallas kernels for 4%

profile of v4, /device:TPU:6, one launch (start us, length us, event | category | flops | bytes accessed | tf_op | source)
XLA Modules:
  0.0 119.8 jit_solution(8690585913365154999)
XLA Ops:
  0.7 1.7 %fusion = (bf16[1,2,32,2,4,128]{5,4,3,2,1,0:T(4,128)(2,1)}, bf16[1,2,32,2,4,128]{5,4,3,2,1,0:T(4,128)(2,1)S(1)}) fusion(bf16[2,2,32,2,4,128]{5,4,3,2,1,0:T(4,128)(2,1)} %param.10), kind=kLoop, calls=%fused_computation.5 | loop fusion | bytes 524288 | tf_op jit(solution)/shard_map/slice | solution.py:540
  2.5 0.9 copy-done.1
  4.2 2.1 %shard_map.93.nat = bf16[12,128,128]{2,1,0:T(8,128)(2,1)} custom-call(bf16[2,256,128]{2,1,0:T(8,128)(2,1)} %bitcast.32, bf16[2,256,128]{2,1,0:T(8,128)(2,1)} %bitcast.33, bf16[2,256,128]{2,1,0:T(8,128)(2,1)} %bitcast.34), custom_call_target="tpu_custom_call" | custom-call | flops 100000000 | bytes 4000000 | tf_op jit(solution)/shard_map/pallas_call | solution.py:304
  6.3 1.3 %collective-permute-start.1 = (bf16[12,128,128]{2,1,0:T(8,128)(2,1)}, bf16[12,128,128]{2,1,0:T(8,128)(2,1)S(1)}, u32[]{:S(2)}, u32[]{:S(2)}) collective-permute-start(bf16[12,128,128]{2,1,0:T(8,128)(2,1)} %shard_map.93.nat), channel_id=1, source_target_pairs={{1,3},{2,0},{3,5},{4,2},{5,7},{6,4},{9,11},{10,8},{11,13},{12,10},... | collective-permute-start | bytes 1179656 | tf_op jit(solution)/shard_map/ppermute | solution.py:423
  7.6 17.9 %collective-permute-start = (bf16[12,128,128]{2,1,0:T(8,128)(2,1)}, bf16[12,128,128]{2,1,0:T(8,128)(2,1)S(1)}, u32[]{:S(2)}, u32[]{:S(2)}) collective-permute-start(bf16[12,128,128]{2,1,0:T(8,128)(2,1)} %shard_map.93.nat), channel_id=1, source_target_pairs={{0,1},{1,0},{2,3},{3,2},{4,5},{5,4},{6,7},{7,6},{8,9},{9,8},{10,11... | collective-permute-start | bytes 1179656 | tf_op jit(solution)/shard_map/ppermute | solution.py:423
  29.3 2.1 %maximum_bitcast_fusion = bf16[4,3,32,3,3,32]{2,0,1,4,3,5:T(4,128)(2,1)} fusion(bf16[2,32,32,3,3,3]{1,0,5,4,3,2:T(2,128)(2,1)S(1)} %reverse_bitcast_fusion, bf16[2,32,32,3,3,3]{1,0,5,4,3,2:T(2,128)(2,1)S(1)} %bitcast.28), kind=kLoop, calls=%fused_computation | loop fusion | flops 442368 | bytes 442368 | tf_op jit(solution)/shard_map/transpose | solution.py:397
  31.3 3.5 %copy.17 = bf16[4,3,32,3,3,32]{5,4,3,2,1,0:T(4,128)(2,1)} copy(bf16[4,3,32,3,3,32]{2,0,1,4,3,5:T(4,128)(2,1)} %maximum_bitcast_fusion) | data formatting | bytes 442368
  34.8 2.0 %pad.4.clone = bf16[4,3,32,3,4,32]{5,4,3,2,1,0:T(4,128)(2,1)S(1)} pad(bf16[4,3,32,3,3,32]{5,4,3,2,1,0:T(4,128)(2,1)} %copy.17, bf16[]{:T(256)} %constant.56.clone.1), padding=0_0x0_0x0_0x0_0x0_1x0_0 | pad | bytes 516098 | tf_op jit(solution)/shard_map/jit(_pad)/pad | solution.py:398
  37.8 1.3 %collective-permute-done.swp = bf16[12,128,128]{2,1,0:T(8,128)(2,1)S(1)} collective-permute-done((bf16[12,128,128]{2,1,0:T(8,128)(2,1)}, bf16[12,128,128]{2,1,0:T(8,128)(2,1)S(1)}, u32[]{:S(2)}, u32[]{:S(2)}) %collective-permute-start) | collective-permute-done | bytes 393248 | tf_op jit(solution)/shard_map/ppermute | solution.py:423
  39.1 3.5 %collective-permute-start.5 = (bf16[12,128,128]{2,1,0:T(8,128)(2,1)S(1)}, bf16[12,128,128]{2,1,0:T(8,128)(2,1)S(1)}, u32[]{:S(2)}, u32[]{:S(2)}) collective-permute-start(bf16[12,128,128]{2,1,0:T(8,128)(2,1)S(1)} %collective-permute-done.swp), channel_id=1, source_target_pairs={{0,2},{2,4},{3,1},{4,6},{5,3},{7,5},{8,10},{10,12},{11,9},{12,14},... | collective-permute-start | bytes 1179656 | tf_op jit(solution)/shard_map/ppermute | solution.py:423
  42.6 5.3 %collective-permute-done.5.far = bf16[12,128,128]{2,1,0:T(8,128)(2,1)S(1)} collective-permute-done((bf16[12,128,128]{2,1,0:T(8,128)(2,1)S(1)}, bf16[12,128,128]{2,1,0:T(8,128)(2,1)S(1)}, u32[]{:S(2)}, u32[]{:S(2)}) %collective-permute-start.5) | collective-permute-done | bytes 393248 | tf_op jit(solution)/shard_map/ppermute | solution.py:423
  47.9 2.7 %shard_map.96 = (bf16[20,128,128]{2,1,0:T(8,128)(2,1)S(1)}, bf16[4,128,128]{2,1,0:T(8,128)(2,1)S(1)}, bf16[4,128,128]{2,1,0:T(8,128)(2,1)S(1)}, f32[2,288,96]{2,1,0:T(8,128)S(1)}) custom-call(s32[7]{0:T(128)S(1)} %stack.73.flags, bf16[4,384,384]{2,1,0:T(8,128)(2,1)S(1)} %shard_map.95.w_ref, bf16[12,128,128]{2,1,0:T(8,128)(2,1)S(1)} %copy-done, ...), custom_call_target="tpu_custom_call" | custom-call | flops 2000000000 | bytes 4000000 | tf_op jit(solution)/shard_map/pallas_call | solution.py:304
  50.6 15.6 %collective-permute-start.6 = (bf16[20,128,128]{2,1,0:T(8,128)(2,1)S(1)}, bf16[20,128,128]{2,1,0:T(8,128)(2,1)S(1)}, u32[]{:S(2)}, u32[]{:S(2)}) collective-permute-start(bf16[20,128,128]{2,1,0:T(8,128)(2,1)S(1)} %get-tuple-element.41), channel_id=1, source_target_pairs={{8,0},{9,1},{10,2},{11,3},{12,4},{13,5},{14,6},{15,7},{16,8},{17,9... | collective-permute-start | bytes 1966088 | tf_op jit(solution)/shard_map/ppermute | solution.py:423
  66.2 1.8 %shard_map.97 = (bf16[8,128,128]{2,1,0:T(8,128)(2,1)S(1)}, bf16[2,128,128]{2,1,0:T(8,128)(2,1)S(1)}, bf16[2,128,128]{2,1,0:T(8,128)(2,1)S(1)}, bf16[2,128,128]{2,1,0:T(8,128)(2,1)S(1)}, bf16[10,128,128]{2,1,0:T(8,128)(2,1)S(1)}) custom-call(s32[7]{0:T(128)S(1)} %stack.73.flags, bf16[4,384,384]{2,1,0:T(8,128)(2,1)S(1)} %shard_map.95.w_ref, ...), custom_call_target="tpu_custom_call" | custom-call | flops 1000000000 | bytes 4000000 | tf_op jit(solution)/shard_map/pallas_call | solution.py:304
  68.0 10.7 %collective-permute-start.9 = (bf16[8,128,128]{2,1,0:T(8,128)(2,1)S(1)}, bf16[8,128,128]{2,1,0:T(8,128)(2,1)S(1)}, u32[]{:S(2)}, u32[]{:S(2)}) collective-permute-start(bf16[8,128,128]{2,1,0:T(8,128)(2,1)S(1)} %get-tuple-element.44.own), channel_id=1, source_target_pairs={{0,8},{1,9},{2,10},{3,11},{4,12},{5,13},{6,14},{7,15},{8,16},{9,17... | collective-permute-start | bytes 786440 | tf_op jit(solution)/shard_map/ppermute | solution.py:423
  78.7 5.8 %collective-permute-start.10 = (bf16[2,128,128]{2,1,0:T(8,128)(2,1)S(1)}, bf16[2,128,128]{2,1,0:T(8,128)(2,1)S(1)}, u32[]{:S(2)}, u32[]{:S(2)}) collective-permute-start(bf16[2,128,128]{2,1,0:T(8,128)(2,1)S(1)} %get-tuple-element.45), channel_id=1, source_target_pairs={{0,10},{2,12},{3,9},{4,14},{5,11},{7,13},{8,18},{10,20},{11,17},{1... | collective-permute-start | bytes 196616 | tf_op jit(solution)/shard_map/ppermute | solution.py:423
  85.2 5.7 %collective-permute-start.7 = (bf16[4,128,128]{2,1,0:T(8,128)(2,1)S(1)}, bf16[4,128,128]{2,1,0:T(8,128)(2,1)S(1)}, u32[]{:S(2)}, u32[]{:S(2)}) collective-permute-start(bf16[4,128,128]{2,1,0:T(8,128)(2,1)S(1)} %get-tuple-element.42), channel_id=1, source_target_pairs={{8,2},{9,3},{10,4},{11,5},{12,6},{13,7},{16,10},{17,11},{18,12},{1... | collective-permute-start | bytes 393224 | tf_op jit(solution)/shard_map/ppermute | solution.py:423
  90.9 1.3 %collective-permute-start.8 = (bf16[4,128,128]{2,1,0:T(8,128)(2,1)S(1)}, bf16[4,128,128]{2,1,0:T(8,128)(2,1)S(1)}, u32[]{:S(2)}, u32[]{:S(2)}) collective-permute-start(bf16[4,128,128]{2,1,0:T(8,128)(2,1)S(1)} %get-tuple-element.43), channel_id=1, source_target_pairs={{10,0},{11,1},{12,2},{13,3},{14,4},{15,5},{18,8},{19,9},{20,10},{2... | collective-permute-start | bytes 393224 | tf_op jit(solution)/shard_map/ppermute | solution.py:423
  93.4 4.0 %collective-permute-done.8.bh = bf16[4,128,128]{2,1,0:T(8,128)(2,1)S(1)} collective-permute-done((bf16[4,128,128]{2,1,0:T(8,128)(2,1)S(1)}, bf16[4,128,128]{2,1,0:T(8,128)(2,1)S(1)}, u32[]{:S(2)}, u32[]{:S(2)}) %collective-permute-start.8) | collective-permute-done | bytes 131104 | tf_op jit(solution)/shard_map/ppermute | solution.py:423
  97.4 3.8 %shard_map.98 = (bf16[4,256,128]{2,1,0:T(8,128)(2,1)S(1)}, bf16[4,80,128]{2,1,0:T(8,128)(2,1)}) custom-call(s32[7]{0:T(128)S(1)} %stack.73.flags, bf16[4,384,384]{2,1,0:T(8,128)(2,1)S(1)} %shard_map.95.w_ref, bf16[20,128,128]{2,1,0:T(8,128)(2,1)S(1)} %collective-permute-done.6.bm, bf16[4,128,128]{2,1,0:T(8,128)(2,1)S(1)} %collective-permute-done.7.bl, ...), custom_call_target="tpu_custom_call" | custom-call | flops 1500000000 | bytes 4000000 | tf_op jit(solution)/shard_map/pallas_call | solution.py:304
  101.2 7.6 %collective-permute-start.13 = (bf16[4,256,128]{2,1,0:T(8,128)(2,1)S(1)}, bf16[4,256,128]{2,1,0:T(8,128)(2,1)S(1)}, u32[]{:S(2)}, u32[]{:S(2)}) collective-permute-start(bf16[4,256,128]{2,1,0:T(8,128)(2,1)S(1)} %get-tuple-element.59), channel_id=1, source_target_pairs={{8,0},{9,1},{10,2},{11,3},{12,4},{13,5},{14,6},{15,7},{16,8},{17,9... | collective-permute-start | bytes 786440 | tf_op jit(solution)/shard_map/ppermute | solution.py:423
  108.9 3.6 %all-to-all-start = ((bf16[4,80,128]{2,1,0:T(8,128)(2,1)}), bf16[4,80,128]{2,1,0:T(8,128)(2,1)S(1)}, u32[]{:S(2)}, u32[]{:S(2)}) async-start(bf16[4,80,128]{2,1,0:T(8,128)(2,1)} %get-tuple-element.63), calls=%async_computation | async-start | bytes 163840 | tf_op jit(solution)/shard_map/all_to_all | solution.py:523
  112.5 2.5 %shard_map.99 = bf16[2,256,128]{2,1,0:T(8,128)(2,1)} custom-call(s32[5]{0:T(128)S(1)} %stack.65.flags, bf16[4,384,384]{2,1,0:T(8,128)(2,1)S(1)} %shard_map.95.w_ref, bf16[8,128,128]{2,1,0:T(8,128)(2,1)S(1)} %collective-permute-done.9.fm, bf16[2,128,128]{2,1,0:T(8,128)(2,1)S(1)} %collective-permute-done.10.fd, ...), custom_call_target="tpu_custom_call" | custom-call | flops 700000000 | bytes 4000000 | tf_op jit(solution)/shard_map/pallas_call | solution.py:304
  114.9 3.2 %all-to-all-done = bf16[4,80,128]{2,1,0:T(8,128)(2,1)S(1)} async-done(((bf16[4,80,128]{2,1,0:T(8,128)(2,1)}), bf16[4,80,128]{2,1,0:T(8,128)(2,1)S(1)}, u32[]{:S(2)}, u32[]{:S(2)}) %all-to-all-start) | async-done | bytes 81952 | tf_op jit(solution)/shard_map/all_to_all | solution.py:523
  (37 shorter events, 9.1 us)
Async XLA Ops:
  0.6 26.9 %copy-start.3 = (bf16[1,2,32,864]{3,2,1,0:T(8,128)(2,1)S(1)}, bf16[1,2,32,864]{3,2,1,0:T(8,128)(2,1)}, u32[]{:S(2)}) copy-start(bf16[1,2,32,864]{3,2,1,0:T(8,128)(2,1)} %param.11) | copy-start | bytes 331780
  2.5 0.9 copy-start.1
  6.3 31.5 %collective-permute-start.1 = (bf16[12,128,128]{2,1,0:T(8,128)(2,1)}, bf16[12,128,128]{2,1,0:T(8,128)(2,1)S(1)}, u32[]{:S(2)}, u32[]{:S(2)}) collective-permute-start(bf16[12,128,128]{2,1,0:T(8,128)(2,1)} %shard_map.93.nat), channel_id=1, source_target_pairs={{1,3},{2,0},{3,5},{4,2},{5,7},{6,4},{9,11},{10,8},{11,13},{12,10},... | collective-permute-start | bytes 1179656 | tf_op jit(solution)/shard_map/ppermute | solution.py:423
  7.6 31.5 %collective-permute-start = (bf16[12,128,128]{2,1,0:T(8,128)(2,1)}, bf16[12,128,128]{2,1,0:T(8,128)(2,1)S(1)}, u32[]{:S(2)}, u32[]{:S(2)}) collective-permute-start(bf16[12,128,128]{2,1,0:T(8,128)(2,1)} %shard_map.93.nat), channel_id=1, source_target_pairs={{0,1},{1,0},{2,3},{3,2},{4,5},{5,4},{6,7},{7,6},{8,9},{9,8},{10,11... | collective-permute-start | bytes 1179656 | tf_op jit(solution)/shard_map/ppermute | solution.py:423
  25.5 12.2 %collective-permute-start.3 = (bf16[2,2,128,128]{3,2,1,0:T(8,128)(2,1)S(1)}, bf16[2,2,128,128]{3,2,1,0:T(8,128)(2,1)S(1)}, u32[]{:S(2)}, u32[]{:S(2)}) collective-permute-start(bf16[2,2,128,128]{3,2,1,0:T(8,128)(2,1)S(1)} %get-tuple-element.36), channel_id=1, source_target_pairs={{113,2},{114,1},{115,4},{116,3},{117,6},{118,5},{393,506},{394,505... | collective-permute-start | bytes 393224 | tf_op jit(solution)/shard_map/ppermute | solution.py:423
  26.2 11.6 %collective-permute-start.2 = (bf16[2,2,128,128]{3,2,1,0:T(8,128)(2,1)S(1)}, bf16[2,2,128,128]{3,2,1,0:T(8,128)(2,1)S(1)}, u32[]{:S(2)}, u32[]{:S(2)}) collective-permute-start(bf16[2,2,128,128]{3,2,1,0:T(8,128)(2,1)S(1)} %get-tuple-element.36), channel_id=1, source_target_pairs={{112,1},{113,0},{114,3},{115,2},{116,5},{117,4},{118,7},{119,6},{3... | collective-permute-start | bytes 393224 | tf_op jit(solution)/shard_map/ppermute | solution.py:423
  26.9 10.9 %collective-permute-start.4 = (bf16[2,2,128,128]{3,2,1,0:T(8,128)(2,1)S(1)}, bf16[2,2,128,128]{3,2,1,0:T(8,128)(2,1)S(1)}, u32[]{:S(2)}, u32[]{:S(2)}) collective-permute-start(bf16[2,2,128,128]{3,2,1,0:T(8,128)(2,1)S(1)} %get-tuple-element.37.last_own), channel_id=1, source_target_pairs={{497,507},{498,504},{499,509},{500,506},{501,511},{502,508}} | collective-permute-start | bytes 393224 | tf_op jit(solution)/shard_map/ppermute | solution.py:423
  36.8 11.1 %copy-start = (bf16[12,128,128]{2,1,0:T(8,128)(2,1)S(1)}, bf16[12,128,128]{2,1,0:T(8,128)(2,1)}, u32[]{:S(2)}) copy-start(bf16[12,128,128]{2,1,0:T(8,128)(2,1)} %shard_map.93.nat) | copy-start | bytes 1179652
  39.1 8.8 %collective-permute-start.5 = (bf16[12,128,128]{2,1,0:T(8,128)(2,1)S(1)}, bf16[12,128,128]{2,1,0:T(8,128)(2,1)S(1)}, u32[]{:S(2)}, u32[]{:S(2)}) collective-permute-start(bf16[12,128,128]{2,1,0:T(8,128)(2,1)S(1)} %collective-permute-done.swp), channel_id=1, source_target_pairs={{0,2},{2,4},{3,1},{4,6},{5,3},{7,5},{8,10},{10,12},{11,9},{12,14},... | collective-permute-start | bytes 1179656 | tf_op jit(solution)/shard_map/ppermute | solution.py:423
  50.6 46.8 %collective-permute-start.6 = (bf16[20,128,128]{2,1,0:T(8,128)(2,1)S(1)}, bf16[20,128,128]{2,1,0:T(8,128)(2,1)S(1)}, u32[]{:S(2)}, u32[]{:S(2)}) collective-permute-start(bf16[20,128,128]{2,1,0:T(8,128)(2,1)S(1)} %get-tuple-element.41), channel_id=1, source_target_pairs={{8,0},{9,1},{10,2},{11,3},{12,4},{13,5},{14,6},{15,7},{16,8},{17,9... | collective-permute-start | bytes 1966088 | tf_op jit(solution)/shard_map/ppermute | solution.py:423
  68.0 29.4 %collective-permute-start.9 = (bf16[8,128,128]{2,1,0:T(8,128)(2,1)S(1)}, bf16[8,128,128]{2,1,0:T(8,128)(2,1)S(1)}, u32[]{:S(2)}, u32[]{:S(2)}) collective-permute-start(bf16[8,128,128]{2,1,0:T(8,128)(2,1)S(1)} %get-tuple-element.44.own), channel_id=1, source_target_pairs={{0,8},{1,9},{2,10},{3,11},{4,12},{5,13},{6,14},{7,15},{8,16},{9,17... | collective-permute-start | bytes 786440 | tf_op jit(solution)/shard_map/ppermute | solution.py:423
  78.7 12.2 %collective-permute-start.10 = (bf16[2,128,128]{2,1,0:T(8,128)(2,1)S(1)}, bf16[2,128,128]{2,1,0:T(8,128)(2,1)S(1)}, u32[]{:S(2)}, u32[]{:S(2)}) collective-permute-start(bf16[2,128,128]{2,1,0:T(8,128)(2,1)S(1)} %get-tuple-element.45), channel_id=1, source_target_pairs={{0,10},{2,12},{3,9},{4,14},{5,11},{7,13},{8,18},{10,20},{11,17},{1... | collective-permute-start | bytes 196616 | tf_op jit(solution)/shard_map/ppermute | solution.py:423
  84.5 7.7 %collective-permute-start.11 = (bf16[2,128,128]{2,1,0:T(8,128)(2,1)S(1)}, bf16[2,128,128]{2,1,0:T(8,128)(2,1)S(1)}, u32[]{:S(2)}, u32[]{:S(2)}) collective-permute-start(bf16[2,128,128]{2,1,0:T(8,128)(2,1)S(1)} %get-tuple-element.46), channel_id=1, source_target_pairs={{504,506},{505,507},{506,508},{507,509},{508,510},{509,511}} | collective-permute-start | bytes 196616 | tf_op jit(solution)/shard_map/ppermute | solution.py:423
  85.2 8.2 %collective-permute-start.7 = (bf16[4,128,128]{2,1,0:T(8,128)(2,1)S(1)}, bf16[4,128,128]{2,1,0:T(8,128)(2,1)S(1)}, u32[]{:S(2)}, u32[]{:S(2)}) collective-permute-start(bf16[4,128,128]{2,1,0:T(8,128)(2,1)S(1)} %get-tuple-element.42), channel_id=1, source_target_pairs={{8,2},{9,3},{10,4},{11,5},{12,6},{13,7},{16,10},{17,11},{18,12},{1... | collective-permute-start | bytes 393224 | tf_op jit(solution)/shard_map/ppermute | solution.py:423
  90.9 6.5 %collective-permute-start.8 = (bf16[4,128,128]{2,1,0:T(8,128)(2,1)S(1)}, bf16[4,128,128]{2,1,0:T(8,128)(2,1)S(1)}, u32[]{:S(2)}, u32[]{:S(2)}) collective-permute-start(bf16[4,128,128]{2,1,0:T(8,128)(2,1)S(1)} %get-tuple-element.43), channel_id=1, source_target_pairs={{10,0},{11,1},{12,2},{13,3},{14,4},{15,5},{18,8},{19,9},{20,10},{2... | collective-permute-start | bytes 393224 | tf_op jit(solution)/shard_map/ppermute | solution.py:423
  92.2 0.7 collective-permute-start.12
  101.2 17.9 %collective-permute-start.13 = (bf16[4,256,128]{2,1,0:T(8,128)(2,1)S(1)}, bf16[4,256,128]{2,1,0:T(8,128)(2,1)S(1)}, u32[]{:S(2)}, u32[]{:S(2)}) collective-permute-start(bf16[4,256,128]{2,1,0:T(8,128)(2,1)S(1)} %get-tuple-element.59), channel_id=1, source_target_pairs={{8,0},{9,1},{10,2},{11,3},{12,4},{13,5},{14,6},{15,7},{16,8},{17,9... | collective-permute-start | bytes 786440 | tf_op jit(solution)/shard_map/ppermute | solution.py:423
  108.9 9.3 %all-to-all-start = ((bf16[4,80,128]{2,1,0:T(8,128)(2,1)}), bf16[4,80,128]{2,1,0:T(8,128)(2,1)S(1)}, u32[]{:S(2)}, u32[]{:S(2)}) async-start(bf16[4,80,128]{2,1,0:T(8,128)(2,1)} %get-tuple-element.63), calls=%async_computation | async-start | bytes 163840 | tf_op jit(solution)/shard_map/all_to_all | solution.py:523
  112.5 6.6 %copy-start.2 = (bf16[1,2,32,2,4,128]{5,4,3,2,1,0:T(4,128)(2,1)S(1)}, bf16[1,2,32,2,4,128]{5,4,3,2,1,0:T(4,128)(2,1)}, u32[]{:S(2)}) copy-start(bf16[1,2,32,2,4,128]{5,4,3,2,1,0:T(4,128)(2,1)} %get-tuple-element.70) | copy-start | bytes 393220

commit v5 on v4

--- a/solution.py
+++ b/solution.py
@@ -46,10 +46,10 @@
             use(start + d + k, y[R : 2 * R, cols] + left + right)
 
 
-def mask(d, v, inner, keep):
-    if d == 0:
+def mask(d, v, inner, keep, edge=1):
+    if d < edge:
         v = v * keep[0]
-    if d == inner - 1:
+    if d >= inner - edge:
         v = v * keep[1]
     return v
 
@@ -60,7 +60,7 @@
         act_b[p] = silu(fb[p])
 
     def one(d, v):
-        out = mask(d, wide(fa[d]) + v, inner, keep).astype(BF16)
+        out = mask(d, wide(fa[d]) + v, inner, keep, max(1, n - 8)).astype(BF16)
         out_a[d] = out
         act_a[d] = silu(out)
 
@@ -145,11 +145,11 @@
     )
 
 
-def tick1_window(zh, b, a, b_at, a_at, nat, swp, near, far):
+def tick1_window(zh, b, a, b_at, a_at, near_b, near_a, nat, swp, near, far):
     move(
         window1(
             zh, b, a, at(nat, b_at, 2), at(nat, a_at, 2), at(swp, b_at, 2), at(swp, a_at, 2),
-            at(near, b_at, 2), at(near, a_at + zh, 1), at(far, b_at, 2), at(far, a_at + 1 - zh, 1),
+            at(near, near_b, 2), at(near, near_a, 1), at(far, b_at, 2), at(far, a_at + 1 - zh, 1),
         )
     )
 
@@ -157,7 +157,7 @@
 def tick1_back(flags, w_ref, nat, swp, near, far, bm, bl, bh, dw, *scratch):
     bb, ba, db, da, rec_a, rec_b, grad_a, grad_b, act_b, act_a = scratch
     for k, (b, a) in enumerate(((bb, ba), (db, da))):
-        tick1_window(flags[0], b, a, 2 * k, 4 + 2 * k, nat, swp, near, far)
+        tick1_window(flags[0], b, a, 2 * k, 4 + 2 * k, 2 * k, 8 + k, nat, swp, near, far)
     backward(keeps(flags), w_ref, bb, ba, db, da, rec_a, rec_b, grad_a, grad_b, act_b, act_a, 0, 4)
     move([
         (rec_b, at(bm, 0, 4)),
@@ -172,27 +172,41 @@
     dw[0], dw[1] = weight_sums(db, grad_a, act_b, act_a)
 
 
-def tick1_forward(flags, w_ref, nat, swp, near, far, last_own, fm, fd, ll, lh, y1w, *scratch):
+def tick1_forward(flags, w_ref, nat, swp, near, far, last_own, e1, e2, fm, fd, own, *scratch):
     fb, fa, out_a, out_b, act_b, act_a = scratch
-    fz = flags[3]
-    tick1_window(flags[0], fb, fa, 8, 10, nat, swp, near, far)
-    forward(8, keeps(flags), w_ref, fb, fa, out_a, out_b, act_b, act_a)
-    move([
-        (out_b, at(fm, 0, 4)),
-        (at(out_a, 2 * fz, 4), at(fm, 4, 4)),
-        (at(out_b, 2 - 2 * fz, 2), fd),
-        (at(out_a, 3, 1), at(ll, 0, 1)),
-        (at(out_b, 3, 1), at(ll, 1, 1)),
-        (at(out_a, 2, 1), at(lh, 0, 1)),
-        (at(out_b, 0, 1), at(lh, 1, 1)),
-        (out_a, at(y1w, 0, 6)),
-        (last_own.at[0], at(y1w, 6, 2)),
-        (last_own.at[1], at(y1w, 8, 2)),
-    ])
+    zh, fz = (flags[0], flags[3])
+
+    @pl.when(flags[6] == 0)
+    def _():
+        tick1_window(zh, fb, fa, 8, 10, 4, 6 + zh, nat, swp, near, far)
+        forward(8, keeps(flags), w_ref, fb, fa, out_a, out_b, act_b, act_a)
+        move([
+            (at(out_b, 0, 4), at(fm, 0, 4)),
+            (at(out_a, 2 * fz, 4), at(fm, 4, 4)),
+            (at(out_b, 2 - 2 * fz, 2), fd),
+        ])
+
+    @pl.when(flags[6] == 1)
+    def _():
+        for win, k in ((at(fb, 1, 8), 8), (fa, 10)):
+            move([
+                (at(nat, k, 2), at(win, 2 + 2 * zh, 2)),
+                (at(swp, k, 2), at(win, 4 - 2 * zh, 2)),
+                (at(near, k - 4, 2), at(win, 6 - 6 * zh, 2)),
+                (at(far, k, 2), at(win, 6 * zh, 2)),
+            ])
+        move([(at(e1, 1 - zh, 1), at(fb, 9 * zh, 1)), (at(e2, zh, 1), at(fb, 9 - 9 * zh, 1))])
+        forward(10, keeps(flags), w_ref, fb, fa, out_a, out_b, act_b, act_a)
+        move([
+            (out_a, at(own, 0, 8)),
+            (out_b, at(own, 8, 6)),
+            (last_own.at[0], at(own, 14, 2)),
+            (last_own.at[1], at(own, 16, 2)),
+        ])
 
 
 def tick2_back(
-    scale, flags, w_ref, bm, bl, bh, sp1, sp2, sp3, y1w, own, ll, lh, dw, out, parts, *scratch
+    scale, flags, w_ref, bm, bl, bh, sp1, sp2, sp3, own, dw, out, parts, *scratch
 ):
     bb, ba, db, da, rec_a, rec_b, grad_a, grad_b, act_b, act_a = scratch
     zh = flags[0]
@@ -200,16 +214,12 @@
     @pl.when(flags[6] == 1)
     def _():
         move(window1(
-            zh, db, da, at(y1w, 8, 2), at(y1w, 6, 2), sp1.at[1], sp1.at[0],
+            zh, db, da, at(own, 16, 2), at(own, 14, 2), sp1.at[1], sp1.at[0],
             sp3.at[1], at(sp3.at[0], zh, 1), sp2.at[1], at(sp2.at[0], 1 - zh, 1),
         ))
         move([
-            (at(y1w, 0, 6), at(bb, 1, 6)),
-            (at(ll, 0, 1), at(bb, 0, 1)),
-            (at(lh, 0, 1), at(bb, 7, 1)),
-            (at(own, 0, 4), at(ba, 1, 4)),
-            (at(ll, 1, 1), at(ba, 0, 1)),
-            (at(lh, 1, 1), at(ba, 5, 1)),
+            (at(own, 0, 8), bb),
+            (at(own, 8, 6), ba),
         ])
 
     @pl.when(flags[6] == 0)
@@ -373,7 +383,15 @@
         nat[2 * k + 1] = v[R:]
 
 
-def prepare_ends_kernel(flags, batch, loss, first_own, last_own, ends):
+def prepare_ends_kernel(flags, batch, loss, nat, first_own, last_own, ends, near, nat_x2):
+    zh = flags[0]
+    move([
+        (at(nat, 0, 4), at(near, 0, 4)),
+        (at(nat, 8, 4), at(near, 4, 4)),
+        (at(nat, 4 + zh, 1), at(near, 8, 1)),
+        (at(nat, 6 + zh, 1), at(near, 9, 1)),
+        (at(nat, 8, 2), nat_x2),
+    ])
     x1, x2, d1, d2 = reorder(to_inside(), [batch[0], batch[1], loss[0], loss[1]])
     for ref, pair in ((first_own, (x1, x2)), (last_own, (d1, d2))):
         for k in range(2):
@@ -451,18 +469,19 @@
         58,
     )
     swp = swap(nat)
-    first_own, last_own, ends = call(
+    first_own, last_own, ends, near, nat_x2 = call(
         prepare_ends_kernel,
-        [shaped(2, 2)] * 3,
+        [shaped(2, 2)] * 3 + [shaped(10), shaped(2)],
         [],
-        (flags1, flat_rows(batch_next), flat_rows(loss_grad[0])),
+        (flags1, flat_rows(batch_next), flat_rows(loss_grad[0]), nat),
         100_000_000,
-        [SMEM] + [VMEM] * 2,
-        [VMEM] * 3,
-    )
-
-    own_planes, ends = lax.optimization_barrier((nat, ends))
-    near = route(own_planes, lambda s, yy, zz: (s, yy - 1 + 2 * zz, zz))
+        [SMEM] + [VMEM] * 3,
+        [VMEM] * 5,
+    )
+
+    near = route(near, lambda s, yy, zz: (s, yy - 1 + 2 * zz, zz))
+    e1 = route(nat_x2, lambda s, yy, zz: (s if s == count - 1 else -1, yy + 1 - 2 * zz, zz))
+    e2 = route(nat_x2, lambda s, yy, zz: (s if s == count - 1 else -1, yy + 1 - 2 * zz, 1 - zz))
 
     def end_of(s):
         return 0 if s == from_first else count - 1 if s == from_last else -1
@@ -473,7 +492,7 @@
     mats = matrices(weights[0])
 
 
-    swp, near, sp1, sp2, sp3, mats = lax.optimization_barrier((swp, near, sp1, sp2, sp3, mats))
+    swp, near, sp1, sp2, sp3, e1, e2, mats = lax.optimization_barrier((swp, near, sp1, sp2, sp3, e1, e2, mats))
 
     far = route(swp, lambda s, yy, zz: (s, yy + 1 - 2 * zz, zz))
     bm, bl, bh, dw = call(
@@ -494,28 +513,26 @@
     bl2 = route(bl, lambda s, yy, zz: (s - 1, yy + 1, back_side(s, zz)))
     bh2 = route(bh, lambda s, yy, zz: (s - 1, yy - 1, back_side(s, zz)))
 
-    fm, fd, ll, lh, y1w = call(
+    fm, fd, own = call(
         tick1_forward,
-        [shaped(8), shaped(2), shaped(2), shaped(2), shaped(10)],
-        [planes(8), planes(6), planes(6), planes(4), planes(8), planes(6)],
-        (flags1, mats, nat, swp, near, far, last_own),
+        [shaped(8), shaped(2), shaped(18)],
+        [planes(10), planes(8), planes(8), planes(6), planes(10), planes(8)],
+        (flags1, mats, nat, swp, near, far, last_own, e1, e2),
         1_000_000_000,
-        [SMEM] + [VMEM] * 6,
-        [VMEM] * 5,
-    )
-    ll2 = route(ll, lambda s, yy, zz: (s if s == count - 1 else -1, yy + 1, zz))
-    lh2 = route(lh, lambda s, yy, zz: (s if s == count - 1 else -1, yy - 1, zz))
+        [SMEM] + [VMEM] * 8,
+        [VMEM] * 3,
+    )
     fd2 = route(fd, fwd_diag)
     fm2 = route(fm, lambda s, yy, zz: (s + 1, yy, fwd_side(s, zz)))
 
-    bm2, bl2, bh2, fm2, fd2, ll2, lh2 = lax.optimization_barrier((bm2, bl2, bh2, fm2, fd2, ll2, lh2))
+    bm2, bl2, bh2, fm2, fd2 = lax.optimization_barrier((bm2, bl2, bh2, fm2, fd2))
     out_b, parts = call(
         functools.partial(tick2_back, scale),
         [((4, 2 * R, W), BF16), ((ny, slab_rows(slabs), W), BF16)],
         [planes(8), planes(6), planes(8), planes(6), planes(6), planes(4), planes(6), planes(4), planes(8), planes(6)],
-        (flags1, mats, bm2, bl2, bh2, sp1, sp2, sp3, y1w, fm, ll2, lh2, dw),
+        (flags1, mats, bm2, bl2, bh2, sp1, sp2, sp3, own, dw),
         1_500_000_000,
-        [SMEM] + [VMEM] * 12,
+        [SMEM] + [VMEM] * 9,
         [VMEM, VMEM],
     )
     back = route(out_b, lambda s, yy, zz: (s - 1, yy, zz))

time: 120 us -> 115 us (0.958)
  waiting for transfers between devices: 14.3 us -> 10.4 us
  starting transfers between devices: 76.4 us -> 72.6 us
  local copies, waits for them, and re-layouts: 11.5 us -> 12.8 us
    ppermute x14, starting transfers between devices: 72.8 us -> 67.5 us  [route(): return lax.ppermute(value, ('segment', 'slab'), pairs)]
    ppermute x14, waiting for transfers between devices: 11.1 us -> 7.17 us  [route(): return lax.ppermute(value, ('segment', 'slab'), pairs)]
    all_to_all x1, starting transfers between devices: 3.59 us -> 5.06 us  [local(): lax.all_to_all(parts, 'slab', 0, 0, axis_index_groups=columns, tiled=True)]
    unnamed x11 -> x21, local copies, waits for them, and re-layouts: 5.83 us -> 7.19 us
  transfers between devices with their start and end apart: 15 -> 15, of which waited for: 5 -> 3; matrix products, arithmetic and copies ran while one was open for 9% -> 11% of each run, Pallas kernels for 4% -> 5%
where the time goes in v5:
time: 115 us; the launch traced here: 114 us
  starting transfers between devices  72.6 us (63%)
  Pallas kernels  14.6 us (13%)
  local copies, waits for them, and re-layouts  12.8 us (11%)
  waiting for transfers between devices  10.4 us (9%)
  other arithmetic  2.79 us (2%)
    ppermute x14, starting transfers between devices, route(): return lax.ppermute(value, ('segment', 'slab'), pairs)  67.5 us
    pallas_call x7, Pallas kernels, call(): pl.pallas_call(kernel, out_shape=tuple((jax.ShapeDtypeStruct(s, t) for s,...  14.6 us
    unnamed x21, local copies, waits for them, and re-layouts  7.19 us
    ppermute x14, waiting for transfers between devices, route(): return lax.ppermute(value, ('segment', 'slab'), pairs)  7.17 us
    all_to_all x1, starting transfers between devices, local(): lax.all_to_all(parts, 'slab', 0, 0, axis_index_groups=columns, tiled=True)  5.06 us
    all_to_all x1, waiting for transfers between devices, local(): lax.all_to_all(parts, 'slab', 0, 0, axis_index_groups=columns, tiled=True)  3.23 us
  transfers between devices with their start and end apart: 15, of which 3 were waited for; matrix products, arithmetic and copies ran while one was open for 11% of the time, Pallas kernels for 5%

profile of v5, /device:TPU:6, one launch (start us, length us, event | category | flops | bytes accessed | tf_op | source)
XLA Modules:
  0.0 114.2 jit_solution(2898705514696076024)
XLA Ops:
  0.7 2.1 %shard_map.93.nat = bf16[12,128,128]{2,1,0:T(8,128)(2,1)} custom-call(bf16[2,256,128]{2,1,0:T(8,128)(2,1)} %bitcast.32, bf16[2,256,128]{2,1,0:T(8,128)(2,1)} %bitcast.33, bf16[2,256,128]{2,1,0:T(8,128)(2,1)} %bitcast.34), custom_call_target="tpu_custom_call" | custom-call | flops 100000000 | bytes 4000000 | tf_op jit(solution)/shard_map/pallas_call | solution.py:314
  2.8 15.7 %collective-permute-start = (bf16[12,128,128]{2,1,0:T(8,128)(2,1)}, bf16[12,128,128]{2,1,0:T(8,128)(2,1)S(1)}, u32[]{:S(2)}, u32[]{:S(2)}) collective-permute-start(bf16[12,128,128]{2,1,0:T(8,128)(2,1)} %shard_map.93.nat), channel_id=1, source_target_pairs={{0,1},{1,0},{2,3},{3,2},{4,5},{5,4},{6,7},{7,6},{8,9},{9,8},{10,11... | collective-permute-start | bytes 1179656 | tf_op jit(solution)/shard_map/ppermute | solution.py:441
  18.5 1.7 %fusion = (bf16[1,2,32,2,4,128]{5,4,3,2,1,0:T(4,128)(2,1)}, bf16[1,2,32,2,4,128]{5,4,3,2,1,0:T(4,128)(2,1)S(1)}) fusion(bf16[2,2,32,2,4,128]{5,4,3,2,1,0:T(4,128)(2,1)} %param.10), kind=kLoop, calls=%fused_computation.5 | loop fusion | bytes 524288 | tf_op jit(solution)/shard_map/slice | solution.py:557
  20.3 1.0 copy-done
  21.3 1.5 %shard_map.94 = (bf16[2,2,128,128]{3,2,1,0:T(8,128)(2,1)S(1)}, bf16[2,2,128,128]{3,2,1,0:T(8,128)(2,1)S(1)}, bf16[2,2,128,128]{3,2,1,0:T(8,128)(2,1)}, bf16[10,1...) custom-call(s32[7]{0:T(128)S(1)} %stack.73.flags, bf16[2,256,128]{2,1,0:T(8,128)(2,1)S(1)} %bitcast.26, ...), custom_call_target="tpu_custom_call" | custom-call | flops 100000000 | bytes 4000000 | tf_op jit(solution)/shard_map/pallas_call | solution.py:314
  23.4 1.3 %collective-permute-start.1 = (bf16[10,128,128]{2,1,0:T(8,128)(2,1)S(1)}, bf16[10,128,128]{2,1,0:T(8,128)(2,1)S(1)}, u32[]{:S(2)}, u32[]{:S(2)}) collective-permute-start(bf16[10,128,128]{2,1,0:T(8,128)(2,1)S(1)} %get-tuple-element.32), channel_id=1, source_target_pairs={{1,3},{2,0},{3,5},{4,2},{5,7},{6,4},{9,11},{10,8},{11,13},{12,10},... | collective-permute-start | bytes 983048 | tf_op jit(solution)/shard_map/ppermute | solution.py:441
  30.4 2.0 %maximum_bitcast_fusion = bf16[4,3,32,3,3,32]{2,0,1,4,3,5:T(4,128)(2,1)} fusion(bf16[2,32,32,3,3,3]{1,0,5,4,3,2:T(2,128)(2,1)S(1)} %reverse_bitcast_fusion, bf16[2,32,32,3,3,3]{1,0,5,4,3,2:T(2,128)(2,1)S(1)} %bitcast.28), kind=kLoop, calls=%fused_computation | loop fusion | flops 442368 | bytes 442368 | tf_op jit(solution)/shard_map/transpose | solution.py:415
  32.5 3.5 %copy.17 = bf16[4,3,32,3,3,32]{5,4,3,2,1,0:T(4,128)(2,1)} copy(bf16[4,3,32,3,3,32]{2,0,1,4,3,5:T(4,128)(2,1)} %maximum_bitcast_fusion) | data formatting | bytes 442368
  35.9 2.0 %pad.4.clone = bf16[4,3,32,3,4,32]{5,4,3,2,1,0:T(4,128)(2,1)S(1)} pad(bf16[4,3,32,3,3,32]{5,4,3,2,1,0:T(4,128)(2,1)} %copy.17, bf16[]{:T(256)} %constant.56.clone.1), padding=0_0x0_0x0_0x0_0x0_1x0_0 | pad | bytes 516098 | tf_op jit(solution)/shard_map/jit(_pad)/pad | solution.py:416
  39.0 4.6 %collective-permute-start.7 = (bf16[12,128,128]{2,1,0:T(8,128)(2,1)S(1)}, bf16[12,128,128]{2,1,0:T(8,128)(2,1)S(1)}, u32[]{:S(2)}, u32[]{:S(2)}) collective-permute-start(bf16[12,128,128]{2,1,0:T(8,128)(2,1)S(1)} %collective-permute-done.swp), channel_id=1, source_target_pairs={{0,2},{2,4},{3,1},{4,6},{5,3},{7,5},{8,10},{10,12},{11,9},{12,14},... | collective-permute-start | bytes 1179656 | tf_op jit(solution)/shard_map/ppermute | solution.py:441
  43.5 5.3 %collective-permute-done.7.far = bf16[12,128,128]{2,1,0:T(8,128)(2,1)S(1)} collective-permute-done((bf16[12,128,128]{2,1,0:T(8,128)(2,1)S(1)}, bf16[12,128,128]{2,1,0:T(8,128)(2,1)S(1)}, u32[]{:S(2)}, u32[]{:S(2)}) %collective-permute-start.7) | collective-permute-done | bytes 393248 | tf_op jit(solution)/shard_map/ppermute | solution.py:441
  48.8 2.7 %shard_map.96 = (bf16[20,128,128]{2,1,0:T(8,128)(2,1)S(1)}, bf16[4,128,128]{2,1,0:T(8,128)(2,1)S(1)}, bf16[4,128,128]{2,1,0:T(8,128)(2,1)S(1)}, f32[2,288,96]{2,1,0:T(8,128)S(1)}) custom-call(s32[7]{0:T(128)S(1)} %stack.73.flags, bf16[4,384,384]{2,1,0:T(8,128)(2,1)S(1)} %shard_map.95.w_ref, bf16[12,128,128]{2,1,0:T(8,128)(2,1)S(1)} %copy-done.1, ...), custom_call_target="tpu_custom_call" | custom-call | flops 2000000000 | bytes 4000000 | tf_op jit(solution)/shard_map/pallas_call | solution.py:314
  51.5 17.1 %collective-permute-start.8 = (bf16[20,128,128]{2,1,0:T(8,128)(2,1)S(1)}, bf16[20,128,128]{2,1,0:T(8,128)(2,1)S(1)}, u32[]{:S(2)}, u32[]{:S(2)}) collective-permute-start(bf16[20,128,128]{2,1,0:T(8,128)(2,1)S(1)} %get-tuple-element.39), channel_id=1, source_target_pairs={{8,0},{9,1},{10,2},{11,3},{12,4},{13,5},{14,6},{15,7},{16,8},{17,9... | collective-permute-start | bytes 1966088 | tf_op jit(solution)/shard_map/ppermute | solution.py:441
  68.7 1.7 %shard_map.97 = (bf16[8,128,128]{2,1,0:T(8,128)(2,1)S(1)}, bf16[2,128,128]{2,1,0:T(8,128)(2,1)S(1)}, bf16[18,128,128]{2,1,0:T(8,128)(2,1)S(1)}) custom-call(s32[7]{0:T(128)S(1)} %stack.73.flags, bf16[4,384,384]{2,1,0:T(8,128)(2,1)S(1)} %shard_map.95.w_ref, bf16[12,128,128]{2,1,0:T(8,128)(2,1)S(1)} %copy-done.1, ...), custom_call_target="tpu_custom_call" | custom-call | flops 1000000000 | bytes 4000000 | tf_op jit(solution)/shard_map/pallas_call | solution.py:314
  70.4 14.3 %collective-permute-start.11 = (bf16[8,128,128]{2,1,0:T(8,128)(2,1)S(1)}, bf16[8,128,128]{2,1,0:T(8,128)(2,1)S(1)}, u32[]{:S(2)}, u32[]{:S(2)}) collective-permute-start(bf16[8,128,128]{2,1,0:T(8,128)(2,1)S(1)} %get-tuple-element.44), channel_id=1, source_target_pairs={{0,8},{1,9},{2,10},{3,11},{4,12},{5,13},{6,14},{7,15},{8,16},{9,17... | collective-permute-start | bytes 786440 | tf_op jit(solution)/shard_map/ppermute | solution.py:441
  84.8 1.3 %collective-permute-start.9 = (bf16[4,128,128]{2,1,0:T(8,128)(2,1)S(1)}, bf16[4,128,128]{2,1,0:T(8,128)(2,1)S(1)}, u32[]{:S(2)}, u32[]{:S(2)}) collective-permute-start(bf16[4,128,128]{2,1,0:T(8,128)(2,1)S(1)} %get-tuple-element.40), channel_id=1, source_target_pairs={{8,2},{9,3},{10,4},{11,5},{12,6},{13,7},{16,10},{17,11},{18,12},{1... | collective-permute-start | bytes 393224 | tf_op jit(solution)/shard_map/ppermute | solution.py:441
  86.1 1.3 %collective-permute-start.10 = (bf16[4,128,128]{2,1,0:T(8,128)(2,1)S(1)}, bf16[4,128,128]{2,1,0:T(8,128)(2,1)S(1)}, u32[]{:S(2)}, u32[]{:S(2)}) collective-permute-start(bf16[4,128,128]{2,1,0:T(8,128)(2,1)S(1)} %get-tuple-element.41), channel_id=1, source_target_pairs={{10,0},{11,1},{12,2},{13,3},{14,4},{15,5},{18,8},{19,9},{20,10},{2... | collective-permute-start | bytes 393224 | tf_op jit(solution)/shard_map/ppermute | solution.py:441
  87.4 6.7 %collective-permute-start.12 = (bf16[2,128,128]{2,1,0:T(8,128)(2,1)S(1)}, bf16[2,128,128]{2,1,0:T(8,128)(2,1)S(1)}, u32[]{:S(2)}, u32[]{:S(2)}) collective-permute-start(bf16[2,128,128]{2,1,0:T(8,128)(2,1)S(1)} %get-tuple-element.45), channel_id=1, source_target_pairs={{0,10},{2,12},{3,9},{4,14},{5,11},{7,13},{8,18},{10,20},{11,17},{1... | collective-permute-start | bytes 196616 | tf_op jit(solution)/shard_map/ppermute | solution.py:441
  94.1 1.9 %collective-permute-done.12.fd = bf16[2,128,128]{2,1,0:T(8,128)(2,1)S(1)} collective-permute-done((bf16[2,128,128]{2,1,0:T(8,128)(2,1)S(1)}, bf16[2,128,128]{2,1,0:T(8,128)(2,1)S(1)}, u32[]{:S(2)}, u32[]{:S(2)}) %collective-permute-start.12) | collective-permute-done | bytes 65568 | tf_op jit(solution)/shard_map/ppermute | solution.py:441
  96.0 3.8 %shard_map.98 = (bf16[4,256,128]{2,1,0:T(8,128)(2,1)S(1)}, bf16[4,80,128]{2,1,0:T(8,128)(2,1)}) custom-call(s32[7]{0:T(128)S(1)} %stack.73.flags, bf16[4,384,384]{2,1,0:T(8,128)(2,1)S(1)} %shard_map.95.w_ref, bf16[20,128,128]{2,1,0:T(8,128)(2,1)S(1)} %collective-permute-done.8.bm, bf16[4,128,128]{2,1,0:T(8,128)(2,1)S(1)} %collective-permute-done.9.bl, ...), custom_call_target="tpu_custom_call" | custom-call | flops 1500000000 | bytes 4000000 | tf_op jit(solution)/shard_map/pallas_call | solution.py:314
  99.7 1.9 %collective-permute-start.13 = (bf16[4,256,128]{2,1,0:T(8,128)(2,1)S(1)}, bf16[4,256,128]{2,1,0:T(8,128)(2,1)S(1)}, u32[]{:S(2)}, u32[]{:S(2)}) collective-permute-start(bf16[4,256,128]{2,1,0:T(8,128)(2,1)S(1)} %get-tuple-element.55), channel_id=1, source_target_pairs={{8,0},{9,1},{10,2},{11,3},{12,4},{13,5},{14,6},{15,7},{16,8},{17,9... | collective-permute-start | bytes 786440 | tf_op jit(solution)/shard_map/ppermute | solution.py:441
  101.8 5.1 %all-to-all-start = ((bf16[4,80,128]{2,1,0:T(8,128)(2,1)}), bf16[4,80,128]{2,1,0:T(8,128)(2,1)S(1)}, u32[]{:S(2)}, u32[]{:S(2)}) async-start(bf16[4,80,128]{2,1,0:T(8,128)(2,1)} %get-tuple-element.59), calls=%async_computation | async-start | bytes 163840 | tf_op jit(solution)/shard_map/all_to_all | solution.py:540
  106.8 2.5 %shard_map.99 = bf16[2,256,128]{2,1,0:T(8,128)(2,1)} custom-call(s32[5]{0:T(128)S(1)} %stack.65.flags, bf16[4,384,384]{2,1,0:T(8,128)(2,1)S(1)} %shard_map.95.w_ref, bf16[8,128,128]{2,1,0:T(8,128)(2,1)S(1)} %collective-permute-done.11.fm, bf16[2,128,128]{2,1,0:T(8,128)(2,1)S(1)} %collective-permute-done.12.fd, ...), custom_call_target="tpu_custom_call" | custom-call | flops 700000000 | bytes 4000000 | tf_op jit(solution)/shard_map/pallas_call | solution.py:314
  109.3 3.2 %all-to-all-done = bf16[4,80,128]{2,1,0:T(8,128)(2,1)S(1)} async-done(((bf16[4,80,128]{2,1,0:T(8,128)(2,1)}), bf16[4,80,128]{2,1,0:T(8,128)(2,1)S(1)}, u32[]{:S(2)}, u32[]{:S(2)}) %all-to-all-start) | async-done | bytes 81952 | tf_op jit(solution)/shard_map/all_to_all | solution.py:540
  (47 shorter events, 9.1 us)
Async XLA Ops:
  0.6 19.7 %copy-start.2 = (bf16[2,32,2,4,128]{4,3,2,1,0:T(4,128)(2,1)S(1)}, bf16[2,32,2,4,128]{4,3,2,1,0:T(4,128)(2,1)}, u32[]{:S(2)}) copy-start(bf16[2,32,2,4,128]{4,3,2,1,0:T(4,128)(2,1)} %param.9) | copy-start | bytes 393220
  0.6 26.1 %copy-start.8 = (bf16[1,2,32,864]{3,2,1,0:T(8,128)(2,1)S(1)}, bf16[1,2,32,864]{3,2,1,0:T(8,128)(2,1)}, u32[]{:S(2)}) copy-start(bf16[1,2,32,864]{3,2,1,0:T(8,128)(2,1)} %param.11) | copy-start | bytes 331780
  2.8 36.2 %collective-permute-start = (bf16[12,128,128]{2,1,0:T(8,128)(2,1)}, bf16[12,128,128]{2,1,0:T(8,128)(2,1)S(1)}, u32[]{:S(2)}, u32[]{:S(2)}) collective-permute-start(bf16[12,128,128]{2,1,0:T(8,128)(2,1)} %shard_map.93.nat), channel_id=1, source_target_pairs={{0,1},{1,0},{2,3},{3,2},{4,5},{5,4},{6,7},{7,6},{8,9},{9,8},{10,11... | collective-permute-start | bytes 1179656 | tf_op jit(solution)/shard_map/ppermute | solution.py:441
  20.3 1.0 copy-start
  22.8 0.7 copy-start.5
  23.4 15.5 %collective-permute-start.1 = (bf16[10,128,128]{2,1,0:T(8,128)(2,1)S(1)}, bf16[10,128,128]{2,1,0:T(8,128)(2,1)S(1)}, u32[]{:S(2)}, u32[]{:S(2)}) collective-permute-start(bf16[10,128,128]{2,1,0:T(8,128)(2,1)S(1)} %get-tuple-element.32), channel_id=1, source_target_pairs={{1,3},{2,0},{3,5},{4,2},{5,7},{6,4},{9,11},{10,8},{11,13},{12,10},... | collective-permute-start | bytes 983048 | tf_op jit(solution)/shard_map/ppermute | solution.py:441
  24.7 3.7 %collective-permute-start.6 = (bf16[2,128,128]{2,1,0:T(8,128)(2,1)S(1)}, bf16[2,128,128]{2,1,0:T(8,128)(2,1)S(1)}, u32[]{:S(2)}, u32[]{:S(2)}) collective-permute-start(bf16[2,128,128]{2,1,0:T(8,128)(2,1)S(1)} %get-tuple-element.35), channel_id=1, source_target_pairs={{504,507},{506,509},{507,504},{508,511},{509,506},{511,508}} | collective-permute-start | bytes 196616 | tf_op jit(solution)/shard_map/ppermute | solution.py:441
  25.4 3.8 %collective-permute-start.5 = (bf16[2,128,128]{2,1,0:T(8,128)(2,1)S(1)}, bf16[2,128,128]{2,1,0:T(8,128)(2,1)S(1)}, u32[]{:S(2)}, u32[]{:S(2)}) collective-permute-start(bf16[2,128,128]{2,1,0:T(8,128)(2,1)S(1)} %get-tuple-element.35), channel_id=1, source_target_pairs={{504,506},{506,508},{507,505},{508,510},{509,507},{511,509}} | collective-permute-start | bytes 196616 | tf_op jit(solution)/shard_map/ppermute | solution.py:441
  26.1 12.8 %collective-permute-start.3 = (bf16[2,2,128,128]{3,2,1,0:T(8,128)(2,1)}, bf16[2,2,128,128]{3,2,1,0:T(8,128)(2,1)S(1)}, u32[]{:S(2)}, u32[]{:S(2)}) collective-permute-start(bf16[2,2,128,128]{3,2,1,0:T(8,128)(2,1)} %get-tuple-element.33), channel_id=1, source_target_pairs={{113,2},{114,1},{115,4},{116,3},{117,6},{118,5},{393,506},{394,505... | collective-permute-start | bytes 393224 | tf_op jit(solution)/shard_map/ppermute | solution.py:441
  28.5 10.5 %collective-permute-start.2 = (bf16[2,2,128,128]{3,2,1,0:T(8,128)(2,1)}, bf16[2,2,128,128]{3,2,1,0:T(8,128)(2,1)S(1)}, u32[]{:S(2)}, u32[]{:S(2)}) collective-permute-start(bf16[2,2,128,128]{3,2,1,0:T(8,128)(2,1)} %get-tuple-element.33), channel_id=1, source_target_pairs={{112,1},{113,0},{114,3},{115,2},{116,5},{117,4},{118,7},{119,6},{3... | collective-permute-start | bytes 393224 | tf_op jit(solution)/shard_map/ppermute | solution.py:441
  29.1 0.6 copy-start.3
  29.8 9.2 %collective-permute-start.4 = (bf16[2,2,128,128]{3,2,1,0:T(8,128)(2,1)S(1)}, bf16[2,2,128,128]{3,2,1,0:T(8,128)(2,1)S(1)}, u32[]{:S(2)}, u32[]{:S(2)}) collective-permute-start(bf16[2,2,128,128]{3,2,1,0:T(8,128)(2,1)S(1)} %get-tuple-element.34.last_own), channel_id=1, source_target_pairs={{497,507},{498,504},{499,509},{500,506},{501,511},{502,508}} | collective-permute-start | bytes 393224 | tf_op jit(solution)/shard_map/ppermute | solution.py:441
  37.9 10.9 %copy-start.1 = (bf16[12,128,128]{2,1,0:T(8,128)(2,1)S(1)}, bf16[12,128,128]{2,1,0:T(8,128)(2,1)}, u32[]{:S(2)}) copy-start(bf16[12,128,128]{2,1,0:T(8,128)(2,1)} %shard_map.93.nat) | copy-start | bytes 1179652
  38.9 29.8 %copy-start.4 = (bf16[2,128,128]{2,1,0:T(8,128)(2,1)S(1)}, bf16[2,128,128]{2,1,0:T(8,128)(2,1)}, u32[]{:S(2)}) copy-start(bf16[2,128,128]{2,1,0:T(8,128)(2,1)} %copy-done.3) | copy-start | bytes 196612
  39.0 9.8 %collective-permute-start.7 = (bf16[12,128,128]{2,1,0:T(8,128)(2,1)S(1)}, bf16[12,128,128]{2,1,0:T(8,128)(2,1)S(1)}, u32[]{:S(2)}, u32[]{:S(2)}) collective-permute-start(bf16[12,128,128]{2,1,0:T(8,128)(2,1)S(1)} %collective-permute-done.swp), channel_id=1, source_target_pairs={{0,2},{2,4},{3,1},{4,6},{5,3},{7,5},{8,10},{10,12},{11,9},{12,14},... | collective-permute-start | bytes 1179656 | tf_op jit(solution)/shard_map/ppermute | solution.py:441
  51.5 44.4 %collective-permute-start.8 = (bf16[20,128,128]{2,1,0:T(8,128)(2,1)S(1)}, bf16[20,128,128]{2,1,0:T(8,128)(2,1)S(1)}, u32[]{:S(2)}, u32[]{:S(2)}) collective-permute-start(bf16[20,128,128]{2,1,0:T(8,128)(2,1)S(1)} %get-tuple-element.39), channel_id=1, source_target_pairs={{8,0},{9,1},{10,2},{11,3},{12,4},{13,5},{14,6},{15,7},{16,8},{17,9... | collective-permute-start | bytes 1966088 | tf_op jit(solution)/shard_map/ppermute | solution.py:441
  70.4 25.5 %collective-permute-start.11 = (bf16[8,128,128]{2,1,0:T(8,128)(2,1)S(1)}, bf16[8,128,128]{2,1,0:T(8,128)(2,1)S(1)}, u32[]{:S(2)}, u32[]{:S(2)}) collective-permute-start(bf16[8,128,128]{2,1,0:T(8,128)(2,1)S(1)} %get-tuple-element.44), channel_id=1, source_target_pairs={{0,8},{1,9},{2,10},{3,11},{4,12},{5,13},{6,14},{7,15},{8,16},{9,17... | collective-permute-start | bytes 786440 | tf_op jit(solution)/shard_map/ppermute | solution.py:441
  84.8 11.2 %collective-permute-start.9 = (bf16[4,128,128]{2,1,0:T(8,128)(2,1)S(1)}, bf16[4,128,128]{2,1,0:T(8,128)(2,1)S(1)}, u32[]{:S(2)}, u32[]{:S(2)}) collective-permute-start(bf16[4,128,128]{2,1,0:T(8,128)(2,1)S(1)} %get-tuple-element.40), channel_id=1, source_target_pairs={{8,2},{9,3},{10,4},{11,5},{12,6},{13,7},{16,10},{17,11},{18,12},{1... | collective-permute-start | bytes 393224 | tf_op jit(solution)/shard_map/ppermute | solution.py:441
  86.1 9.9 %collective-permute-start.10 = (bf16[4,128,128]{2,1,0:T(8,128)(2,1)S(1)}, bf16[4,128,128]{2,1,0:T(8,128)(2,1)S(1)}, u32[]{:S(2)}, u32[]{:S(2)}) collective-permute-start(bf16[4,128,128]{2,1,0:T(8,128)(2,1)S(1)} %get-tuple-element.41), channel_id=1, source_target_pairs={{10,0},{11,1},{12,2},{13,3},{14,4},{15,5},{18,8},{19,9},{20,10},{2... | collective-permute-start | bytes 393224 | tf_op jit(solution)/shard_map/ppermute | solution.py:441
  87.4 8.6 %collective-permute-start.12 = (bf16[2,128,128]{2,1,0:T(8,128)(2,1)S(1)}, bf16[2,128,128]{2,1,0:T(8,128)(2,1)S(1)}, u32[]{:S(2)}, u32[]{:S(2)}) collective-permute-start(bf16[2,128,128]{2,1,0:T(8,128)(2,1)S(1)} %get-tuple-element.45), channel_id=1, source_target_pairs={{0,10},{2,12},{3,9},{4,14},{5,11},{7,13},{8,18},{10,20},{11,17},{1... | collective-permute-start | bytes 196616 | tf_op jit(solution)/shard_map/ppermute | solution.py:441
  96.0 10.9 %copy-start.6 = (bf16[2,2,128,128]{3,2,1,0:T(8,128)(2,1)S(1)}, bf16[2,2,128,128]{3,2,1,0:T(8,128)(2,1)}, u32[]{:S(2)}) copy-start(bf16[2,2,128,128]{3,2,1,0:T(8,128)(2,1)} %copy-done.5) | copy-start | bytes 393220
  99.7 13.7 %collective-permute-start.13 = (bf16[4,256,128]{2,1,0:T(8,128)(2,1)S(1)}, bf16[4,256,128]{2,1,0:T(8,128)(2,1)S(1)}, u32[]{:S(2)}, u32[]{:S(2)}) collective-permute-start(bf16[4,256,128]{2,1,0:T(8,128)(2,1)S(1)} %get-tuple-element.55), channel_id=1, source_target_pairs={{8,0},{9,1},{10,2},{11,3},{12,4},{13,5},{14,6},{15,7},{16,8},{17,9... | collective-permute-start | bytes 786440 | tf_op jit(solution)/shard_map/ppermute | solution.py:441
  101.8 10.8 %all-to-all-start = ((bf16[4,80,128]{2,1,0:T(8,128)(2,1)}), bf16[4,80,128]{2,1,0:T(8,128)(2,1)S(1)}, u32[]{:S(2)}, u32[]{:S(2)}) async-start(bf16[4,80,128]{2,1,0:T(8,128)(2,1)} %get-tuple-element.59), calls=%async_computation | async-start | bytes 163840 | tf_op jit(solution)/shard_map/all_to_all | solution.py:540
  106.8 6.6 %copy-start.7 = (bf16[1,2,32,2,4,128]{5,4,3,2,1,0:T(4,128)(2,1)S(1)}, bf16[1,2,32,2,4,128]{5,4,3,2,1,0:T(4,128)(2,1)}, u32[]{:S(2)}) copy-start(bf16[1,2,32,2,4,128]{5,4,3,2,1,0:T(4,128)(2,1)} %get-tuple-element.66) | copy-start | bytes 393220

commit v6 on v5

--- a/solution.py
+++ b/solution.py
@@ -525,7 +525,7 @@
     fd2 = route(fd, fwd_diag)
     fm2 = route(fm, lambda s, yy, zz: (s + 1, yy, fwd_side(s, zz)))
 
-    bm2, bl2, bh2, fm2, fd2 = lax.optimization_barrier((bm2, bl2, bh2, fm2, fd2))
+    bm2, bl2, bh2, fd2 = lax.optimization_barrier((bm2, bl2, bh2, fd2))
     out_b, parts = call(
         functools.partial(tick2_back, scale),
         [((4, 2 * R, W), BF16), ((ny, slab_rows(slabs), W), BF16)],

time: 115 us -> 112 us (0.974)
  starting transfers between devices: 72.6 us -> 70.7 us
  waiting for transfers between devices: 10.4 us -> 9.08 us
    all_to_all x1, starting transfers between devices: 5.06 us -> 3.3 us  [local(): lax.all_to_all(parts, 'slab', 0, 0, axis_index_groups=columns, tiled=True)]
    ppermute x14, waiting for transfers between devices: 7.17 us -> 5.76 us  [route(): return lax.ppermute(value, ('segment', 'slab'), pairs)]
  transfers between devices with their start and end apart: 15 -> 15, of which waited for: 3 -> 3; matrix products, arithmetic and copies ran while one was open for 11% -> 11% of each run, Pallas kernels for 5% -> 9%
where the time goes in v6:
time: 112 us; the launch traced here: 111 us
  starting transfers between devices  70.7 us (63%)
  Pallas kernels  14.6 us (13%)
  local copies, waits for them, and re-layouts  12.8 us (11%)
  waiting for transfers between devices  9.08 us (8%)
  other arithmetic  2.79 us (2%)
    ppermute x14, starting transfers between devices, route(): return lax.ppermute(value, ('segment', 'slab'), pairs)  67.4 us
    pallas_call x7, Pallas kernels, call(): pl.pallas_call(kernel, out_shape=tuple((jax.ShapeDtypeStruct(s, t) for s,...  14.6 us
    unnamed x21, local copies, waits for them, and re-layouts  7.2 us
    ppermute x14, waiting for transfers between devices, route(): return lax.ppermute(value, ('segment', 'slab'), pairs)  5.76 us
    all_to_all x1, waiting for transfers between devices, local(): lax.all_to_all(parts, 'slab', 0, 0, axis_index_groups=columns, tiled=True)  3.32 us
    all_to_all x1, starting transfers between devices, local(): lax.all_to_all(parts, 'slab', 0, 0, axis_index_groups=columns, tiled=True)  3.3 us
  transfers between devices with their start and end apart: 15, of which 3 were waited for; matrix products, arithmetic and copies ran while one was open for 11% of the time, Pallas kernels for 9%

profile of v6, /device:TPU:6, one launch (start us, length us, event | category | flops | bytes accessed | tf_op | source)
XLA Modules:
  0.0 111.0 jit_solution(4800204333074609441)
XLA Ops:
  0.7 2.1 %shard_map.93.nat = bf16[12,128,128]{2,1,0:T(8,128)(2,1)} custom-call(bf16[2,256,128]{2,1,0:T(8,128)(2,1)} %bitcast.32, bf16[2,256,128]{2,1,0:T(8,128)(2,1)} %bitcast.33, bf16[2,256,128]{2,1,0:T(8,128)(2,1)} %bitcast.34), custom_call_target="tpu_custom_call" | custom-call | flops 100000000 | bytes 4000000 | tf_op jit(solution)/shard_map/pallas_call | solution.py:314
  2.8 15.7 %collective-permute-start = (bf16[12,128,128]{2,1,0:T(8,128)(2,1)}, bf16[12,128,128]{2,1,0:T(8,128)(2,1)S(1)}, u32[]{:S(2)}, u32[]{:S(2)}) collective-permute-start(bf16[12,128,128]{2,1,0:T(8,128)(2,1)} %shard_map.93.nat), channel_id=1, source_target_pairs={{0,1},{1,0},{2,3},{3,2},{4,5},{5,4},{6,7},{7,6},{8,9},{9,8},{10,11... | collective-permute-start | bytes 1179656 | tf_op jit(solution)/shard_map/ppermute | solution.py:441
  18.5 1.7 %fusion = (bf16[1,2,32,2,4,128]{5,4,3,2,1,0:T(4,128)(2,1)}, bf16[1,2,32,2,4,128]{5,4,3,2,1,0:T(4,128)(2,1)S(1)}) fusion(bf16[2,2,32,2,4,128]{5,4,3,2,1,0:T(4,128)(2,1)} %param.10), kind=kLoop, calls=%fused_computation.5 | loop fusion | bytes 524288 | tf_op jit(solution)/shard_map/slice | solution.py:557
  20.3 1.0 copy-done
  21.3 1.5 %shard_map.94 = (bf16[2,2,128,128]{3,2,1,0:T(8,128)(2,1)S(1)}, bf16[2,2,128,128]{3,2,1,0:T(8,128)(2,1)S(1)}, bf16[2,2,128,128]{3,2,1,0:T(8,128)(2,1)}, bf16[10,1...) custom-call(s32[7]{0:T(128)S(1)} %stack.73.flags, bf16[2,256,128]{2,1,0:T(8,128)(2,1)S(1)} %bitcast.26, ...), custom_call_target="tpu_custom_call" | custom-call | flops 100000000 | bytes 4000000 | tf_op jit(solution)/shard_map/pallas_call | solution.py:314
  23.4 1.3 %collective-permute-start.1 = (bf16[10,128,128]{2,1,0:T(8,128)(2,1)S(1)}, bf16[10,128,128]{2,1,0:T(8,128)(2,1)S(1)}, u32[]{:S(2)}, u32[]{:S(2)}) collective-permute-start(bf16[10,128,128]{2,1,0:T(8,128)(2,1)S(1)} %get-tuple-element.31), channel_id=1, source_target_pairs={{1,3},{2,0},{3,5},{4,2},{5,7},{6,4},{9,11},{10,8},{11,13},{12,10},... | collective-permute-start | bytes 983048 | tf_op jit(solution)/shard_map/ppermute | solution.py:441
  26.7 0.7 copy.12
  30.4 2.0 %maximum_bitcast_fusion = bf16[4,3,32,3,3,32]{2,0,1,4,3,5:T(4,128)(2,1)} fusion(bf16[2,32,32,3,3,3]{1,0,5,4,3,2:T(2,128)(2,1)S(1)} %reverse_bitcast_fusion, bf16[2,32,32,3,3,3]{1,0,5,4,3,2:T(2,128)(2,1)S(1)} %bitcast.28), kind=kLoop, calls=%fused_computation | loop fusion | flops 442368 | bytes 442368 | tf_op jit(solution)/shard_map/transpose | solution.py:415
  32.5 3.5 %copy.17 = bf16[4,3,32,3,3,32]{5,4,3,2,1,0:T(4,128)(2,1)} copy(bf16[4,3,32,3,3,32]{2,0,1,4,3,5:T(4,128)(2,1)} %maximum_bitcast_fusion) | data formatting | bytes 442368
  35.9 2.0 %pad.4.clone = bf16[4,3,32,3,4,32]{5,4,3,2,1,0:T(4,128)(2,1)S(1)} pad(bf16[4,3,32,3,3,32]{5,4,3,2,1,0:T(4,128)(2,1)} %copy.17, bf16[]{:T(256)} %constant.56.clone.1), padding=0_0x0_0x0_0x0_0x0_1x0_0 | pad | bytes 516098 | tf_op jit(solution)/shard_map/jit(_pad)/pad | solution.py:416
  39.0 4.6 %collective-permute-start.7 = (bf16[12,128,128]{2,1,0:T(8,128)(2,1)S(1)}, bf16[12,128,128]{2,1,0:T(8,128)(2,1)S(1)}, u32[]{:S(2)}, u32[]{:S(2)}) collective-permute-start(bf16[12,128,128]{2,1,0:T(8,128)(2,1)S(1)} %collective-permute-done.swp), channel_id=1, source_target_pairs={{0,2},{2,4},{3,1},{4,6},{5,3},{7,5},{8,10},{10,12},{11,9},{12,14},... | collective-permute-start | bytes 1179656 | tf_op jit(solution)/shard_map/ppermute | solution.py:441
  43.5 5.3 %collective-permute-done.7.far = bf16[12,128,128]{2,1,0:T(8,128)(2,1)S(1)} collective-permute-done((bf16[12,128,128]{2,1,0:T(8,128)(2,1)S(1)}, bf16[12,128,128]{2,1,0:T(8,128)(2,1)S(1)}, u32[]{:S(2)}, u32[]{:S(2)}) %collective-permute-start.7) | collective-permute-done | bytes 393248 | tf_op jit(solution)/shard_map/ppermute | solution.py:441
  48.8 2.7 %shard_map.97 = (bf16[20,128,128]{2,1,0:T(8,128)(2,1)S(1)}, bf16[4,128,128]{2,1,0:T(8,128)(2,1)S(1)}, bf16[4,128,128]{2,1,0:T(8,128)(2,1)S(1)}, f32[2,288,96]{2,1,0:T(8,128)S(1)}) custom-call(s32[7]{0:T(128)S(1)} %stack.73.flags, bf16[4,384,384]{2,1,0:T(8,128)(2,1)S(1)} %shard_map.95.w_ref, bf16[12,128,128]{2,1,0:T(8,128)(2,1)S(1)} %copy-done.1, ...), custom_call_target="tpu_custom_call" | custom-call | flops 2000000000 | bytes 4000000 | tf_op jit(solution)/shard_map/pallas_call | solution.py:314
  51.5 17.1 %collective-permute-start.9 = (bf16[20,128,128]{2,1,0:T(8,128)(2,1)S(1)}, bf16[20,128,128]{2,1,0:T(8,128)(2,1)S(1)}, u32[]{:S(2)}, u32[]{:S(2)}) collective-permute-start(bf16[20,128,128]{2,1,0:T(8,128)(2,1)S(1)} %get-tuple-element.41), channel_id=1, source_target_pairs={{8,0},{9,1},{10,2},{11,3},{12,4},{13,5},{14,6},{15,7},{16,8},{17,9... | collective-permute-start | bytes 1966088 | tf_op jit(solution)/shard_map/ppermute | solution.py:441
  68.7 4.6 %collective-permute-start.10 = (bf16[4,128,128]{2,1,0:T(8,128)(2,1)S(1)}, bf16[4,128,128]{2,1,0:T(8,128)(2,1)S(1)}, u32[]{:S(2)}, u32[]{:S(2)}) collective-permute-start(bf16[4,128,128]{2,1,0:T(8,128)(2,1)S(1)} %get-tuple-element.42), channel_id=1, source_target_pairs={{8,2},{9,3},{10,4},{11,5},{12,6},{13,7},{16,10},{17,11},{18,12},{1... | collective-permute-start | bytes 393224 | tf_op jit(solution)/shard_map/ppermute | solution.py:441
  73.3 1.3 %collective-permute-start.11 = (bf16[4,128,128]{2,1,0:T(8,128)(2,1)S(1)}, bf16[4,128,128]{2,1,0:T(8,128)(2,1)S(1)}, u32[]{:S(2)}, u32[]{:S(2)}) collective-permute-start(bf16[4,128,128]{2,1,0:T(8,128)(2,1)S(1)} %get-tuple-element.43), channel_id=1, source_target_pairs={{10,0},{11,1},{12,2},{13,3},{14,4},{15,5},{18,8},{19,9},{20,10},{2... | collective-permute-start | bytes 393224 | tf_op jit(solution)/shard_map/ppermute | solution.py:441
  74.6 1.7 %shard_map.96 = (bf16[8,128,128]{2,1,0:T(8,128)(2,1)S(1)}, bf16[2,128,128]{2,1,0:T(8,128)(2,1)S(1)}, bf16[18,128,128]{2,1,0:T(8,128)(2,1)S(1)}) custom-call(s32[7]{0:T(128)S(1)} %stack.73.flags, bf16[4,384,384]{2,1,0:T(8,128)(2,1)S(1)} %shard_map.95.w_ref, bf16[12,128,128]{2,1,0:T(8,128)(2,1)S(1)} %copy-done.1, ...), custom_call_target="tpu_custom_call" | custom-call | flops 1000000000 | bytes 4000000 | tf_op jit(solution)/shard_map/pallas_call | solution.py:314
  76.3 14.1 %collective-permute-start.12 = (bf16[2,128,128]{2,1,0:T(8,128)(2,1)S(1)}, bf16[2,128,128]{2,1,0:T(8,128)(2,1)S(1)}, u32[]{:S(2)}, u32[]{:S(2)}) collective-permute-start(bf16[2,128,128]{2,1,0:T(8,128)(2,1)S(1)} %get-tuple-element.44), channel_id=1, source_target_pairs={{0,10},{2,12},{3,9},{4,14},{5,11},{7,13},{8,18},{10,20},{11,17},{1... | collective-permute-start | bytes 196616 | tf_op jit(solution)/shard_map/ppermute | solution.py:441
  90.4 3.5 %collective-permute-start.8 = (bf16[8,128,128]{2,1,0:T(8,128)(2,1)S(1)}, bf16[8,128,128]{2,1,0:T(8,128)(2,1)S(1)}, u32[]{:S(2)}, u32[]{:S(2)}) collective-permute-start(bf16[8,128,128]{2,1,0:T(8,128)(2,1)S(1)} %get-tuple-element.40), channel_id=1, source_target_pairs={{0,8},{1,9},{2,10},{3,11},{4,12},{5,13},{6,14},{7,15},{8,16},{9,17... | collective-permute-start | bytes 786440 | tf_op jit(solution)/shard_map/ppermute | solution.py:441
  93.9 3.8 %shard_map.98 = (bf16[4,256,128]{2,1,0:T(8,128)(2,1)S(1)}, bf16[4,80,128]{2,1,0:T(8,128)(2,1)}) custom-call(s32[7]{0:T(128)S(1)} %stack.73.flags, bf16[4,384,384]{2,1,0:T(8,128)(2,1)S(1)} %shard_map.95.w_ref, bf16[20,128,128]{2,1,0:T(8,128)(2,1)S(1)} %collective-permute-done.9.bm, bf16[4,128,128]{2,1,0:T(8,128)(2,1)S(1)} %collective-permute-done.10.bl, ...), custom_call_target="tpu_custom_call" | custom-call | flops 1500000000 | bytes 4000000 | tf_op jit(solution)/shard_map/pallas_call | solution.py:314
  97.7 1.9 %collective-permute-start.13 = (bf16[4,256,128]{2,1,0:T(8,128)(2,1)S(1)}, bf16[4,256,128]{2,1,0:T(8,128)(2,1)S(1)}, u32[]{:S(2)}, u32[]{:S(2)}) collective-permute-start(bf16[4,256,128]{2,1,0:T(8,128)(2,1)S(1)} %get-tuple-element.53), channel_id=1, source_target_pairs={{8,0},{9,1},{10,2},{11,3},{12,4},{13,5},{14,6},{15,7},{16,8},{17,9... | collective-permute-start | bytes 786440 | tf_op jit(solution)/shard_map/ppermute | solution.py:441
  100.2 3.3 %all-to-all-start = ((bf16[4,80,128]{2,1,0:T(8,128)(2,1)}), bf16[4,80,128]{2,1,0:T(8,128)(2,1)S(1)}, u32[]{:S(2)}, u32[]{:S(2)}) async-start(bf16[4,80,128]{2,1,0:T(8,128)(2,1)} %get-tuple-element.57), calls=%async_computation | async-start | bytes 163840 | tf_op jit(solution)/shard_map/all_to_all | solution.py:540
  103.5 2.5 %shard_map.99 = bf16[2,256,128]{2,1,0:T(8,128)(2,1)} custom-call(s32[5]{0:T(128)S(1)} %stack.65.flags, bf16[4,384,384]{2,1,0:T(8,128)(2,1)S(1)} %shard_map.95.w_ref, bf16[8,128,128]{2,1,0:T(8,128)(2,1)S(1)} %collective-permute-done.8.fm, bf16[2,128,128]{2,1,0:T(8,128)(2,1)S(1)} %collective-permute-done.12.fd, ...), custom_call_target="tpu_custom_call" | custom-call | flops 700000000 | bytes 4000000 | tf_op jit(solution)/shard_map/pallas_call | solution.py:314
  106.0 3.3 %all-to-all-done = bf16[4,80,128]{2,1,0:T(8,128)(2,1)S(1)} async-done(((bf16[4,80,128]{2,1,0:T(8,128)(2,1)}), bf16[4,80,128]{2,1,0:T(8,128)(2,1)S(1)}, u32[]{:S(2)}, u32[]{:S(2)}) %all-to-all-start) | async-done | bytes 81952 | tf_op jit(solution)/shard_map/all_to_all | solution.py:540
  (47 shorter events, 8.8 us)
Async XLA Ops:
  0.6 19.7 %copy-start.2 = (bf16[2,32,2,4,128]{4,3,2,1,0:T(4,128)(2,1)S(1)}, bf16[2,32,2,4,128]{4,3,2,1,0:T(4,128)(2,1)}, u32[]{:S(2)}) copy-start(bf16[2,32,2,4,128]{4,3,2,1,0:T(4,128)(2,1)} %param.9) | copy-start | bytes 393220
  0.6 26.1 %copy-start.8 = (bf16[1,2,32,864]{3,2,1,0:T(8,128)(2,1)S(1)}, bf16[1,2,32,864]{3,2,1,0:T(8,128)(2,1)}, u32[]{:S(2)}) copy-start(bf16[1,2,32,864]{3,2,1,0:T(8,128)(2,1)} %param.11) | copy-start | bytes 331780
  2.8 36.2 %collective-permute-start = (bf16[12,128,128]{2,1,0:T(8,128)(2,1)}, bf16[12,128,128]{2,1,0:T(8,128)(2,1)S(1)}, u32[]{:S(2)}, u32[]{:S(2)}) collective-permute-start(bf16[12,128,128]{2,1,0:T(8,128)(2,1)} %shard_map.93.nat), channel_id=1, source_target_pairs={{0,1},{1,0},{2,3},{3,2},{4,5},{5,4},{6,7},{7,6},{8,9},{9,8},{10,11... | collective-permute-start | bytes 1179656 | tf_op jit(solution)/shard_map/ppermute | solution.py:441
  20.3 1.0 copy-start
  22.8 0.7 copy-start.5
  23.4 15.5 %collective-permute-start.1 = (bf16[10,128,128]{2,1,0:T(8,128)(2,1)S(1)}, bf16[10,128,128]{2,1,0:T(8,128)(2,1)S(1)}, u32[]{:S(2)}, u32[]{:S(2)}) collective-permute-start(bf16[10,128,128]{2,1,0:T(8,128)(2,1)S(1)} %get-tuple-element.31), channel_id=1, source_target_pairs={{1,3},{2,0},{3,5},{4,2},{5,7},{6,4},{9,11},{10,8},{11,13},{12,10},... | collective-permute-start | bytes 983048 | tf_op jit(solution)/shard_map/ppermute | solution.py:441
  24.7 3.7 %collective-permute-start.6 = (bf16[2,128,128]{2,1,0:T(8,128)(2,1)S(1)}, bf16[2,128,128]{2,1,0:T(8,128)(2,1)S(1)}, u32[]{:S(2)}, u32[]{:S(2)}) collective-permute-start(bf16[2,128,128]{2,1,0:T(8,128)(2,1)S(1)} %get-tuple-element.34), channel_id=1, source_target_pairs={{504,507},{506,509},{507,504},{508,511},{509,506},{511,508}} | collective-permute-start | bytes 196616 | tf_op jit(solution)/shard_map/ppermute | solution.py:441
  25.4 3.8 %collective-permute-start.5 = (bf16[2,128,128]{2,1,0:T(8,128)(2,1)S(1)}, bf16[2,128,128]{2,1,0:T(8,128)(2,1)S(1)}, u32[]{:S(2)}, u32[]{:S(2)}) collective-permute-start(bf16[2,128,128]{2,1,0:T(8,128)(2,1)S(1)} %get-tuple-element.34), channel_id=1, source_target_pairs={{504,506},{506,508},{507,505},{508,510},{509,507},{511,509}} | collective-permute-start | bytes 196616 | tf_op jit(solution)/shard_map/ppermute | solution.py:441
  26.1 12.8 %collective-permute-start.3 = (bf16[2,2,128,128]{3,2,1,0:T(8,128)(2,1)}, bf16[2,2,128,128]{3,2,1,0:T(8,128)(2,1)S(1)}, u32[]{:S(2)}, u32[]{:S(2)}) collective-permute-start(bf16[2,2,128,128]{3,2,1,0:T(8,128)(2,1)} %get-tuple-element.32), channel_id=1, source_target_pairs={{113,2},{114,1},{115,4},{116,3},{117,6},{118,5},{393,506},{394,505... | collective-permute-start | bytes 393224 | tf_op jit(solution)/shard_map/ppermute | solution.py:441
  28.5 10.5 %collective-permute-start.2 = (bf16[2,2,128,128]{3,2,1,0:T(8,128)(2,1)}, bf16[2,2,128,128]{3,2,1,0:T(8,128)(2,1)S(1)}, u32[]{:S(2)}, u32[]{:S(2)}) collective-permute-start(bf16[2,2,128,128]{3,2,1,0:T(8,128)(2,1)} %get-tuple-element.32), channel_id=1, source_target_pairs={{112,1},{113,0},{114,3},{115,2},{116,5},{117,4},{118,7},{119,6},{3... | collective-permute-start | bytes 393224 | tf_op jit(solution)/shard_map/ppermute | solution.py:441
  29.1 0.6 copy-start.3
  29.8 9.2 %collective-permute-start.4 = (bf16[2,2,128,128]{3,2,1,0:T(8,128)(2,1)S(1)}, bf16[2,2,128,128]{3,2,1,0:T(8,128)(2,1)S(1)}, u32[]{:S(2)}, u32[]{:S(2)}) collective-permute-start(bf16[2,2,128,128]{3,2,1,0:T(8,128)(2,1)S(1)} %get-tuple-element.33.last_own), channel_id=1, source_target_pairs={{497,507},{498,504},{499,509},{500,506},{501,511},{502,508}} | collective-permute-start | bytes 393224 | tf_op jit(solution)/shard_map/ppermute | solution.py:441
  37.9 10.9 %copy-start.1 = (bf16[12,128,128]{2,1,0:T(8,128)(2,1)S(1)}, bf16[12,128,128]{2,1,0:T(8,128)(2,1)}, u32[]{:S(2)}) copy-start(bf16[12,128,128]{2,1,0:T(8,128)(2,1)} %shard_map.93.nat) | copy-start | bytes 1179652
  38.9 35.7 %copy-start.4 = (bf16[2,128,128]{2,1,0:T(8,128)(2,1)S(1)}, bf16[2,128,128]{2,1,0:T(8,128)(2,1)}, u32[]{:S(2)}) copy-start(bf16[2,128,128]{2,1,0:T(8,128)(2,1)} %copy-done.3) | copy-start | bytes 196612
  39.0 9.8 %collective-permute-start.7 = (bf16[12,128,128]{2,1,0:T(8,128)(2,1)S(1)}, bf16[12,128,128]{2,1,0:T(8,128)(2,1)S(1)}, u32[]{:S(2)}, u32[]{:S(2)}) collective-permute-start(bf16[12,128,128]{2,1,0:T(8,128)(2,1)S(1)} %collective-permute-done.swp), channel_id=1, source_target_pairs={{0,2},{2,4},{3,1},{4,6},{5,3},{7,5},{8,10},{10,12},{11,9},{12,14},... | collective-permute-start | bytes 1179656 | tf_op jit(solution)/shard_map/ppermute | solution.py:441
  51.5 42.4 %collective-permute-start.9 = (bf16[20,128,128]{2,1,0:T(8,128)(2,1)S(1)}, bf16[20,128,128]{2,1,0:T(8,128)(2,1)S(1)}, u32[]{:S(2)}, u32[]{:S(2)}) collective-permute-start(bf16[20,128,128]{2,1,0:T(8,128)(2,1)S(1)} %get-tuple-element.41), channel_id=1, source_target_pairs={{8,0},{9,1},{10,2},{11,3},{12,4},{13,5},{14,6},{15,7},{16,8},{17,9... | collective-permute-start | bytes 1966088 | tf_op jit(solution)/shard_map/ppermute | solution.py:441
  68.7 25.2 %collective-permute-start.10 = (bf16[4,128,128]{2,1,0:T(8,128)(2,1)S(1)}, bf16[4,128,128]{2,1,0:T(8,128)(2,1)S(1)}, u32[]{:S(2)}, u32[]{:S(2)}) collective-permute-start(bf16[4,128,128]{2,1,0:T(8,128)(2,1)S(1)} %get-tuple-element.42), channel_id=1, source_target_pairs={{8,2},{9,3},{10,4},{11,5},{12,6},{13,7},{16,10},{17,11},{18,12},{1... | collective-permute-start | bytes 393224 | tf_op jit(solution)/shard_map/ppermute | solution.py:441
  73.3 20.6 %collective-permute-start.11 = (bf16[4,128,128]{2,1,0:T(8,128)(2,1)S(1)}, bf16[4,128,128]{2,1,0:T(8,128)(2,1)S(1)}, u32[]{:S(2)}, u32[]{:S(2)}) collective-permute-start(bf16[4,128,128]{2,1,0:T(8,128)(2,1)S(1)} %get-tuple-element.43), channel_id=1, source_target_pairs={{10,0},{11,1},{12,2},{13,3},{14,4},{15,5},{18,8},{19,9},{20,10},{2... | collective-permute-start | bytes 393224 | tf_op jit(solution)/shard_map/ppermute | solution.py:441
  76.3 17.6 %collective-permute-start.12 = (bf16[2,128,128]{2,1,0:T(8,128)(2,1)S(1)}, bf16[2,128,128]{2,1,0:T(8,128)(2,1)S(1)}, u32[]{:S(2)}, u32[]{:S(2)}) collective-permute-start(bf16[2,128,128]{2,1,0:T(8,128)(2,1)S(1)} %get-tuple-element.44), channel_id=1, source_target_pairs={{0,10},{2,12},{3,9},{4,14},{5,11},{7,13},{8,18},{10,20},{11,17},{1... | collective-permute-start | bytes 196616 | tf_op jit(solution)/shard_map/ppermute | solution.py:441
  90.4 9.8 %collective-permute-start.8 = (bf16[8,128,128]{2,1,0:T(8,128)(2,1)S(1)}, bf16[8,128,128]{2,1,0:T(8,128)(2,1)S(1)}, u32[]{:S(2)}, u32[]{:S(2)}) collective-permute-start(bf16[8,128,128]{2,1,0:T(8,128)(2,1)S(1)} %get-tuple-element.40), channel_id=1, source_target_pairs={{0,8},{1,9},{2,10},{3,11},{4,12},{5,13},{6,14},{7,15},{8,16},{9,17... | collective-permute-start | bytes 786440 | tf_op jit(solution)/shard_map/ppermute | solution.py:441
  93.9 9.6 %copy-start.6 = (bf16[2,2,128,128]{3,2,1,0:T(8,128)(2,1)S(1)}, bf16[2,2,128,128]{3,2,1,0:T(8,128)(2,1)}, u32[]{:S(2)}) copy-start(bf16[2,2,128,128]{3,2,1,0:T(8,128)(2,1)} %copy-done.5) | copy-start | bytes 393220
  97.7 12.5 %collective-permute-start.13 = (bf16[4,256,128]{2,1,0:T(8,128)(2,1)S(1)}, bf16[4,256,128]{2,1,0:T(8,128)(2,1)S(1)}, u32[]{:S(2)}, u32[]{:S(2)}) collective-permute-start(bf16[4,256,128]{2,1,0:T(8,128)(2,1)S(1)} %get-tuple-element.53), channel_id=1, source_target_pairs={{8,0},{9,1},{10,2},{11,3},{12,4},{13,5},{14,6},{15,7},{16,8},{17,9... | collective-permute-start | bytes 786440 | tf_op jit(solution)/shard_map/ppermute | solution.py:441
  100.2 9.1 %all-to-all-start = ((bf16[4,80,128]{2,1,0:T(8,128)(2,1)}), bf16[4,80,128]{2,1,0:T(8,128)(2,1)S(1)}, u32[]{:S(2)}, u32[]{:S(2)}) async-start(bf16[4,80,128]{2,1,0:T(8,128)(2,1)} %get-tuple-element.57), calls=%async_computation | async-start | bytes 163840 | tf_op jit(solution)/shard_map/all_to_all | solution.py:540
  103.5 6.7 %copy-start.7 = (bf16[1,2,32,2,4,128]{5,4,3,2,1,0:T(4,128)(2,1)S(1)}, bf16[1,2,32,2,4,128]{5,4,3,2,1,0:T(4,128)(2,1)}, u32[]{:S(2)}) copy-start(bf16[1,2,32,2,4,128]{5,4,3,2,1,0:T(4,128)(2,1)} %get-tuple-element.64) | copy-start | bytes 393220

commit v7 on v6

--- a/solution.py
+++ b/solution.py
@@ -525,7 +525,7 @@
     fd2 = route(fd, fwd_diag)
     fm2 = route(fm, lambda s, yy, zz: (s + 1, yy, fwd_side(s, zz)))
 
-    bm2, bl2, bh2, fd2 = lax.optimization_barrier((bm2, bl2, bh2, fd2))
+    bm2, bl2, bh2 = lax.optimization_barrier((bm2, bl2, bh2))
     out_b, parts = call(
         functools.partial(tick2_back, scale),
         [((4, 2 * R, W), BF16), ((ny, slab_rows(slabs), W), BF16)],

time: 112 us -> 113 us (level)
  starting transfers between devices: 70.7 us -> 72.1 us
  waiting for transfers between devices: 9.08 us -> 10.4 us
  local copies, waits for them, and re-layouts: 12.8 us -> 11.6 us
    ppermute x14, waiting for transfers between devices: 5.76 us -> 7.27 us  [route(): return lax.ppermute(value, ('segment', 'slab'), pairs)]
    ppermute x14, starting transfers between devices: 67.4 us -> 68.8 us  [route(): return lax.ppermute(value, ('segment', 'slab'), pairs)]
    unnamed x21, local copies, waits for them, and re-layouts: 7.2 us -> 5.95 us
  transfers between devices with their start and end apart: 15 -> 15, of which waited for: 3 -> 3; matrix products, arithmetic and copies ran while one was open for 11% -> 9% of each run, Pallas kernels for 9% -> 9%
where the time goes in v7:
time: 113 us; the launch traced here: 112 us
  starting transfers between devices  72.1 us (64%)
  Pallas kernels  14.5 us (13%)
  local copies, waits for them, and re-layouts  11.6 us (10%)
  waiting for transfers between devices  10.4 us (9%)
  other arithmetic  1.89 us (2%)
    ppermute x14, starting transfers between devices, route(): return lax.ppermute(value, ('segment', 'slab'), pairs)  68.8 us
    pallas_call x7, Pallas kernels, call(): pl.pallas_call(kernel, out_shape=tuple((jax.ShapeDtypeStruct(s, t) for s,...  14.5 us
    ppermute x14, waiting for transfers between devices, route(): return lax.ppermute(value, ('segment', 'slab'), pairs)  7.27 us
    unnamed x21, local copies, waits for them, and re-layouts  5.95 us
    all_to_all x1, starting transfers between devices, local(): lax.all_to_all(parts, 'slab', 0, 0, axis_index_groups=columns, tiled=True)  3.3 us
    all_to_all x1, waiting for transfers between devices, local(): lax.all_to_all(parts, 'slab', 0, 0, axis_index_groups=columns, tiled=True)  3.17 us
  transfers between devices with their start and end apart: 15, of which 3 were waited for; matrix products, arithmetic and copies ran while one was open for 9% of the time, Pallas kernels for 9%

profile of v7, /device:TPU:6, one launch (start us, length us, event | category | flops | bytes accessed | tf_op | source)
XLA Modules:
  0.0 111.6 jit_solution(5467206212906025066)
XLA Ops:
  0.7 2.1 %shard_map.93.nat = bf16[12,128,128]{2,1,0:T(8,128)(2,1)} custom-call(bf16[2,256,128]{2,1,0:T(8,128)(2,1)} %bitcast.32, bf16[2,256,128]{2,1,0:T(8,128)(2,1)} %bitcast.33, bf16[2,256,128]{2,1,0:T(8,128)(2,1)} %bitcast.34), custom_call_target="tpu_custom_call" | custom-call | flops 100000000 | bytes 4000000 | tf_op jit(solution)/shard_map/pallas_call | solution.py:314
  2.8 15.7 %collective-permute-start = (bf16[12,128,128]{2,1,0:T(8,128)(2,1)}, bf16[12,128,128]{2,1,0:T(8,128)(2,1)S(1)}, u32[]{:S(2)}, u32[]{:S(2)}) collective-permute-start(bf16[12,128,128]{2,1,0:T(8,128)(2,1)} %shard_map.93.nat), channel_id=1, source_target_pairs={{0,1},{1,0},{2,3},{3,2},{4,5},{5,4},{6,7},{7,6},{8,9},{9,8},{10,11... | collective-permute-start | bytes 1179656 | tf_op jit(solution)/shard_map/ppermute | solution.py:441
  18.5 1.7 %fusion = (bf16[1,2,32,2,4,128]{5,4,3,2,1,0:T(4,128)(2,1)}, bf16[1,2,32,2,4,128]{5,4,3,2,1,0:T(4,128)(2,1)S(1)}) fusion(bf16[2,2,32,2,4,128]{5,4,3,2,1,0:T(4,128)(2,1)} %param.10), kind=kLoop, calls=%fused_computation.5 | loop fusion | bytes 524288 | tf_op jit(solution)/shard_map/slice | solution.py:557
  20.3 1.0 copy-done
  21.3 1.5 %shard_map.94 = (bf16[2,2,128,128]{3,2,1,0:T(8,128)(2,1)S(1)}, bf16[2,2,128,128]{3,2,1,0:T(8,128)(2,1)S(1)}, bf16[2,2,128,128]{3,2,1,0:T(8,128)(2,1)}, bf16[10,1...) custom-call(s32[7]{0:T(128)S(1)} %stack.73.flags, bf16[2,256,128]{2,1,0:T(8,128)(2,1)S(1)} %bitcast.26, ...), custom_call_target="tpu_custom_call" | custom-call | flops 100000000 | bytes 4000000 | tf_op jit(solution)/shard_map/pallas_call | solution.py:314
  23.4 1.3 %collective-permute-start.1 = (bf16[10,128,128]{2,1,0:T(8,128)(2,1)S(1)}, bf16[10,128,128]{2,1,0:T(8,128)(2,1)S(1)}, u32[]{:S(2)}, u32[]{:S(2)}) collective-permute-start(bf16[10,128,128]{2,1,0:T(8,128)(2,1)S(1)} %get-tuple-element.30), channel_id=1, source_target_pairs={{1,3},{2,0},{3,5},{4,2},{5,7},{6,4},{9,11},{10,8},{11,13},{12,10},... | collective-permute-start | bytes 983048 | tf_op jit(solution)/shard_map/ppermute | solution.py:441
  30.4 1.1 %maximum_bitcast_fusion = bf16[4,3,32,3,3,32]{2,0,1,4,3,5:T(4,128)(2,1)S(1)} fusion(bf16[2,32,32,3,3,3]{1,0,5,4,3,2:T(2,128)(2,1)S(1)} %reverse_bitcast_fusion, bf16[2,32,32,3,3,3]{1,0,5,4,3,2:T(2,128)(2,1)S(1)} %bitcast.28), kind=kLoop, calls=%fused_computation | loop fusion | flops 442368 | bytes 442368 | tf_op jit(solution)/shard_map/transpose | solution.py:415
  31.6 2.2 %copy.17 = bf16[4,3,32,3,3,32]{5,4,3,2,1,0:T(4,128)(2,1)} copy(bf16[4,3,32,3,3,32]{2,0,1,4,3,5:T(4,128)(2,1)S(1)} %maximum_bitcast_fusion) | data formatting | bytes 442368
  33.8 2.0 %pad.4.clone = bf16[4,3,32,3,4,32]{5,4,3,2,1,0:T(4,128)(2,1)S(1)} pad(bf16[4,3,32,3,3,32]{5,4,3,2,1,0:T(4,128)(2,1)} %copy.17, bf16[]{:T(256)} %constant.56.clone.1), padding=0_0x0_0x0_0x0_0x0_1x0_0 | pad | bytes 516098 | tf_op jit(solution)/shard_map/jit(_pad)/pad | solution.py:416
  36.8 4.6 %collective-permute-start.7 = (bf16[12,128,128]{2,1,0:T(8,128)(2,1)S(1)}, bf16[12,128,128]{2,1,0:T(8,128)(2,1)S(1)}, u32[]{:S(2)}, u32[]{:S(2)}) collective-permute-start(bf16[12,128,128]{2,1,0:T(8,128)(2,1)S(1)} %collective-permute-done.swp), channel_id=1, source_target_pairs={{0,2},{2,4},{3,1},{4,6},{5,3},{7,5},{8,10},{10,12},{11,9},{12,14},... | collective-permute-start | bytes 1179656 | tf_op jit(solution)/shard_map/ppermute | solution.py:441
  41.4 5.3 %collective-permute-done.7.far = bf16[12,128,128]{2,1,0:T(8,128)(2,1)S(1)} collective-permute-done((bf16[12,128,128]{2,1,0:T(8,128)(2,1)S(1)}, bf16[12,128,128]{2,1,0:T(8,128)(2,1)S(1)}, u32[]{:S(2)}, u32[]{:S(2)}) %collective-permute-start.7) | collective-permute-done | bytes 393248 | tf_op jit(solution)/shard_map/ppermute | solution.py:441
  46.7 2.7 %shard_map.97 = (bf16[20,128,128]{2,1,0:T(8,128)(2,1)S(1)}, bf16[4,128,128]{2,1,0:T(8,128)(2,1)S(1)}, bf16[4,128,128]{2,1,0:T(8,128)(2,1)S(1)}, f32[2,288,96]{2,1,0:T(8,128)S(1)}) custom-call(s32[7]{0:T(128)S(1)} %stack.73.flags, bf16[4,384,384]{2,1,0:T(8,128)(2,1)S(1)} %shard_map.95.w_ref, bf16[12,128,128]{2,1,0:T(8,128)(2,1)S(1)} %copy-done.1, ...), custom_call_target="tpu_custom_call" | custom-call | flops 2000000000 | bytes 4000000 | tf_op jit(solution)/shard_map/pallas_call | solution.py:314
  49.4 19.3 %collective-permute-start.9 = (bf16[20,128,128]{2,1,0:T(8,128)(2,1)S(1)}, bf16[20,128,128]{2,1,0:T(8,128)(2,1)S(1)}, u32[]{:S(2)}, u32[]{:S(2)}) collective-permute-start(bf16[20,128,128]{2,1,0:T(8,128)(2,1)S(1)} %get-tuple-element.40), channel_id=1, source_target_pairs={{8,0},{9,1},{10,2},{11,3},{12,4},{13,5},{14,6},{15,7},{16,8},{17,9... | collective-permute-start | bytes 1966088 | tf_op jit(solution)/shard_map/ppermute | solution.py:441
  68.6 4.6 %collective-permute-start.10 = (bf16[4,128,128]{2,1,0:T(8,128)(2,1)S(1)}, bf16[4,128,128]{2,1,0:T(8,128)(2,1)S(1)}, u32[]{:S(2)}, u32[]{:S(2)}) collective-permute-start(bf16[4,128,128]{2,1,0:T(8,128)(2,1)S(1)} %get-tuple-element.41), channel_id=1, source_target_pairs={{8,2},{9,3},{10,4},{11,5},{12,6},{13,7},{16,10},{17,11},{18,12},{1... | collective-permute-start | bytes 393224 | tf_op jit(solution)/shard_map/ppermute | solution.py:441
  73.3 1.3 %collective-permute-start.11 = (bf16[4,128,128]{2,1,0:T(8,128)(2,1)S(1)}, bf16[4,128,128]{2,1,0:T(8,128)(2,1)S(1)}, u32[]{:S(2)}, u32[]{:S(2)}) collective-permute-start(bf16[4,128,128]{2,1,0:T(8,128)(2,1)S(1)} %get-tuple-element.42), channel_id=1, source_target_pairs={{10,0},{11,1},{12,2},{13,3},{14,4},{15,5},{18,8},{19,9},{20,10},{2... | collective-permute-start | bytes 393224 | tf_op jit(solution)/shard_map/ppermute | solution.py:441
  74.6 1.7 %shard_map.96 = (bf16[8,128,128]{2,1,0:T(8,128)(2,1)S(1)}, bf16[2,128,128]{2,1,0:T(8,128)(2,1)S(1)}, bf16[18,128,128]{2,1,0:T(8,128)(2,1)S(1)}) custom-call(s32[7]{0:T(128)S(1)} %stack.73.flags, bf16[4,384,384]{2,1,0:T(8,128)(2,1)S(1)} %shard_map.95.w_ref, bf16[12,128,128]{2,1,0:T(8,128)(2,1)S(1)} %copy-done.1, ...), custom_call_target="tpu_custom_call" | custom-call | flops 1000000000 | bytes 4000000 | tf_op jit(solution)/shard_map/pallas_call | solution.py:314
  76.3 8.9 %collective-permute-start.8 = (bf16[8,128,128]{2,1,0:T(8,128)(2,1)S(1)}, bf16[8,128,128]{2,1,0:T(8,128)(2,1)S(1)}, u32[]{:S(2)}, u32[]{:S(2)}) collective-permute-start(bf16[8,128,128]{2,1,0:T(8,128)(2,1)S(1)} %get-tuple-element.39), channel_id=1, source_target_pairs={{0,8},{1,9},{2,10},{3,11},{4,12},{5,13},{6,14},{7,15},{8,16},{9,17... | collective-permute-start | bytes 786440 | tf_op jit(solution)/shard_map/ppermute | solution.py:441
  85.2 2.0 %collective-permute-done.11.bh = bf16[4,128,128]{2,1,0:T(8,128)(2,1)S(1)} collective-permute-done((bf16[4,128,128]{2,1,0:T(8,128)(2,1)S(1)}, bf16[4,128,128]{2,1,0:T(8,128)(2,1)S(1)}, u32[]{:S(2)}, u32[]{:S(2)}) %collective-permute-start.11) | collective-permute-done | bytes 131104 | tf_op jit(solution)/shard_map/ppermute | solution.py:441
  87.2 3.7 %shard_map.98 = (bf16[4,256,128]{2,1,0:T(8,128)(2,1)S(1)}, bf16[4,80,128]{2,1,0:T(8,128)(2,1)}) custom-call(s32[7]{0:T(128)S(1)} %stack.73.flags, bf16[4,384,384]{2,1,0:T(8,128)(2,1)S(1)} %shard_map.95.w_ref, bf16[20,128,128]{2,1,0:T(8,128)(2,1)S(1)} %collective-permute-done.9.bm, bf16[4,128,128]{2,1,0:T(8,128)(2,1)S(1)} %collective-permute-done.10.bl, ...), custom_call_target="tpu_custom_call" | custom-call | flops 1500000000 | bytes 4000000 | tf_op jit(solution)/shard_map/pallas_call | solution.py:314
  90.9 3.7 %collective-permute-start.13 = (bf16[4,256,128]{2,1,0:T(8,128)(2,1)S(1)}, bf16[4,256,128]{2,1,0:T(8,128)(2,1)S(1)}, u32[]{:S(2)}, u32[]{:S(2)}) collective-permute-start(bf16[4,256,128]{2,1,0:T(8,128)(2,1)S(1)} %get-tuple-element.51), channel_id=1, source_target_pairs={{8,0},{9,1},{10,2},{11,3},{12,4},{13,5},{14,6},{15,7},{16,8},{17,9... | collective-permute-start | bytes 786440 | tf_op jit(solution)/shard_map/ppermute | solution.py:441
  94.6 6.2 %collective-permute-start.12 = (bf16[2,128,128]{2,1,0:T(8,128)(2,1)S(1)}, bf16[2,128,128]{2,1,0:T(8,128)(2,1)S(1)}, u32[]{:S(2)}, u32[]{:S(2)}) collective-permute-start(bf16[2,128,128]{2,1,0:T(8,128)(2,1)S(1)} %get-tuple-element.53), channel_id=1, source_target_pairs={{0,10},{2,12},{3,9},{4,14},{5,11},{7,13},{8,18},{10,20},{11,17},{1... | collective-permute-start | bytes 196616 | tf_op jit(solution)/shard_map/ppermute | solution.py:441
  100.9 3.3 %all-to-all-start = ((bf16[4,80,128]{2,1,0:T(8,128)(2,1)}), bf16[4,80,128]{2,1,0:T(8,128)(2,1)S(1)}, u32[]{:S(2)}, u32[]{:S(2)}) async-start(bf16[4,80,128]{2,1,0:T(8,128)(2,1)} %get-tuple-element.55), calls=%async_computation | async-start | bytes 163840 | tf_op jit(solution)/shard_map/all_to_all | solution.py:540
  104.3 2.5 %shard_map.99 = bf16[2,256,128]{2,1,0:T(8,128)(2,1)} custom-call(s32[5]{0:T(128)S(1)} %stack.65.flags, bf16[4,384,384]{2,1,0:T(8,128)(2,1)S(1)} %shard_map.95.w_ref, bf16[8,128,128]{2,1,0:T(8,128)(2,1)S(1)} %collective-permute-done.8.fm, bf16[2,128,128]{2,1,0:T(8,128)(2,1)S(1)} %collective-permute-done.12.fd, ...), custom_call_target="tpu_custom_call" | custom-call | flops 700000000 | bytes 4000000 | tf_op jit(solution)/shard_map/pallas_call | solution.py:314
  106.7 3.2 %all-to-all-done = bf16[4,80,128]{2,1,0:T(8,128)(2,1)S(1)} async-done(((bf16[4,80,128]{2,1,0:T(8,128)(2,1)}), bf16[4,80,128]{2,1,0:T(8,128)(2,1)S(1)}, u32[]{:S(2)}, u32[]{:S(2)}) %all-to-all-start) | async-done | bytes 81952 | tf_op jit(solution)/shard_map/all_to_all | solution.py:540
  (47 shorter events, 9.1 us)
Async XLA Ops:
  0.6 19.7 %copy-start.2 = (bf16[2,32,2,4,128]{4,3,2,1,0:T(4,128)(2,1)S(1)}, bf16[2,32,2,4,128]{4,3,2,1,0:T(4,128)(2,1)}, u32[]{:S(2)}) copy-start(bf16[2,32,2,4,128]{4,3,2,1,0:T(4,128)(2,1)} %param.9) | copy-start | bytes 393220
  0.6 26.1 %copy-start.8 = (bf16[1,2,32,864]{3,2,1,0:T(8,128)(2,1)S(1)}, bf16[1,2,32,864]{3,2,1,0:T(8,128)(2,1)}, u32[]{:S(2)}) copy-start(bf16[1,2,32,864]{3,2,1,0:T(8,128)(2,1)} %param.11) | copy-start | bytes 331780
  2.8 34.0 %collective-permute-start = (bf16[12,128,128]{2,1,0:T(8,128)(2,1)}, bf16[12,128,128]{2,1,0:T(8,128)(2,1)S(1)}, u32[]{:S(2)}, u32[]{:S(2)}) collective-permute-start(bf16[12,128,128]{2,1,0:T(8,128)(2,1)} %shard_map.93.nat), channel_id=1, source_target_pairs={{0,1},{1,0},{2,3},{3,2},{4,5},{5,4},{6,7},{7,6},{8,9},{9,8},{10,11... | collective-permute-start | bytes 1179656 | tf_op jit(solution)/shard_map/ppermute | solution.py:441
  20.3 1.0 copy-start
  22.8 0.7 copy-start.5
  23.4 13.4 %collective-permute-start.1 = (bf16[10,128,128]{2,1,0:T(8,128)(2,1)S(1)}, bf16[10,128,128]{2,1,0:T(8,128)(2,1)S(1)}, u32[]{:S(2)}, u32[]{:S(2)}) collective-permute-start(bf16[10,128,128]{2,1,0:T(8,128)(2,1)S(1)} %get-tuple-element.30), channel_id=1, source_target_pairs={{1,3},{2,0},{3,5},{4,2},{5,7},{6,4},{9,11},{10,8},{11,13},{12,10},... | collective-permute-start | bytes 983048 | tf_op jit(solution)/shard_map/ppermute | solution.py:441
  24.7 3.7 %collective-permute-start.6 = (bf16[2,128,128]{2,1,0:T(8,128)(2,1)S(1)}, bf16[2,128,128]{2,1,0:T(8,128)(2,1)S(1)}, u32[]{:S(2)}, u32[]{:S(2)}) collective-permute-start(bf16[2,128,128]{2,1,0:T(8,128)(2,1)S(1)} %get-tuple-element.33), channel_id=1, source_target_pairs={{504,507},{506,509},{507,504},{508,511},{509,506},{511,508}} | collective-permute-start | bytes 196616 | tf_op jit(solution)/shard_map/ppermute | solution.py:441
  25.4 3.8 %collective-permute-start.5 = (bf16[2,128,128]{2,1,0:T(8,128)(2,1)S(1)}, bf16[2,128,128]{2,1,0:T(8,128)(2,1)S(1)}, u32[]{:S(2)}, u32[]{:S(2)}) collective-permute-start(bf16[2,128,128]{2,1,0:T(8,128)(2,1)S(1)} %get-tuple-element.33), channel_id=1, source_target_pairs={{504,506},{506,508},{507,505},{508,510},{509,507},{511,509}} | collective-permute-start | bytes 196616 | tf_op jit(solution)/shard_map/ppermute | solution.py:441
  26.1 10.7 %collective-permute-start.3 = (bf16[2,2,128,128]{3,2,1,0:T(8,128)(2,1)}, bf16[2,2,128,128]{3,2,1,0:T(8,128)(2,1)S(1)}, u32[]{:S(2)}, u32[]{:S(2)}) collective-permute-start(bf16[2,2,128,128]{3,2,1,0:T(8,128)(2,1)} %get-tuple-element.31), channel_id=1, source_target_pairs={{113,2},{114,1},{115,4},{116,3},{117,6},{118,5},{393,506},{394,505... | collective-permute-start | bytes 393224 | tf_op jit(solution)/shard_map/ppermute | solution.py:441
  28.5 8.3 %collective-permute-start.2 = (bf16[2,2,128,128]{3,2,1,0:T(8,128)(2,1)}, bf16[2,2,128,128]{3,2,1,0:T(8,128)(2,1)S(1)}, u32[]{:S(2)}, u32[]{:S(2)}) collective-permute-start(bf16[2,2,128,128]{3,2,1,0:T(8,128)(2,1)} %get-tuple-element.31), channel_id=1, source_target_pairs={{112,1},{113,0},{114,3},{115,2},{116,5},{117,4},{118,7},{119,6},{3... | collective-permute-start | bytes 393224 | tf_op jit(solution)/shard_map/ppermute | solution.py:441
  29.2 0.6 copy-start.3
  29.8 7.0 %collective-permute-start.4 = (bf16[2,2,128,128]{3,2,1,0:T(8,128)(2,1)S(1)}, bf16[2,2,128,128]{3,2,1,0:T(8,128)(2,1)S(1)}, u32[]{:S(2)}, u32[]{:S(2)}) collective-permute-start(bf16[2,2,128,128]{3,2,1,0:T(8,128)(2,1)S(1)} %get-tuple-element.32.last_own), channel_id=1, source_target_pairs={{497,507},{498,504},{499,509},{500,506},{501,511},{502,508}} | collective-permute-start | bytes 393224 | tf_op jit(solution)/shard_map/ppermute | solution.py:441
  35.8 10.9 %copy-start.1 = (bf16[12,128,128]{2,1,0:T(8,128)(2,1)S(1)}, bf16[12,128,128]{2,1,0:T(8,128)(2,1)}, u32[]{:S(2)}) copy-start(bf16[12,128,128]{2,1,0:T(8,128)(2,1)} %shard_map.93.nat) | copy-start | bytes 1179652
  36.8 37.8 %copy-start.4 = (bf16[2,128,128]{2,1,0:T(8,128)(2,1)S(1)}, bf16[2,128,128]{2,1,0:T(8,128)(2,1)}, u32[]{:S(2)}) copy-start(bf16[2,128,128]{2,1,0:T(8,128)(2,1)} %copy-done.3) | copy-start | bytes 196612
  36.8 9.8 %collective-permute-start.7 = (bf16[12,128,128]{2,1,0:T(8,128)(2,1)S(1)}, bf16[12,128,128]{2,1,0:T(8,128)(2,1)S(1)}, u32[]{:S(2)}, u32[]{:S(2)}) collective-permute-start(bf16[12,128,128]{2,1,0:T(8,128)(2,1)S(1)} %collective-permute-done.swp), channel_id=1, source_target_pairs={{0,2},{2,4},{3,1},{4,6},{5,3},{7,5},{8,10},{10,12},{11,9},{12,14},... | collective-permute-start | bytes 1179656 | tf_op jit(solution)/shard_map/ppermute | solution.py:441
  49.4 37.8 %collective-permute-start.9 = (bf16[20,128,128]{2,1,0:T(8,128)(2,1)S(1)}, bf16[20,128,128]{2,1,0:T(8,128)(2,1)S(1)}, u32[]{:S(2)}, u32[]{:S(2)}) collective-permute-start(bf16[20,128,128]{2,1,0:T(8,128)(2,1)S(1)} %get-tuple-element.40), channel_id=1, source_target_pairs={{8,0},{9,1},{10,2},{11,3},{12,4},{13,5},{14,6},{15,7},{16,8},{17,9... | collective-permute-start | bytes 1966088 | tf_op jit(solution)/shard_map/ppermute | solution.py:441
  68.6 16.6 %collective-permute-start.10 = (bf16[4,128,128]{2,1,0:T(8,128)(2,1)S(1)}, bf16[4,128,128]{2,1,0:T(8,128)(2,1)S(1)}, u32[]{:S(2)}, u32[]{:S(2)}) collective-permute-start(bf16[4,128,128]{2,1,0:T(8,128)(2,1)S(1)} %get-tuple-element.41), channel_id=1, source_target_pairs={{8,2},{9,3},{10,4},{11,5},{12,6},{13,7},{16,10},{17,11},{18,12},{1... | collective-permute-start | bytes 393224 | tf_op jit(solution)/shard_map/ppermute | solution.py:441
  73.3 13.9 %collective-permute-start.11 = (bf16[4,128,128]{2,1,0:T(8,128)(2,1)S(1)}, bf16[4,128,128]{2,1,0:T(8,128)(2,1)S(1)}, u32[]{:S(2)}, u32[]{:S(2)}) collective-permute-start(bf16[4,128,128]{2,1,0:T(8,128)(2,1)S(1)} %get-tuple-element.42), channel_id=1, source_target_pairs={{10,0},{11,1},{12,2},{13,3},{14,4},{15,5},{18,8},{19,9},{20,10},{2... | collective-permute-start | bytes 393224 | tf_op jit(solution)/shard_map/ppermute | solution.py:441
  76.3 24.6 %collective-permute-start.8 = (bf16[8,128,128]{2,1,0:T(8,128)(2,1)S(1)}, bf16[8,128,128]{2,1,0:T(8,128)(2,1)S(1)}, u32[]{:S(2)}, u32[]{:S(2)}) collective-permute-start(bf16[8,128,128]{2,1,0:T(8,128)(2,1)S(1)} %get-tuple-element.39), channel_id=1, source_target_pairs={{0,8},{1,9},{2,10},{3,11},{4,12},{5,13},{6,14},{7,15},{8,16},{9,17... | collective-permute-start | bytes 786440 | tf_op jit(solution)/shard_map/ppermute | solution.py:441
  87.2 17.0 %copy-start.6 = (bf16[2,2,128,128]{3,2,1,0:T(8,128)(2,1)S(1)}, bf16[2,2,128,128]{3,2,1,0:T(8,128)(2,1)}, u32[]{:S(2)}) copy-start(bf16[2,2,128,128]{3,2,1,0:T(8,128)(2,1)} %copy-done.5) | copy-start | bytes 393220
  90.9 19.9 %collective-permute-start.13 = (bf16[4,256,128]{2,1,0:T(8,128)(2,1)S(1)}, bf16[4,256,128]{2,1,0:T(8,128)(2,1)S(1)}, u32[]{:S(2)}, u32[]{:S(2)}) collective-permute-start(bf16[4,256,128]{2,1,0:T(8,128)(2,1)S(1)} %get-tuple-element.51), channel_id=1, source_target_pairs={{8,0},{9,1},{10,2},{11,3},{12,4},{13,5},{14,6},{15,7},{16,8},{17,9... | collective-permute-start | bytes 786440 | tf_op jit(solution)/shard_map/ppermute | solution.py:441
  94.6 9.6 %collective-permute-start.12 = (bf16[2,128,128]{2,1,0:T(8,128)(2,1)S(1)}, bf16[2,128,128]{2,1,0:T(8,128)(2,1)S(1)}, u32[]{:S(2)}, u32[]{:S(2)}) collective-permute-start(bf16[2,128,128]{2,1,0:T(8,128)(2,1)S(1)} %get-tuple-element.53), channel_id=1, source_target_pairs={{0,10},{2,12},{3,9},{4,14},{5,11},{7,13},{8,18},{10,20},{11,17},{1... | collective-permute-start | bytes 196616 | tf_op jit(solution)/shard_map/ppermute | solution.py:441
  100.9 9.0 %all-to-all-start = ((bf16[4,80,128]{2,1,0:T(8,128)(2,1)}), bf16[4,80,128]{2,1,0:T(8,128)(2,1)S(1)}, u32[]{:S(2)}, u32[]{:S(2)}) async-start(bf16[4,80,128]{2,1,0:T(8,128)(2,1)} %get-tuple-element.55), calls=%async_computation | async-start | bytes 163840 | tf_op jit(solution)/shard_map/all_to_all | solution.py:540
  104.2 6.6 %copy-start.7 = (bf16[1,2,32,2,4,128]{5,4,3,2,1,0:T(4,128)(2,1)S(1)}, bf16[1,2,32,2,4,128]{5,4,3,2,1,0:T(4,128)(2,1)}, u32[]{:S(2)}) copy-start(bf16[1,2,32,2,4,128]{5,4,3,2,1,0:T(4,128)(2,1)} %get-tuple-element.62) | copy-start | bytes 393220
